TPU v7x, 32 devices: a whole 2x2x4 slice. The times are simulated.
32 devices in a mesh: rows: 4 (over z), cols: 8 (over y, x, core).
Axes of the slice: x: 2, y: 2, z: 4, core: 2. Of those that a mesh axis runs over, the one named last changes fastest.
Arguments:
- model_dir: float32 [65536, 128], P('cols'), may hold values from -6 to 6
- sens_blocks: bfloat16 [4, 3072, 128, 128], P('rows', 'cols'), may hold values from -0.09375 to 0.09375
- blk_row: int32 [4, 3072], P('rows', 'cols'), may hold values from 0 to 31, as said below
- blk_col: int32 [4, 3072], P('rows', 'cols'), may hold values from 0 to 63, as said below
- blk_count: int32 [4, 8], P('rows', 'cols'), may hold values from 48 to 384, as said below
- send_order: int32 [8, 64], P('cols'), may hold values from 0 to 63, each once within a row
- neighbors: int32 [4, 65536], P(None, 'cols'), may hold values from 0 to 65535, as said below
- face_weight: float32 [4, 65536], P(None, 'cols'), may hold values from 0.05 to 0.5
Outputs:
- data_image: float32 [16384, 128], P('rows')
- normal_product: float32 [65536, 128], P('cols')
Inputs may be any that keep to these rules, and one draw needn't show every extreme that they name: Within one device's 384 slots the pairs (blk_row, blk_col) are all different. `blk_col`: paired with blk_row as stated there. The live slots of a device are its first blk_count slots; some device has all 384 live. `send_order`: each row is a permutation. `neighbors`: every neighbour lies within 64 of the cell's own number.
All inputs are finite; a program needn't handle non-finite values.
Results may differ from a plain program's by a relative error of at most 0.0029.
Values may be sent and summed in bfloat16 or wider, within the bound.
No kernel may reach another device: no remote copies, remote signals or barrier semaphores. Data moves between devices by JAX's collectives and lax.ppermute only.
A program may use at most 192 MiB of HBM per device.

v0:
```python
import math

import jax
import jax.numpy as jnp
from jax import lax
from jax.sharding import PartitionSpec as P

BLK = 128
RB_DEV = 32
RIM = 64


def padded_2(block, sides, width):
    for axis, dim in sides:
        count = lax.axis_size(axis)
        forward = [(i, i + 1) for i in range(count - 1)]
        backward = [(target, source) for source, target in forward]
        low = lax.ppermute(
            lax.slice_in_dim(block, block.shape[dim] - width, None, axis=dim), axis, forward
        )
        high = lax.ppermute(lax.slice_in_dim(block, 0, width, axis=dim), axis, backward)
        block = jnp.concatenate([low, block, high], axis=dim)
    return block


def haar_matrix(order_n):
    matrix = jnp.ones((1, 1), jnp.float32)
    factor = 1.0 / math.sqrt(2.0)
    while matrix.shape[0] < order_n:
        length = matrix.shape[0]
        upper_half = jnp.kron(matrix, jnp.array([[1.0, 1.0]], jnp.float32))
        lower_half = jnp.kron(
            jnp.eye(length, dtype=jnp.float32), jnp.array([[1.0, -1.0]], jnp.float32)
        )
        matrix = jnp.concatenate([upper_half, lower_half], axis=0) * factor
    return matrix


def one_hot(indices, length, dtype):
    return (indices[:, None] == lax.iota(jnp.int32, length)[None, :]).astype(dtype)


def smoothing(extended, center, neighbors, face_weight, offset):
    cell_count, width = center.shape
    tile_count = cell_count // BLK
    tiles = extended.reshape(tile_count + 1, BLK, width)
    window = jnp.concatenate([tiles[:-1], tiles[1:]], axis=1)
    starts = lax.iota(jnp.int32, tile_count) * BLK
    local_index = (neighbors - offset).reshape(4, tile_count, BLK) - starts[None, :, None]
    span = lax.iota(jnp.int32, 2 * BLK)
    weights = jnp.zeros((tile_count, BLK, 2 * BLK), jnp.float32)
    for face in range(4):
        face_w = face_weight[face].reshape(tile_count, BLK)
        weights = weights + jnp.where(
            local_index[face][:, :, None] == span[None, None, :], face_w[:, :, None], 0.0
        )
    mixed = jnp.einsum("bij,bjn->bin", weights, window, precision=lax.Precision.HIGHEST)
    total_w = jnp.sum(face_weight, axis=0)
    return total_w[:, None] * center - mixed.reshape(cell_count, width)


def synthesize(haar_basis, returned, send_onehot, block_count, cell_count):
    share_cols = returned.shape[-1]
    flat_back = returned.reshape(block_count, BLK * share_cols)
    cell_side = jnp.einsum("jb,jm->bm", send_onehot, flat_back, precision=lax.Precision.HIGHEST)
    cell_side = cell_side.reshape(block_count, BLK, share_cols)
    result = jnp.einsum("ji,bjn->bin", haar_basis, cell_side, precision=lax.Precision.HIGHEST)
    return result.reshape(cell_count, share_cols)


def local(model_dir, sens_blocks, blk_row, blk_col, blk_count, send_order, neighbors, face_weight):
    highest = lax.Precision.HIGHEST
    cell_count, vec_width = model_dir.shape
    block_count = cell_count // BLK
    col_devices = lax.axis_size("cols")
    per_peer = block_count // col_devices
    haar_basis = jnp.asarray(haar_matrix(BLK), jnp.float32)
    cell_blocks = model_dir.reshape(block_count, BLK, vec_width)
    coeffs = jnp.einsum("ij,bjn->bin", haar_basis, cell_blocks, precision=highest).astype(
        jnp.bfloat16
    )
    order_here = send_order[0]
    send_half = one_hot(order_here, block_count, jnp.bfloat16)
    ordered = jnp.dot(
        send_half, coeffs.reshape(block_count, BLK * vec_width), preferred_element_type=jnp.float32
    )
    outgoing = ordered.astype(jnp.bfloat16).reshape(col_devices, per_peer * BLK, vec_width)
    wavelet = lax.all_to_all(outgoing, "cols", split_axis=0, concat_axis=0, tiled=True).reshape(
        block_count, BLK * vec_width
    )
    rows_here = blk_row[0]
    cols_here = blk_col[0]
    sensors = sens_blocks[0]
    slot_count = sensors.shape[0]
    live_slot = lax.iota(jnp.int32, slot_count) < blk_count[0, 0]
    pick_cols = one_hot(cols_here, block_count, jnp.bfloat16)
    picked = jnp.dot(pick_cols, wavelet, preferred_element_type=jnp.float32).astype(jnp.bfloat16)
    picked = picked.reshape(slot_count, BLK, vec_width)
    forward = jnp.einsum("kij,kjn->kin", sensors, picked, preferred_element_type=jnp.float32)
    row_mask = (one_hot(rows_here, RB_DEV, jnp.float32) * live_slot[:, None].astype(jnp.float32)).T
    partial_rows = jnp.dot(
        row_mask, forward.reshape(slot_count, BLK * vec_width), precision=highest
    )
    partial_rows = partial_rows.reshape(RB_DEV, BLK, vec_width)
    predicted = lax.psum(partial_rows, "cols")
    data_image = predicted.reshape(RB_DEV * BLK, vec_width)
    image_half = predicted.astype(jnp.bfloat16).reshape(RB_DEV, BLK * vec_width)
    pick_rows = one_hot(rows_here, RB_DEV, jnp.bfloat16)
    chosen = jnp.dot(pick_rows, image_half, preferred_element_type=jnp.float32).astype(jnp.bfloat16)
    chosen = chosen.reshape(slot_count, BLK, vec_width)
    adjoint = jnp.einsum("kij,kin->kjn", sensors, chosen, preferred_element_type=jnp.float32)
    col_mask = (
        one_hot(cols_here, block_count, jnp.float32) * live_slot[:, None].astype(jnp.float32)
    ).T
    partial_cols = jnp.dot(
        col_mask, adjoint.reshape(slot_count, BLK * vec_width), precision=highest
    )
    partial_cols = partial_cols.reshape(block_count, BLK, vec_width)
    extended = padded_2(model_dir, (("cols", 0),), RIM)
    offset = lax.axis_index("cols") * cell_count - RIM
    send_full = one_hot(order_here, block_count, jnp.float32)
    summed = lax.psum(partial_cols, "rows")
    returned = lax.all_to_all(
        summed.reshape(col_devices, per_peer * BLK, vec_width),
        "cols",
        split_axis=0,
        concat_axis=0,
        tiled=True,
    )
    synthesis = synthesize(haar_basis, returned, send_full, block_count, cell_count)
    normal_product = synthesis + smoothing(extended, model_dir, neighbors, face_weight, offset)
    return (data_image, normal_product)


def solution(mesh):
    placed = (
        P("cols", None),
        P("rows", "cols", None, None),
        P("rows", "cols"),
        P("rows", "cols"),
        P("rows", "cols"),
        P("cols", None),
        P(None, "cols"),
        P(None, "cols"),
    )
    return jax.shard_map(
        local,
        mesh=mesh,
        in_specs=placed,
        out_specs=(P("rows", None), P("cols", None)),
        check_vma=False,
    )
```

profile of v0, /device:TPU:0, one launch (start us, length us, event | category | flops | bytes accessed | tf_op | source)
XLA Modules:
  0.0 533.1 jit_solution(13362242330737147679)
XLA Ops:
  7.3 0.1 copy.30
  7.3 0.7 mul.557
  8.0 0.1 mul.558
  8.2 0.7 mul.541
  8.8 0.1 mul.542
  8.9 0.7 mul.525
  9.6 0.1 mul.526
  9.7 0.7 mul.509
  10.3 0.1 mul.510
  10.4 0.7 mul.493
  11.1 0.1 mul.494
  11.2 0.1 mul.475
  11.2 0.1 mul.476
  11.3 0.7 mul.478
  12.0 0.1 mul.479
  12.1 0.7 mul.468
  12.8 0.1 mul.469
  12.9 0.1 copy.29
  13.0 0.1 broadcast_multiply_fusion.1
  13.1 0.1 broadcast_multiply_fusion.2
  13.2 0.1 broadcast_multiply_fusion.3
  13.3 0.1 broadcast_multiply_fusion.4
  13.3 0.1 maximum_multiply_fusion.4
  13.4 0.1 maximum_multiply_fusion.3
  13.5 0.1 maximum_multiply_fusion.2
  13.6 0.1 maximum_multiply_fusion.1
  13.7 0.1 copy.31
  13.8 6.0 %convolution_convert_fusion.3 = bf16[128,64,128]{2,0,1:T(8,128)(2,1)S(1)} fusion(f32[64,128,128]{2,1,0:T(8,128)} %bitcast.118, f32[64,128]{1,0:T(8,128)S(1)} %broadcast_multiply_fusion, f32[64,128]{1,0:T(8,128)S(1)} %copy.31), kind=kOutput, calls=%fused_computation.50 | convolution fusion | flops 1611694080 | bytes 6356992 | tf_op jit(solution)/shard_map/ij,bjn->bin/dot_general | solution.py:79
  19.9 1.7 convolution_convert_fusion.2
  21.6 2.3 reshape.406
  23.9 5.2 all-to-all-start
  29.1 0.2 all-reduce.3.cloned.1.call-start
  30.0 25.7 %all-to-all-done = bf16[8,1024,128]{2,1,0:T(8,128)(2,1)S(1)} async-done(((bf16[8,1024,128]{2,1,0:T(8,128)(2,1)}), bf16[8,1024,128]{2,1,0:T(8,128)(2,1)S(1)}, u32[]{:S(2)}, u32[]{:S(2)}) %all-to-all-start) | async-done | bytes 2097184 | tf_op jit(solution)/shard_map/all_to_all | solution.py:88
  55.7 2.3 reshape.407
  58.0 5.1 fusion.25
  63.1 6.5 %copy.49 = bf16[48,8,128,128]{3,2,1,0:T(8,128)(2,1)} copy(bf16[48,8,128,128]{3,1,2,0:T(8,128)(2,1)S(1)} %fusion.25) | data formatting | bytes 25165824
  69.6 22.1 %fusion.8 = f32[384,128,128]{1,2,0:T(8,128)} fusion(bf16[384,128,128]{2,1,0:T(8,128)(2,1)} %bitcast.116, bf16[1,384,128,128]{3,2,1,0:T(8,128)(2,1)} %param.23), kind=kOutput, calls=%fused_computation.11 | convolution fusion | flops 1610612736 | bytes 50331648 | tf_op jit(solution)/shard_map/kij,kjn->kin/dot_general | solution.py:99
  91.7 25.0 %copy.33 = f32[384,128,128]{0,2,1:T(8,128)} copy(f32[384,128,128]{1,2,0:T(8,128)} %fusion.8) | data formatting | bytes 50331648 | tf_op jit(solution)/shard_map/kij,kjn->kin/dot_general | solution.py:99
  116.7 27.2 %fusion.2 = f32[32,128,128]{2,0,1:T(8,128)} fusion(f32[384,128,128]{0,2,1:T(8,128)} %copy.33, f32[384]{0:T(512)S(1)} %fusion.70, s32[384]{0:T(512)S(1)} %reduce), kind=kOutput, calls=%fused_computation.2 | convolution fusion | flops 2415943680 | bytes 27266048 | tf_op jit(solution)/shard_map/dot_general | solution.py:101
  143.9 0.0 all-reduce.5.cloned.1.call-start
  143.9 61.0 %all-reduce.3.cloned.1.call-done = f32[32,128,128]{2,0,1:T(8,128)} async-done(((f32[32,128,128]{2,0,1:T(8,128)}), f32[32,128,128]{2,0,1:T(8,128)}) %all-reduce.3.cloned.1.call-update) | async-done | bytes 2097168 | tf_op jit(solution)/shard_map/psum | solution.py:105
  204.9 9.7 %fusion.26 = bf16[48,8,128,128]{3,1,2,0:T(8,128)(2,1)} fusion(s32[384]{0:T(512)S(1)} %reduce, f32[32,128,128]{2,0,1:T(8,128)} %all-reduce.3.cloned.1.call-done), kind=kOutput, calls=%fused_computation.29 | convolution fusion | flops 409481216 | bytes 14681600 | tf_op jit(solution)/shard_map/dot_general | solution.py:109
  214.6 12.2 %copy.50 = bf16[48,8,128,128]{3,2,1,0:T(8,128)(2,1)} copy(bf16[48,8,128,128]{3,1,2,0:T(8,128)(2,1)} %fusion.26) | data formatting | bytes 25165824
  226.8 13.2 %fusion.11 = f32[384,128,128]{1,2,0:T(8,128)} fusion(bf16[384,128,128]{2,1,0:T(8,128)(2,1)} %bitcast.117, bf16[1,384,128,128]{3,2,1,0:T(8,128)(2,1)S(1)} %bitcast.115), kind=kOutput, calls=%fused_computation.12 | convolution fusion | flops 1610612736 | bytes 50331648 | tf_op jit(solution)/shard_map/kij,kin->kjn/dot_general | solution.py:111
  240.1 25.0 %copy.37 = f32[384,128,128]{0,2,1:T(8,128)} copy(f32[384,128,128]{1,2,0:T(8,128)} %fusion.11) | data formatting | bytes 50331648 | tf_op jit(solution)/shard_map/kij,kin->kjn/dot_general | solution.py:111
  265.0 27.9 %fusion = f32[64,128,128]{2,0,1:T(8,128)S(1)} fusion(f32[384,128,128]{0,2,1:T(8,128)} %copy.37, f32[384]{0:T(512)S(1)} %fusion.70, s32[384]{0:T(512)S(1)} %reduce.1), kind=kOutput, calls=%fused_computation | convolution fusion | flops 4831887360 | bytes 29363200 | tf_op jit(solution)/shard_map/dot_general | solution.py:115
  292.9 4.4 copy.38
  297.4 0.8 fusion.80
  298.2 1.3 collective-permute-start
  299.5 1.4 collective-permute-start.1
  300.9 150.8 %all-reduce.5.cloned.1.call-done = f32[8,1024,128]{2,1,0:T(8,128)} async-done(((f32[8,1024,128]{2,1,0:T(8,128)}), f32[8,1024,128]{2,1,0:T(8,128)}) %all-reduce.5.cloned.1.call-update) | async-done | bytes 4194320 | tf_op jit(solution)/shard_map/psum | solution.py:122
  451.7 4.8 all-to-all-start.1
  456.5 0.1 fusion.81
  456.7 0.1 bitcast_subtract_fusion.1
  456.8 0.1 reduce_sum.9
  456.9 4.0 pad_maximum_fusion.1
  460.9 3.8 fusion.93
  464.6 20.2 %fusion.14 = f32[64,128,128]{2,1,0:T(8,128)} fusion(f32[64,128]{1,0:T(8,128)S(1)} %bitcast.134, s32[64,128]{1,0:T(8,128)S(1)} %get-tuple-element.7, f32[64,128]{1,0:T(8,128)S(1)} %bitcast.135, s32[64,128]{1,0:T(8,128)S(1)} %get-tuple-element.8, f32[64,128]{1,0:T(8,128)S(1)} %bitcast.133, s32[64,128]{1,0:T(8,128)S(1)} %get-tuple-element.9, ...), kind=kOutput, calls=%fused_computation.13 | convolution fusion | flops 3244294144 | bytes 12845056 | tf_op jit(solution)/shard_map/bij,bjn->bin/dot_general | solution.py:57
  484.8 2.5 copy.34
  487.3 18.3 %all-to-all-done.1 = f32[8,1024,128]{2,1,0:T(8,128)} async-done(((f32[8,1024,128]{2,1,0:T(8,128)}), f32[8,1024,128]{2,1,0:T(8,128)}, u32[]{:S(2)}, u32[]{:S(2)}) %all-to-all-start.1) | async-done | bytes 4194336 | tf_op jit(solution)/shard_map/all_to_all | solution.py:123
  505.6 4.9 reshape.415
  510.6 4.6 fusion.27
  515.2 6.3 %fusion.30 = f32[64,128,128]{1,2,0:T(8,128)S(1)} fusion(f32[64,128,128]{2,0,1:T(8,128)S(1)} %fusion.27, f32[64,128]{1,0:T(8,128)S(1)} %broadcast_multiply_fusion, f32[64,128]{1,0:T(8,128)S(1)} %copy.31), kind=kOutput, calls=%fused_computation.37 | convolution fusion | flops 1610645504 | bytes 8454144 | tf_op jit(solution)/shard_map/ji,bjn->bin/dot_general | solution.py:67
  521.5 4.6 bitcast_add_fusion
  (52 shorter events, 0.3 us)
Async XLA Ops:
  7.2 12.7 %copy-start.5 = (s32[1,64]{1,0:T(1,128)S(1)}, s32[1,64]{1,0:T(1,128)}, u32[]{:S(2)}) copy-start(s32[1,64]{1,0:T(1,128)} %param.27) | copy-start | bytes 772
  21.6 8.4 %copy-start.6 = (s32[1,384]{1,0:T(1,128)S(1)}, s32[1,384]{1,0:T(1,128)}, u32[]{:S(2)}) copy-start(s32[1,384]{1,0:T(1,128)} %param.25) | copy-start | bytes 4612
  21.6 8.4 %copy-start.7 = (s32[1,384]{1,0:T(1,128)S(1)}, s32[1,384]{1,0:T(1,128)}, u32[]{:S(2)}) copy-start(s32[1,384]{1,0:T(1,128)} %param.24) | copy-start | bytes 4612
  23.9 31.8 %all-to-all-start = ((bf16[8,1024,128]{2,1,0:T(8,128)(2,1)}), bf16[8,1024,128]{2,1,0:T(8,128)(2,1)S(1)}, u32[]{:S(2)}, u32[]{:S(2)}) async-start(bf16[8,1024,128]{2,1,0:T(8,128)(2,1)} %reshape.406), calls=%async_computation | async-start | bytes 4194304 | tf_op jit(solution)/shard_map/all_to_all | solution.py:88
  29.1 175.8 %all-reduce.3.cloned.1.call-start = ((), (), s32[]{:S(2)}) async-start(), calls=%async_computation.2 | async-start | bytes 4194304 | tf_op jit(solution)/shard_map/psum | solution.py:105
  143.9 307.8 %all-reduce.5.cloned.1.call-start = ((), (), s32[]{:S(2)}) async-start(), calls=%async_computation.3 | async-start | bytes 8388608 | tf_op jit(solution)/shard_map/psum | solution.py:122
  204.9 21.9 %slice-start = ((s8[12582912]{0:T(1024)(128)(4,1)}), s8[4194304]{0:T(1024)(128)(4,1)S(1)}, s32[]{:S(2)}) async-start(s8[12582912]{0:T(1024)(128)(4,1)} %bitcast.114), calls=%async_computation.4 | async-start | bytes 8388608
  204.9 21.9 %slice-start.1 = ((s8[12582912]{0:T(1024)(128)(4,1)}), s8[4194304]{0:T(1024)(128)(4,1)S(1)}, s32[]{:S(2)}) async-start(s8[12582912]{0:T(1024)(128)(4,1)} %bitcast.114), calls=%async_computation.5 | async-start | bytes 8388608
  214.6 12.2 %slice-start.2 = ((s8[12582912]{0:T(1024)(128)(4,1)}), s8[4194304]{0:T(1024)(128)(4,1)S(1)}, s32[]{:S(2)}) async-start(s8[12582912]{0:T(1024)(128)(4,1)} %bitcast.114), calls=%async_computation.6 | async-start | bytes 8388608
  298.2 158.7 %collective-permute-start = (f32[64,128]{1,0:T(8,128)S(1)}, f32[64,128]{1,0:T(8,128)S(1)}, u32[]{:S(2)}, u32[]{:S(2)}) collective-permute-start(f32[64,128]{1,0:T(8,128)S(1)} %get-tuple-element.4), channel_id=1, source_target_pairs={{0,1},{1,2},{2,3},{3,4},{4,5},{5,6},{6,7},{8,9},{9,10},{10,11},{11... | collective-permute-start | bytes 98312 | tf_op jit(solution)/shard_map/ppermute | solution.py:18
  299.5 157.0 %copy-start.3 = (f32[4,8192]{1,0:T(4,128)S(1)}, f32[4,8192]{1,0:T(4,128)}, u32[]{:S(2)}) copy-start(f32[4,8192]{1,0:T(4,128)} %param.29) | copy-start | bytes 393220
  299.5 157.2 %copy-start.4 = (s32[4,8192]{1,0:T(4,128)S(1)}, s32[4,8192]{1,0:T(4,128)}, u32[]{:S(2)}) copy-start(s32[4,8192]{1,0:T(4,128)} %param.28) | copy-start | bytes 393220
  299.5 157.4 %collective-permute-start.1 = (f32[64,128]{1,0:T(8,128)S(1)}, f32[64,128]{1,0:T(8,128)S(1)}, u32[]{:S(2)}, u32[]{:S(2)}) collective-permute-start(f32[64,128]{1,0:T(8,128)S(1)} %get-tuple-element.5), channel_id=1, source_target_pairs={{1,0},{2,1},{3,2},{4,3},{5,4},{6,5},{7,6},{9,8},{10,9},{11,10},{12... | collective-permute-start | bytes 98312 | tf_op jit(solution)/shard_map/ppermute | solution.py:21
  451.7 53.9 %all-to-all-start.1 = ((f32[8,1024,128]{2,1,0:T(8,128)}), f32[8,1024,128]{2,1,0:T(8,128)}, u32[]{:S(2)}, u32[]{:S(2)}) async-start(f32[8,1024,128]{2,1,0:T(8,128)} %all-reduce.5.cloned.1.call-done), calls=%async_computation.1 | async-start | bytes 8388608 | tf_op jit(solution)/shard_map/all_to_all | solution.py:123
  464.6 20.2 %copy-start.1 = (f32[32,128,128]{2,0,1:T(8,128)S(1)}, f32[32,128,128]{2,0,1:T(8,128)}, u32[]{:S(2)}) copy-start(f32[32,128,128]{2,0,1:T(8,128)} %all-reduce.3.cloned.1.call-done) | copy-start | bytes 6291460
  515.2 6.3 %copy-start = (f32[8192,128]{1,0:T(8,128)S(1)}, f32[8192,128]{1,0:T(8,128)}, u32[]{:S(2)}) copy-start(f32[8192,128]{1,0:T(8,128)} %param.22) | copy-start | bytes 12582916
  515.2 6.3 %copy-start.2 = (f32[64,128,128]{2,1,0:T(8,128)S(1)}, f32[64,128,128]{2,1,0:T(8,128)}, u32[]{:S(2)}) copy-start(f32[64,128,128]{2,1,0:T(8,128)} %fusion.14) | copy-start | bytes 12582916
Sparse Core Ops, SparseCore 0:
  144.0 60.8 all-reduce.2
  297.5 154.1 all-reduce.4
where the time goes:
time: 539 us; the launch traced here: 533 us
  waiting for transfers between devices  256 us (47%)
  matrix products  144 us (27%)
  local copies, waits for them, and re-layouts  92 us (17%)
  between operations  15.2 us (3%)
  other arithmetic  13.2 us (2%)
  starting transfers between devices  12.9 us (2%)
    psum x1, waiting for transfers between devices, local(): summed = lax.psum(partial_cols, 'rows')  151 us
    psum x1, waiting for transfers between devices, local(): predicted = lax.psum(partial_rows, 'cols')  61 us
    dot_general x1, matrix products, local(): jnp.dot(col_mask, adjoint.reshape(slot_count, BLK * vec_width), precision...  27.9 us
    dot_general x1, matrix products, local(): jnp.dot(row_mask, forward.reshape(slot_count, BLK * vec_width), precision...  27.2 us
    all_to_all x1, waiting for transfers between devices, local(): lax.all_to_all(outgoing, 'cols', split_axis=0, concat_axis=0, tiled=True)  25.7 us
    dot_general x1, local copies, waits for them, and re-layouts, local(): jnp.einsum('kij,kin->kjn', sensors, chosen, preferred_element_type=jnp.fl...  25 us
    dot_general x1, local copies, waits for them, and re-layouts, local(): jnp.einsum('kij,kjn->kin', sensors, picked, preferred_element_type=jnp.fl...  25 us
    dot_general x1, matrix products, local(): jnp.einsum('kij,kjn->kin', sensors, picked, preferred_element_type=jnp.fl...  22.1 us
  transfers between devices with their start and end apart: 6, of which 4 were waited for; matrix products, arithmetic and copies ran while one was open for 6% of the time, Pallas kernels for 0%

commit v1 on v0

v1 whole, which is shorter than its diff:
```python
import math

import jax
import jax.numpy as jnp
import numpy as np
from jax import lax
from jax.experimental import pallas as pl
from jax.experimental.pallas import tpu as pltpu
from jax.sharding import PartitionSpec as P

BLK = 128
RB_DEV = 32
RIM = 64
STEP = 16
MIB = 1 << 20


def haar_matrix(order_n):
    matrix = np.ones((1, 1))
    while matrix.shape[0] < order_n:
        length = matrix.shape[0]
        upper = np.kron(matrix, np.array([[1.0, 1.0]]))
        lower = np.kron(np.eye(length), np.array([[1.0, -1.0]]))
        matrix = np.concatenate([upper, lower], axis=0) / math.sqrt(2.0)
    return matrix


def split3(x):
    hi = x.astype(jnp.bfloat16)
    rest = x - hi.astype(jnp.float32)
    mid = rest.astype(jnp.bfloat16)
    low = (rest - mid.astype(jnp.float32)).astype(jnp.bfloat16)
    return jnp.concatenate([hi, mid, low], axis=0)


def analyze_body(place_ref, sign_ref, scale_ref, model_ref, out_ref):
    per_step = model_ref.shape[0]
    first = pl.program_id(0) * per_step
    for b in range(per_step):
        parts = split3(model_ref[b])
        raw = jnp.dot(sign_ref[...], parts, preferred_element_type=jnp.float32)
        out_ref[place_ref[first + b]] = (raw * scale_ref[...]).astype(jnp.bfloat16)


def analyze(place, model_blocks):
    blocks = model_blocks.shape[0]
    width = model_blocks.shape[2]
    per_step = 8
    haar = haar_matrix(BLK)
    scale = np.abs(haar).max(axis=1)
    sign = np.sign(haar)
    signs = jnp.asarray(np.concatenate([sign, sign, sign], axis=1), jnp.bfloat16)
    scales = jnp.asarray(np.broadcast_to(scale[:, None], (BLK, width)), jnp.float32)
    return pl.pallas_call(
        analyze_body,
        out_shape=jax.ShapeDtypeStruct((blocks, BLK, width), jnp.bfloat16),
        grid_spec=pltpu.PrefetchScalarGridSpec(
            num_scalar_prefetch=1,
            grid=(blocks // per_step,),
            in_specs=[
                pl.BlockSpec((BLK, 3 * BLK), lambda i, *_: (0, 0)),
                pl.BlockSpec((BLK, width), lambda i, *_: (0, 0)),
                pl.BlockSpec((per_step, BLK, width), lambda i, *_: (i, 0, 0)),
            ],
            out_specs=pl.BlockSpec((blocks, BLK, width), lambda i, *_: (0, 0, 0)),
        ),
        compiler_params=pltpu.CompilerParams(vmem_limit_bytes=24 * MIB),
        cost_estimate=pl.CostEstimate(
            flops=6 * blocks * BLK * BLK * width, bytes_accessed=6 * blocks * BLK * width,
            transcendentals=0,
        ),
        name="analyze",
    )(place, signs, scales, model_blocks)


def forward_body(rows_ref, cols_ref, count_ref, sens_ref, wave_ref, out_ref, acc_ref):
    step = pl.program_id(0)
    row_blocks = out_ref.shape[0]

    @pl.when(step == 0)
    def _():
        acc_ref[...] = jnp.zeros_like(acc_ref)

    @pl.when(step * STEP < count_ref[0])
    def _():
        for k in range(STEP):
            slot = step * STEP + k
            row = jnp.where(slot < count_ref[0], rows_ref[slot], row_blocks)
            acc_ref[row] += jnp.dot(
                sens_ref[k], wave_ref[cols_ref[slot]], preferred_element_type=jnp.float32
            )

    @pl.when(step == pl.num_programs(0) - 1)
    def _():
        out_ref[...] = acc_ref[:row_blocks].astype(out_ref.dtype)


def live_step(i, rows_ref, cols_ref, count_ref):
    return (jnp.minimum(i, (count_ref[0] - 1) // STEP), 0, 0)


def forward(rows, cols, count, sens, wave):
    slots = sens.shape[0]
    width = wave.shape[2]
    return pl.pallas_call(
        forward_body,
        out_shape=jax.ShapeDtypeStruct((RB_DEV, BLK, width), jnp.bfloat16),
        grid_spec=pltpu.PrefetchScalarGridSpec(
            num_scalar_prefetch=3,
            grid=(slots // STEP,),
            in_specs=[
                pl.BlockSpec((STEP, BLK, BLK), live_step),
                pl.BlockSpec(wave.shape, lambda i, *_: (0, 0, 0)),
            ],
            out_specs=pl.BlockSpec((RB_DEV, BLK, width), lambda i, *_: (0, 0, 0)),
            scratch_shapes=[pltpu.VMEM((RB_DEV + 1, BLK, width), jnp.float32)],
        ),
        compiler_params=pltpu.CompilerParams(vmem_limit_bytes=24 * MIB),
        cost_estimate=pl.CostEstimate(
            flops=2 * slots * BLK * BLK * width, bytes_accessed=2 * slots * BLK * BLK,
            transcendentals=0,
        ),
        name="forward",
    )(rows, cols, count, sens, wave)


def adjoint_body(rows_ref, cols_ref, count_ref, sens_ref, image_ref, out_ref, acc_ref):
    step = pl.program_id(0)
    parts, col_blocks, piece = out_ref.shape[:3]

    @pl.when(step == 0)
    def _():
        acc_ref[...] = jnp.zeros_like(acc_ref)

    @pl.when(step * STEP < count_ref[0])
    def _():
        for k in range(STEP):
            slot = step * STEP + k
            col = jnp.where(slot < count_ref[0], cols_ref[slot], col_blocks)
            acc_ref[col] += lax.dot_general(
                sens_ref[k], image_ref[rows_ref[slot]], (((0,), (0,)), ((), ())),
                preferred_element_type=jnp.float32,
            )

    @pl.when(step == pl.num_programs(0) - 1)
    def _():
        for r in range(parts):
            out_ref[r] = acc_ref[:col_blocks, r * piece : (r + 1) * piece].astype(out_ref.dtype)


def adjoint(rows, cols, count, sens, image, col_blocks, parts):
    slots = sens.shape[0]
    width = image.shape[2]
    piece = BLK // parts
    return pl.pallas_call(
        adjoint_body,
        out_shape=jax.ShapeDtypeStruct((parts, col_blocks, piece, width), jnp.bfloat16),
        grid_spec=pltpu.PrefetchScalarGridSpec(
            num_scalar_prefetch=3,
            grid=(slots // STEP,),
            in_specs=[
                pl.BlockSpec((STEP, BLK, BLK), live_step),
                pl.BlockSpec(image.shape, lambda i, *_: (0, 0, 0)),
            ],
            out_specs=pl.BlockSpec(
                (parts, col_blocks, piece, width), lambda i, *_: (0, 0, 0, 0)
            ),
            scratch_shapes=[pltpu.VMEM((col_blocks + 1, BLK, width), jnp.float32)],
        ),
        compiler_params=pltpu.CompilerParams(vmem_limit_bytes=24 * MIB),
        cost_estimate=pl.CostEstimate(
            flops=2 * slots * BLK * BLK * width, bytes_accessed=2 * slots * BLK * BLK,
            transcendentals=0,
        ),
        name="adjoint",
    )(rows, cols, count, sens, image)


def smooth_body(offset_ref, ext_ref, near_ref, weight_ref, out_ref):
    tiles = out_ref.shape[0] // BLK
    first = pl.program_id(0) * tiles
    span = lax.broadcasted_iota(jnp.int32, (2 * BLK, BLK), 0)
    center = lax.broadcasted_iota(jnp.int32, (2 * BLK, BLK), 1) + RIM
    for t in range(tiles):
        start = (first + t) * BLK
        cells = slice(t * BLK, (t + 1) * BLK)
        near = near_ref[:, cells] - (offset_ref[0] + start)
        face = weight_ref[:, cells]
        total = jnp.sum(face, axis=0, keepdims=True)
        mix = jnp.where(span == center, total, 0.0)
        for k in range(4):
            mix = mix - jnp.where(span == near[k : k + 1], face[k : k + 1], 0.0)
        window = ext_ref[pl.ds(pl.multiple_of(start, BLK), 2 * BLK), :]
        out_ref[cells, :] = lax.dot_general(
            mix, window, (((0,), (0,)), ((), ())),
            precision=lax.Precision.HIGHEST, preferred_element_type=jnp.float32,
        )


def smoothing(offset, extended, neighbors, face_weight):
    cells = neighbors.shape[1]
    width = extended.shape[1]
    per_step = 8 * BLK
    return pl.pallas_call(
        smooth_body,
        out_shape=jax.ShapeDtypeStruct((cells, width), jnp.float32),
        grid_spec=pltpu.PrefetchScalarGridSpec(
            num_scalar_prefetch=1,
            grid=(cells // per_step,),
            in_specs=[
                pl.BlockSpec(extended.shape, lambda i, *_: (0, 0)),
                pl.BlockSpec((4, per_step), lambda i, *_: (0, i)),
                pl.BlockSpec((4, per_step), lambda i, *_: (0, i)),
            ],
            out_specs=pl.BlockSpec((per_step, width), lambda i, *_: (i, 0)),
        ),
        compiler_params=pltpu.CompilerParams(vmem_limit_bytes=24 * MIB),
        cost_estimate=pl.CostEstimate(
            flops=24 * cells * BLK * width, bytes_accessed=16 * cells * width, transcendentals=0
        ),
        name="smoothing",
    )(offset, extended, neighbors, face_weight)


def finish_body(place_ref, basis_ref, wave_ref, smooth_ref, out_ref):
    per_step = out_ref.shape[0]
    first = pl.program_id(0) * per_step
    parts = wave_ref.shape[0]
    for b in range(per_step):
        at = place_ref[first + b]
        block = jnp.concatenate([wave_ref[r, at] for r in range(parts)], axis=0)
        both = jnp.concatenate([block, block], axis=0)
        out_ref[b] = smooth_ref[b] + jnp.dot(
            basis_ref[...], both, preferred_element_type=jnp.float32
        )


def finish(place, wave, smooth_blocks):
    blocks, _, width = smooth_blocks.shape
    per_step = 8
    basis = haar_matrix(BLK).T.astype(np.float32)
    high = basis.astype(jnp.bfloat16)
    low = (basis - high.astype(np.float32)).astype(jnp.bfloat16)
    basis2 = jnp.asarray(np.concatenate([high, low], axis=1))
    return pl.pallas_call(
        finish_body,
        out_shape=jax.ShapeDtypeStruct((blocks, BLK, width), jnp.float32),
        grid_spec=pltpu.PrefetchScalarGridSpec(
            num_scalar_prefetch=1,
            grid=(blocks // per_step,),
            in_specs=[
                pl.BlockSpec((BLK, 2 * BLK), lambda i, *_: (0, 0)),
                pl.BlockSpec(wave.shape, lambda i, *_: (0, 0, 0, 0)),
                pl.BlockSpec((per_step, BLK, width), lambda i, *_: (i, 0, 0)),
            ],
            out_specs=pl.BlockSpec((per_step, BLK, width), lambda i, *_: (i, 0, 0)),
        ),
        compiler_params=pltpu.CompilerParams(vmem_limit_bytes=24 * MIB),
        cost_estimate=pl.CostEstimate(
            flops=4 * blocks * BLK * BLK * width, bytes_accessed=10 * blocks * BLK * width,
            transcendentals=0,
        ),
        name="finish",
    )(place, basis2, wave, smooth_blocks)


def extend(block, axis, width):
    count = lax.axis_size(axis)
    forward_pairs = [(i, i + 1) for i in range(count - 1)]
    backward_pairs = [(target, source) for source, target in forward_pairs]
    low = lax.ppermute(block[block.shape[0] - width :], axis, forward_pairs)
    high = lax.ppermute(block[:width], axis, backward_pairs)
    return jnp.concatenate([low, block, high], axis=0)


def local(model_dir, sens_blocks, blk_row, blk_col, blk_count, send_order, neighbors, face_weight):
    cell_count, width = model_dir.shape
    blocks = cell_count // BLK
    col_devices = lax.axis_size("cols")
    row_devices = lax.axis_size("rows")
    per_peer = blocks // col_devices
    piece = BLK // row_devices
    model_blocks = model_dir.reshape(blocks, BLK, width)
    order = send_order[0]
    positions = lax.iota(jnp.int32, blocks)
    place = jnp.sum(
        jnp.where(order[None, :] == positions[:, None], positions[None, :], 0), axis=1
    )
    sens = sens_blocks[0]
    rows, cols, count = blk_row[0], blk_col[0], blk_count[0]

    outgoing = analyze(place, model_blocks)
    wave = lax.all_to_all(
        outgoing.reshape(col_devices, per_peer * BLK, width), "cols", 0, 0, tiled=True
    ).reshape(blocks, BLK, width)

    extended = extend(model_dir, "cols", RIM)
    offset = (lax.axis_index("cols") * cell_count - RIM).astype(jnp.int32).reshape(1)
    smooth = smoothing(offset, extended, neighbors, face_weight)

    partial_rows = forward(rows, cols, count, sens, wave)
    shares = lax.all_to_all(
        partial_rows.reshape(col_devices, -1, width), "cols", 0, 0, tiled=True
    )
    image_share = jnp.sum(shares.astype(jnp.float32), axis=0).astype(jnp.bfloat16)
    image_half = lax.all_gather(image_share, "cols", axis=0, tiled=True)
    data_image = image_half.astype(jnp.float32)

    partial_cols = adjoint(
        rows, cols, count, sens, image_half.reshape(RB_DEV, BLK, width), blocks, row_devices
    )
    pieces = lax.all_to_all(
        partial_cols.reshape(row_devices * col_devices, per_peer * piece, width),
        ("rows", "cols"), 0, 0, tiled=True,
    ).reshape(row_devices, blocks, piece, width)
    summed = jnp.sum(pieces.astype(jnp.float32), axis=0).astype(jnp.bfloat16)
    gathered = lax.all_gather(summed, "rows", axis=0, tiled=False)
    normal = finish(place, gathered, smooth.reshape(blocks, BLK, width))
    return (data_image, normal.reshape(cell_count, width))


def solution(mesh):
    placed = (
        P("cols", None),
        P("rows", "cols", None, None),
        P("rows", "cols"),
        P("rows", "cols"),
        P("rows", "cols"),
        P("cols", None),
        P(None, "cols"),
        P(None, "cols"),
    )
    return jax.shard_map(
        local,
        mesh=mesh,
        in_specs=placed,
        out_specs=(P("rows", None), P("cols", None)),
        check_vma=False,
    )
```

time: 539 us -> 233 us (0.43)
  waiting for transfers between devices: 256 us -> 73 us
  matrix products: 144 us -> 0 us
  blocking collectives: 0 us -> 78.1 us
  local copies, waits for them, and re-layouts: 92 us -> 20.9 us
  Pallas kernels: 0 us -> 29.5 us
  other arithmetic: 13.2 us -> 7.54 us
    psum x2 -> x0, waiting for transfers between devices: 212 us -> none  [the longest x1 151 us: local(): summed = lax.psum(partial_cols, 'rows')]
    dot_general x11 -> x0, matrix products: 144 us -> none  [the longest x1 27.9 us: local(): jnp.dot(col_mask, adjoint.reshape(slot_count, BLK * vec_width), precision...]
    all_to_all x0 -> x2, blocking collectives: none -> 78.1 us  [the longest x1 57.8 us: local(): lax.all_to_all(partial_cols.reshape(row_devices * col_devices, per_peer *...]
    dot_general x3 -> x0, local copies, waits for them, and re-layouts: 54.4 us -> none  [the longest x1 25 us: local(): jnp.einsum('kij,kin->kjn', sensors, chosen, preferred_element_type=jnp.fl...]
    all_gather x0 -> x2, waiting for transfers between devices: none -> 43.5 us  [the longest x1 23.9 us: local(): image_half = lax.all_gather(image_share, 'cols', axis=0, tiled=True)]
    pallas_call x0 -> x5, Pallas kernels: none -> 29.5 us  [the longest x1 11.8 us: smoothing(): pl.pallas_call(smooth_body, out_shape=jax.ShapeDtypeStruct((cells, width)...]
    all_to_all x2 -> x1, waiting for transfers between devices: 44 us -> 25.9 us  [local(): lax.all_to_all(outgoing.reshape(col_devices, per_peer * BLK, width), 'col...]
    reshape x3 -> x0, local copies, waits for them, and re-layouts: 9.56 us -> none  [the longest x1 4.94 us: synthesize(): flat_back = returned.reshape(block_count, BLK * share_cols)]
  transfers between devices with their start and end apart: 6 -> 5, of which waited for: 4 -> 4; matrix products, arithmetic and copies ran while one was open for 6% -> 2% of each run, Pallas kernels for 0% -> 5%
where the time goes in v1:
time: 233 us; the launch traced here: 232 us
  blocking collectives  78.1 us (34%)
  waiting for transfers between devices  73 us (31%)
  Pallas kernels  29.5 us (13%)
  local copies, waits for them, and re-layouts  20.9 us (9%)
  between operations  14.8 us (6%)
  starting transfers between devices  7.82 us (3%)
  other arithmetic  7.54 us (3%)
    all_to_all x1, blocking collectives, local(): lax.all_to_all(partial_cols.reshape(row_devices * col_devices, per_peer *...  57.8 us
    all_to_all x1, waiting for transfers between devices, local(): lax.all_to_all(outgoing.reshape(col_devices, per_peer * BLK, width), 'col...  25.9 us
    all_gather x1, waiting for transfers between devices, local(): image_half = lax.all_gather(image_share, 'cols', axis=0, tiled=True)  23.9 us
    all_to_all x1, blocking collectives, local(): lax.all_to_all(partial_rows.reshape(col_devices, -1, width), 'cols', 0, 0...  20.3 us
    unnamed x30, local copies, waits for them, and re-layouts  20.1 us
    all_gather x1, waiting for transfers between devices, local(): gathered = lax.all_gather(summed, 'rows', axis=0, tiled=False)  19.7 us
    pallas_call x1, Pallas kernels, smoothing(): pl.pallas_call(smooth_body, out_shape=jax.ShapeDtypeStruct((cells, width)...  11.8 us
    pallas_call x1, Pallas kernels, finish(): pl.pallas_call(finish_body, out_shape=jax.ShapeDtypeStruct((blocks, BLK,...  5.19 us
  transfers between devices with their start and end apart: 5, of which 4 were waited for; matrix products, arithmetic and copies ran while one was open for 2% of the time, Pallas kernels for 5%

profile of v1, /device:TPU:0, one launch (start us, length us, event | category | flops | bytes accessed | tf_op | source)
XLA Modules:
  0.0 231.7 jit_solution(13149993503742846954)
XLA Ops:
  7.2 0.8 select_reduce_fusion.place_ref
  7.9 0.0 copy-start.2
  7.9 2.2 copy-done.2
  10.1 0.0 copy-start.8
  10.1 0.9 copy-done.8
  11.0 0.0 copy-start.10
  11.0 0.8 copy-done.10
  11.9 0.0 copy-start.13
  11.9 0.0 copy-start.14
  11.9 4.9 %analyze.1 = bf16[64,128,128]{2,1,0:T(8,128)(2,1)} custom-call(s32[64]{0:T(128)S(1)} %select_reduce_fusion.place_ref, bf16[128,384]{1,0:T(8,128)(2,1)S(1)} %copy-done.8, f32[128,128]{1,0:T(8,128)S(1)} %copy-done.10, f32[64,128,128]{2,1,0:T(8,128)S(1)} %bitcast.18), custom_call_target="tpu_custom_call" | custom-call | flops 805306368 | bytes 6291456 | tf_op jit(solution)/shard_map/analyze/pallas_call | solution.py:54
  16.8 5.2 %all-to-all-start = ((bf16[8,1024,128]{2,1,0:T(8,128)(2,1)}), bf16[8,1024,128]{2,1,0:T(8,128)(2,1)S(1)}, u32[]{:S(2)}, u32[]{:S(2)}) async-start(bf16[8,1024,128]{2,1,0:T(8,128)(2,1)} %bitcast.4), calls=%async_computation | async-start | bytes 4194304 | tf_op jit(solution)/shard_map/all_to_all | solution.py:293
  21.9 0.0 all-gather.4.cloned.1.call-start
  22.0 0.0 copy-done.13
  22.0 0.0 copy-done.14
  22.7 25.9 %all-to-all-done = bf16[8,1024,128]{2,1,0:T(8,128)(2,1)S(1)} async-done(((bf16[8,1024,128]{2,1,0:T(8,128)(2,1)}), bf16[8,1024,128]{2,1,0:T(8,128)(2,1)S(1)}, u32[]{:S(2)}, u32[]{:S(2)}) %all-to-all-start) | async-done | bytes 2097184 | tf_op jit(solution)/shard_map/all_to_all | solution.py:293
  48.6 0.0 copy-start
  48.6 4.6 %copy-done = bf16[1,384,128,128]{3,2,1,0:T(8,128)(2,1)S(1)} copy-done((bf16[1,384,128,128]{3,2,1,0:T(8,128)(2,1)S(1)}, bf16[1,384,128,128]{3,2,1,0:T(8,128)(2,1)}, u32[]{:S(2)}) %copy-start) | copy-done | bytes 12582936
  53.2 3.5 %forward.1 = bf16[32,128,128]{2,1,0:T(8,128)(2,1)S(1)} custom-call(s32[384]{0:T(512)S(1)} %reduce.2.rows_ref, s32[384]{0:T(512)S(1)} %reduce.3.cols_ref, s32[1]{0:T(128)} %bitcast.14.count_ref, bf16[384,128,128]{2,1,0:T(8,128)(2,1)S(1)} %bitcast.16, bf16[64,128,128]{2,1,0:T(8,128)(2,1)S(1)} %bitcast.19), custom_call_target="tpu_custom_call" | custom-call | flops 1610612736 | bytes 12582912 | tf_op jit(solution)/shard_map/forward/pallas_call | solution.py:105
  56.7 20.3 %all_to_all.15 = bf16[8,512,128]{2,1,0:T(8,128)(2,1)S(1)} all-to-all(bf16[8,512,128]{2,1,0:T(8,128)(2,1)S(1)} %bitcast.23), channel_id=1, replica_groups=mesh['rows'=4,'cols'=8] {'cols'}, dimensions={0} | all-to-all | bytes 2097152 | tf_op jit(solution)/shard_map/all_to_all | solution.py:302
  77.0 0.8 reduce_sum.34
  77.8 0.0 all-gather.4.cloned.1.call-update
  77.8 0.0 all-gather.6.cloned.1.call-start
  77.8 23.9 %all-gather.4.cloned.1.call-done = bf16[4096,128]{1,0:T(8,128)(2,1)} async-done(((bf16[512,128]{1,0:T(8,128)(2,1)}), bf16[4096,128]{1,0:T(8,128)(2,1)}) %all-gather.4.cloned.1.call-update) | async-done | bytes 1048592 | tf_op jit(solution)/shard_map/all_gather | solution.py:306
  101.7 0.0 copy-start.1
  101.7 4.6 %copy-done.1 = bf16[1,384,128,128]{3,2,1,0:T(8,128)(2,1)S(1)} copy-done((bf16[1,384,128,128]{3,2,1,0:T(8,128)(2,1)S(1)}, bf16[1,384,128,128]{3,2,1,0:T(8,128)(2,1)}, u32[]{:S(2)}) %copy-start.1) | copy-done | bytes 12582936
  106.3 0.0 copy-start.5
  106.3 1.2 copy-done.5
  107.5 4.1 %adjoint.1 = bf16[4,64,32,128]{3,2,1,0:T(8,128)(2,1)S(1)} custom-call(s32[384]{0:T(512)S(1)} %reduce.2.rows_ref, s32[384]{0:T(512)S(1)} %reduce.3.cols_ref, s32[1]{0:T(128)} %bitcast.15.count_ref, bf16[384,128,128]{2,1,0:T(8,128)(2,1)S(1)} %bitcast.17, bf16[32,128,128]{2,1,0:T(8,128)(2,1)S(1)} %bitcast.22), custom_call_target="tpu_custom_call" | custom-call | flops 1610612736 | bytes 12582912 | tf_op jit(solution)/shard_map/adjoint/pallas_call | solution.py:155
  111.6 57.8 %all_to_all.16 = bf16[32,256,128]{2,1,0:T(8,128)(2,1)S(1)} all-to-all(bf16[32,256,128]{2,1,0:T(8,128)(2,1)S(1)} %bitcast.20), channel_id=1, replica_groups=mesh['rows'=4,'cols'=8] {'rows','cols'}, dimensions={0} | all-to-all | bytes 4194304 | tf_op jit(solution)/shard_map/all_to_all | solution.py:312
  169.4 1.3 reduce_sum.35
  170.7 0.0 all-gather.6.cloned.1.call-update
  170.7 0.8 fusion
  171.5 1.3 collective-permute-start
  172.8 1.3 collective-permute-start.1
  174.1 0.0 copy-start.11
  174.1 0.0 copy-start.12
  174.1 0.0 collective-permute-done
  174.1 3.5 %collective-permute-done.1 = f32[64,128]{1,0:T(8,128)S(1)} collective-permute-done((f32[64,128]{1,0:T(8,128)S(1)}, f32[64,128]{1,0:T(8,128)S(1)}, u32[]{:S(2)}, u32[]{:S(2)}) %collective-permute-start.1) | collective-permute-done | bytes 32800 | tf_op jit(solution)/shard_map/ppermute | solution.py:272
  177.6 3.2 %pad_maximum_fusion.ext_ref = f32[8320,128]{1,0:T(8,128)S(1)} fusion(f32[64,128]{1,0:T(8,128)S(1)} %collective-permute-done.1, f32[8192,128]{1,0:T(8,128)} %param.11, f32[64,128]{1,0:T(8,128)S(1)} %collective-permute-done), kind=kLoop, calls=%fused_computation | loop fusion | flops 2129920 | bytes 8519680 | tf_op jit(solution)/shard_map/concatenate | solution.py:273
  180.8 0.0 copy-done.11
  180.8 0.0 copy-done.12
  180.9 0.0 copy-start.6
  180.9 0.0 copy-start.9
  180.9 11.8 %smoothing.1 = f32[8192,128]{1,0:T(8,128)S(1)} custom-call(s32[1]{0:T(128)} %bitcast.11.offset_ref, f32[8320,128]{1,0:T(8,128)S(1)} %pad_maximum_fusion.ext_ref, s32[4,8192]{1,0:T(4,128)S(1)} %copy-done.11, f32[4,8192]{1,0:T(4,128)S(1)} %copy-done.12), custom_call_target="tpu_custom_call" | custom-call | flops 3221225472 | bytes 16777216 | tf_op jit(solution)/shard_map/smoothing/pallas_call | solution.py:204
  192.7 0.0 copy-start.3
  192.7 2.0 copy-done.3
  194.7 0.0 copy-done.6
  194.7 1.5 convert_element_type.2
  196.2 19.7 %all-gather.6.cloned.1.call-done = bf16[256,32,128]{2,1,0:T(8,128)(2,1)} async-done(((bf16[64,32,128]{2,1,0:T(8,128)(2,1)}), bf16[256,32,128]{2,1,0:T(8,128)(2,1)}) %all-gather.6.cloned.1.call-update) | async-done | bytes 2097168 | tf_op jit(solution)/shard_map/all_gather | solution.py:317
  215.9 0.0 copy-done.9
  215.9 0.0 copy-start.4
  215.9 2.2 copy-done.4
  218.1 0.0 copy-start.7
  218.1 1.6 copy-done.7
  219.7 5.2 %finish.1 = f32[64,128,128]{2,1,0:T(8,128)} custom-call(s32[64]{0:T(128)S(1)} %select_reduce_fusion.place_ref, bf16[128,256]{1,0:T(8,128)(2,1)S(1)} %copy-done.9, bf16[4,64,32,128]{3,2,1,0:T(8,128)(2,1)S(1)} %bitcast.24, f32[64,128,128]{2,1,0:T(8,128)S(1)} %bitcast.21), custom_call_target="tpu_custom_call" | custom-call | flops 536870912 | bytes 10485760 | tf_op jit(solution)/shard_map/finish/pallas_call | solution.py:245
  (2 shorter events, 0.0 us)
Async XLA Ops:
  7.9 2.2 copy-start.2
  10.1 0.9 copy-start.8
  11.0 0.8 copy-start.10
  11.9 10.1 %copy-start.13 = (s32[1,384]{1,0:T(1,128)S(1)}, s32[1,384]{1,0:T(1,128)}, u32[]{:S(2)}) copy-start(s32[1,384]{1,0:T(1,128)} %param.13) | copy-start | bytes 4612
  11.9 10.2 %copy-start.14 = (s32[1,384]{1,0:T(1,128)S(1)}, s32[1,384]{1,0:T(1,128)}, u32[]{:S(2)}) copy-start(s32[1,384]{1,0:T(1,128)} %param.14) | copy-start | bytes 4612
  16.8 31.8 %all-to-all-start = ((bf16[8,1024,128]{2,1,0:T(8,128)(2,1)}), bf16[8,1024,128]{2,1,0:T(8,128)(2,1)S(1)}, u32[]{:S(2)}, u32[]{:S(2)}) async-start(bf16[8,1024,128]{2,1,0:T(8,128)(2,1)} %bitcast.4), calls=%async_computation | async-start | bytes 4194304 | tf_op jit(solution)/shard_map/all_to_all | solution.py:293
  21.9 79.8 %all-gather.4.cloned.1.call-start = ((), (), s32[]{:S(2)}) async-start(), calls=%async_computation.3 | async-start | bytes 1179648 | tf_op jit(solution)/shard_map/all_gather | solution.py:306
  48.6 4.6 %copy-start = (bf16[1,384,128,128]{3,2,1,0:T(8,128)(2,1)S(1)}, bf16[1,384,128,128]{3,2,1,0:T(8,128)(2,1)}, u32[]{:S(2)}) copy-start(bf16[1,384,128,128]{3,2,1,0:T(8,128)(2,1)} %param.12) | copy-start | bytes 37748740
  77.8 138.1 %all-gather.6.cloned.1.call-start = ((), (), s32[]{:S(2)}) async-start(), calls=%async_computation.4 | async-start | bytes 2621440 | tf_op jit(solution)/shard_map/all_gather | solution.py:317
  101.7 4.6 %copy-start.1 = (bf16[1,384,128,128]{3,2,1,0:T(8,128)(2,1)S(1)}, bf16[1,384,128,128]{3,2,1,0:T(8,128)(2,1)}, u32[]{:S(2)}) copy-start(bf16[1,384,128,128]{3,2,1,0:T(8,128)(2,1)} %param.12) | copy-start | bytes 37748740
  106.3 1.2 copy-start.5
  171.5 2.6 %collective-permute-start = (f32[64,128]{1,0:T(8,128)S(1)}, f32[64,128]{1,0:T(8,128)S(1)}, u32[]{:S(2)}, u32[]{:S(2)}) collective-permute-start(f32[64,128]{1,0:T(8,128)S(1)} %get-tuple-element.2), channel_id=1, source_target_pairs={{0,1},{1,2},{2,3},{3,4},{4,5},{5,6},{6,7},{8,9},{9,10},{10,11},{11... | collective-permute-start | bytes 98312 | tf_op jit(solution)/shard_map/ppermute | solution.py:271
  172.8 4.8 %collective-permute-start.1 = (f32[64,128]{1,0:T(8,128)S(1)}, f32[64,128]{1,0:T(8,128)S(1)}, u32[]{:S(2)}, u32[]{:S(2)}) collective-permute-start(f32[64,128]{1,0:T(8,128)S(1)} %get-tuple-element.3), channel_id=1, source_target_pairs={{1,0},{2,1},{3,2},{4,3},{5,4},{6,5},{7,6},{9,8},{10,9},{11,10},{12... | collective-permute-start | bytes 98312 | tf_op jit(solution)/shard_map/ppermute | solution.py:272
  174.1 6.8 %copy-start.11 = (s32[4,8192]{1,0:T(4,128)S(1)}, s32[4,8192]{1,0:T(4,128)}, u32[]{:S(2)}) copy-start(s32[4,8192]{1,0:T(4,128)} %near_ref.1) | copy-start | bytes 393220
  174.1 6.8 %copy-start.12 = (f32[4,8192]{1,0:T(4,128)S(1)}, f32[4,8192]{1,0:T(4,128)}, u32[]{:S(2)}) copy-start(f32[4,8192]{1,0:T(4,128)} %weight_ref.1) | copy-start | bytes 393220
  180.9 13.9 %copy-start.6 = (bf16[4096,128]{1,0:T(8,128)(2,1)S(1)}, bf16[4096,128]{1,0:T(8,128)(2,1)}, u32[]{:S(2)}) copy-start(bf16[4096,128]{1,0:T(8,128)(2,1)} %all-gather.4.cloned.1.call-done) | copy-start | bytes 3145732
  180.9 35.0 %copy-start.9 = (bf16[128,256]{1,0:T(8,128)(2,1)S(1)}, bf16[128,256]{1,0:T(8,128)(2,1)}, u32[]{:S(2)}) copy-start(bf16[128,256]{1,0:T(8,128)(2,1)} %constant.23.clone.basis_ref) | copy-start | bytes 196612
  192.7 2.0 copy-start.3
  215.9 2.2 copy-start.4
  218.1 1.6 copy-start.7
Sparse Core Ops, SparseCore 0:
  77.9 23.7 all-gather.3
  170.8 44.9 all-gather.5

commit v2 on v1

--- a/solution.py
+++ b/solution.py
@@ -12,7 +12,9 @@
 RB_DEV = 32
 RIM = 64
 STEP = 16
+CHUNKS = 4
 MIB = 1 << 20
+LARGE = 56 * MIB
 
 
 def haar_matrix(order_n):
@@ -25,31 +27,44 @@
     return matrix
 
 
-def split3(x):
-    hi = x.astype(jnp.bfloat16)
-    rest = x - hi.astype(jnp.float32)
-    mid = rest.astype(jnp.bfloat16)
-    low = (rest - mid.astype(jnp.float32)).astype(jnp.bfloat16)
-    return jnp.concatenate([hi, mid, low], axis=0)
-
-
-def analyze_body(place_ref, sign_ref, scale_ref, model_ref, out_ref):
-    per_step = model_ref.shape[0]
-    first = pl.program_id(0) * per_step
+def analyze_body(order_ref, sign_ref, scale_ref, model_ref, out_ref, block_ref, sems):
+    per_step = out_ref.shape[0]
+    step = pl.program_id(0)
+    steps = model_ref.shape[0] // per_step
+
+    def fetch(j):
+        return pltpu.make_async_copy(
+            model_ref.at[order_ref[0, j]], block_ref.at[j], sems.at[j // per_step]
+        )
+
+    @pl.when(step == 0)
+    def _():
+        for j in range(steps * per_step):
+            fetch(j).start()
+
     for b in range(per_step):
-        parts = split3(model_ref[b])
-        raw = jnp.dot(sign_ref[...], parts, preferred_element_type=jnp.float32)
-        out_ref[place_ref[first + b]] = (raw * scale_ref[...]).astype(jnp.bfloat16)
-
-
-def analyze(place, model_blocks):
+        pltpu.make_async_copy(
+            model_ref.at[0], block_ref.at[step * per_step + b], sems.at[step]
+        ).wait()
+    for b in range(per_step):
+        x = block_ref[step * per_step + b]
+        high = x.astype(jnp.bfloat16)
+        low = (x - high.astype(jnp.float32)).astype(jnp.bfloat16)
+        raw = jnp.dot(
+            sign_ref[...], jnp.concatenate([high, low], axis=0),
+            preferred_element_type=jnp.float32,
+        )
+        out_ref[b] = (raw * scale_ref[...]).astype(jnp.bfloat16)
+
+
+def analyze(order, model_blocks):
     blocks = model_blocks.shape[0]
     width = model_blocks.shape[2]
     per_step = 8
     haar = haar_matrix(BLK)
     scale = np.abs(haar).max(axis=1)
     sign = np.sign(haar)
-    signs = jnp.asarray(np.concatenate([sign, sign, sign], axis=1), jnp.bfloat16)
+    signs = jnp.asarray(np.concatenate([sign, sign], axis=1), jnp.bfloat16)
     scales = jnp.asarray(np.broadcast_to(scale[:, None], (BLK, width)), jnp.float32)
     return pl.pallas_call(
         analyze_body,
@@ -58,19 +73,23 @@
             num_scalar_prefetch=1,
             grid=(blocks // per_step,),
             in_specs=[
-                pl.BlockSpec((BLK, 3 * BLK), lambda i, *_: (0, 0)),
+                pl.BlockSpec((BLK, 2 * BLK), lambda i, *_: (0, 0)),
                 pl.BlockSpec((BLK, width), lambda i, *_: (0, 0)),
-                pl.BlockSpec((per_step, BLK, width), lambda i, *_: (i, 0, 0)),
-            ],
-            out_specs=pl.BlockSpec((blocks, BLK, width), lambda i, *_: (0, 0, 0)),
-        ),
-        compiler_params=pltpu.CompilerParams(vmem_limit_bytes=24 * MIB),
-        cost_estimate=pl.CostEstimate(
-            flops=6 * blocks * BLK * BLK * width, bytes_accessed=6 * blocks * BLK * width,
+                pl.BlockSpec(memory_space=pl.ANY),
+            ],
+            out_specs=pl.BlockSpec((per_step, BLK, width), lambda i, *_: (i, 0, 0)),
+            scratch_shapes=[
+                pltpu.VMEM((blocks, BLK, width), jnp.float32),
+                pltpu.SemaphoreType.DMA((blocks // per_step,)),
+            ],
+        ),
+        compiler_params=pltpu.CompilerParams(vmem_limit_bytes=LARGE),
+        cost_estimate=pl.CostEstimate(
+            flops=4 * blocks * BLK * BLK * width, bytes_accessed=6 * blocks * BLK * width,
             transcendentals=0,
         ),
         name="analyze",
-    )(place, signs, scales, model_blocks)
+    )(order, signs, scales, model_blocks)
 
 
 def forward_body(rows_ref, cols_ref, count_ref, sens_ref, wave_ref, out_ref, acc_ref):
@@ -115,7 +134,7 @@
             out_specs=pl.BlockSpec((RB_DEV, BLK, width), lambda i, *_: (0, 0, 0)),
             scratch_shapes=[pltpu.VMEM((RB_DEV + 1, BLK, width), jnp.float32)],
         ),
-        compiler_params=pltpu.CompilerParams(vmem_limit_bytes=24 * MIB),
+        compiler_params=pltpu.CompilerParams(vmem_limit_bytes=LARGE),
         cost_estimate=pl.CostEstimate(
             flops=2 * slots * BLK * BLK * width, bytes_accessed=2 * slots * BLK * BLK,
             transcendentals=0,
@@ -124,9 +143,10 @@
     )(rows, cols, count, sens, wave)
 
 
-def adjoint_body(rows_ref, cols_ref, count_ref, sens_ref, image_ref, out_ref, acc_ref):
+def adjoint_body(rows_ref, cols_ref, count_ref, sens_ref, image_ref, *refs):
     step = pl.program_id(0)
-    parts, col_blocks, piece = out_ref.shape[:3]
+    out_refs, acc_ref = refs[:-1], refs[-1]
+    col_blocks, piece = out_refs[0].shape[:2]
 
     @pl.when(step == 0)
     def _():
@@ -144,17 +164,17 @@
 
     @pl.when(step == pl.num_programs(0) - 1)
     def _():
-        for r in range(parts):
-            out_ref[r] = acc_ref[:col_blocks, r * piece : (r + 1) * piece].astype(out_ref.dtype)
-
-
-def adjoint(rows, cols, count, sens, image, col_blocks, parts):
+        for c, out_ref in enumerate(out_refs):
+            out_ref[...] = acc_ref[:col_blocks, c * piece : (c + 1) * piece].astype(jnp.bfloat16)
+
+
+def adjoint(rows, cols, count, sens, image, col_blocks):
     slots = sens.shape[0]
     width = image.shape[2]
-    piece = BLK // parts
+    chunk = (col_blocks, BLK // CHUNKS, width)
     return pl.pallas_call(
         adjoint_body,
-        out_shape=jax.ShapeDtypeStruct((parts, col_blocks, piece, width), jnp.bfloat16),
+        out_shape=[jax.ShapeDtypeStruct(chunk, jnp.bfloat16)] * CHUNKS,
         grid_spec=pltpu.PrefetchScalarGridSpec(
             num_scalar_prefetch=3,
             grid=(slots // STEP,),
@@ -162,12 +182,10 @@
                 pl.BlockSpec((STEP, BLK, BLK), live_step),
                 pl.BlockSpec(image.shape, lambda i, *_: (0, 0, 0)),
             ],
-            out_specs=pl.BlockSpec(
-                (parts, col_blocks, piece, width), lambda i, *_: (0, 0, 0, 0)
-            ),
+            out_specs=[pl.BlockSpec(chunk, lambda i, *_: (0, 0, 0))] * CHUNKS,
             scratch_shapes=[pltpu.VMEM((col_blocks + 1, BLK, width), jnp.float32)],
         ),
-        compiler_params=pltpu.CompilerParams(vmem_limit_bytes=24 * MIB),
+        compiler_params=pltpu.CompilerParams(vmem_limit_bytes=LARGE),
         cost_estimate=pl.CostEstimate(
             flops=2 * slots * BLK * BLK * width, bytes_accessed=2 * slots * BLK * BLK,
             transcendentals=0,
@@ -222,20 +240,20 @@
     )(offset, extended, neighbors, face_weight)
 
 
-def finish_body(place_ref, basis_ref, wave_ref, smooth_ref, out_ref):
+def finish_body(place_ref, basis_ref, *refs):
+    wave_refs, smooth_ref, out_ref = refs[:-2], refs[-2], refs[-1]
     per_step = out_ref.shape[0]
     first = pl.program_id(0) * per_step
-    parts = wave_ref.shape[0]
     for b in range(per_step):
         at = place_ref[first + b]
-        block = jnp.concatenate([wave_ref[r, at] for r in range(parts)], axis=0)
-        both = jnp.concatenate([block, block], axis=0)
+        pieces = [ref[at] for ref in wave_refs]
+        both = jnp.concatenate(pieces + pieces, axis=0)
         out_ref[b] = smooth_ref[b] + jnp.dot(
             basis_ref[...], both, preferred_element_type=jnp.float32
         )
 
 
-def finish(place, wave, smooth_blocks):
+def finish(place, waves, smooth_blocks):
     blocks, _, width = smooth_blocks.shape
     per_step = 8
     basis = haar_matrix(BLK).T.astype(np.float32)
@@ -250,18 +268,75 @@
             grid=(blocks // per_step,),
             in_specs=[
                 pl.BlockSpec((BLK, 2 * BLK), lambda i, *_: (0, 0)),
-                pl.BlockSpec(wave.shape, lambda i, *_: (0, 0, 0, 0)),
+                *[pl.BlockSpec(w.shape, lambda i, *_: (0, 0, 0)) for w in waves],
                 pl.BlockSpec((per_step, BLK, width), lambda i, *_: (i, 0, 0)),
             ],
             out_specs=pl.BlockSpec((per_step, BLK, width), lambda i, *_: (i, 0, 0)),
         ),
-        compiler_params=pltpu.CompilerParams(vmem_limit_bytes=24 * MIB),
+        compiler_params=pltpu.CompilerParams(vmem_limit_bytes=LARGE),
         cost_estimate=pl.CostEstimate(
             flops=4 * blocks * BLK * BLK * width, bytes_accessed=10 * blocks * BLK * width,
             transcendentals=0,
         ),
         name="finish",
-    )(place, basis2, wave, smooth_blocks)
+    )(place, basis2, *waves, smooth_blocks)
+
+
+def merge_body(take_ref, got_ref, mine_ref, after_ref, out_ref, *, final):
+    got, mine = got_ref[...], mine_ref[...]
+    if final:
+        out_ref[...] = jnp.where(take_ref[0] > 0, got, mine)
+    else:
+        out_ref[...] = (got.astype(jnp.float32) + mine.astype(jnp.float32)).astype(mine.dtype)
+
+
+def merge(take, got, mine, after, final):
+    return pl.pallas_call(
+        lambda *refs: merge_body(*refs, final=final),
+        out_shape=jax.ShapeDtypeStruct(mine.shape, mine.dtype),
+        in_specs=[
+            pl.BlockSpec(memory_space=pltpu.SMEM),
+            pl.BlockSpec(memory_space=pltpu.VMEM),
+            pl.BlockSpec(memory_space=pltpu.VMEM),
+            pl.BlockSpec(memory_space=pl.ANY),
+        ],
+        out_specs=pl.BlockSpec(memory_space=pltpu.VMEM),
+        compiler_params=pltpu.CompilerParams(vmem_limit_bytes=8 * MIB),
+        cost_estimate=pl.CostEstimate(
+            flops=mine.size, bytes_accessed=6 * mine.size, transcendentals=0
+        ),
+        name="merge",
+    )(take, got, mine, after)
+
+
+def line_sums(parts, axis, deliver):
+    count = lax.axis_size(axis)
+    half = count // 2
+    me = lax.axis_index(axis)
+    stages = []
+    for hop in range(half - 1):
+        stages.append(([(hop, hop + 1), (count - 1 - hop, count - 2 - hop)], False))
+    stages.append(([(half - 1, half), (half, half - 1)], False))
+    for hop in range(half - 1):
+        left, right = half - 1 - hop, half + hop
+        stages.append(([(left, left - 1), (right, right + 1)], True))
+    state = list(parts)
+    got = [lax.ppermute(part, axis, stages[0][0]) for part in parts]
+    done = [None] * len(parts)
+    after = parts[0]
+    for time in range(len(parts) + len(stages) - 1):
+        for s, (pairs, final) in enumerate(stages):
+            k = time - s
+            if not 0 <= k < len(parts):
+                continue
+            take = (me == pairs[0][1]) | (me == pairs[1][1])
+            take = take.astype(jnp.int32).reshape(1)
+            state[k] = after = merge(take, got[k], state[k], after, final)
+            if s + 1 < len(stages):
+                got[k] = lax.ppermute(state[k], axis, stages[s + 1][0])
+            else:
+                done[k] = deliver(state[k])
+    return done
 
 
 def extend(block, axis, width):
@@ -289,33 +364,40 @@
     sens = sens_blocks[0]
     rows, cols, count = blk_row[0], blk_col[0], blk_count[0]
 
-    outgoing = analyze(place, model_blocks)
+    outgoing = analyze(send_order, model_blocks)
     wave = lax.all_to_all(
         outgoing.reshape(col_devices, per_peer * BLK, width), "cols", 0, 0, tiled=True
     ).reshape(blocks, BLK, width)
 
-    extended = extend(model_dir, "cols", RIM)
+    model_late, _ = lax.optimization_barrier((model_dir, outgoing))
+    extended = extend(model_late, "cols", RIM)
     offset = (lax.axis_index("cols") * cell_count - RIM).astype(jnp.int32).reshape(1)
     smooth = smoothing(offset, extended, neighbors, face_weight)
+    wave, smooth = lax.optimization_barrier((wave, smooth))
 
     partial_rows = forward(rows, cols, count, sens, wave)
     shares = lax.all_to_all(
         partial_rows.reshape(col_devices, -1, width), "cols", 0, 0, tiled=True
     )
     image_share = jnp.sum(shares.astype(jnp.float32), axis=0).astype(jnp.bfloat16)
-    image_half = lax.all_gather(image_share, "cols", axis=0, tiled=True)
+    image_half = lax.all_to_all(
+        jnp.broadcast_to(image_share, shares.shape), "cols", 0, 0, tiled=True
+    ).reshape(-1, width)
     data_image = image_half.astype(jnp.float32)
 
     partial_cols = adjoint(
-        rows, cols, count, sens, image_half.reshape(RB_DEV, BLK, width), blocks, row_devices
+        rows, cols, count, sens, image_half.reshape(RB_DEV, BLK, width), blocks
     )
-    pieces = lax.all_to_all(
-        partial_cols.reshape(row_devices * col_devices, per_peer * piece, width),
-        ("rows", "cols"), 0, 0, tiled=True,
-    ).reshape(row_devices, blocks, piece, width)
-    summed = jnp.sum(pieces.astype(jnp.float32), axis=0).astype(jnp.bfloat16)
-    gathered = lax.all_gather(summed, "rows", axis=0, tiled=False)
-    normal = finish(place, gathered, smooth.reshape(blocks, BLK, width))
+    rows_each = BLK // CHUNKS
+
+    def to_cells(chunk):
+        back = lax.all_to_all(
+            chunk.reshape(col_devices, per_peer * rows_each, width), "cols", 0, 0, tiled=True
+        )
+        return back.reshape(blocks, rows_each, width)
+
+    returned = line_sums(partial_cols, "rows", to_cells)
+    normal = finish(place, returned, smooth.reshape(blocks, BLK, width))
     return (data_image, normal.reshape(cell_count, width))
 
 

time: 233 us -> 240 us (1.030)
  starting transfers between devices: 7.82 us -> 72.4 us
  waiting for transfers between devices: 73 us -> 44.9 us
  blocking collectives: 78.1 us -> 56.7 us
  Pallas kernels: 29.5 us -> 48.4 us
  local copies, waits for them, and re-layouts: 20.9 us -> 7.09 us
  between operations: 14.8 us -> 1.68 us
    ppermute x0 -> x12, starting transfers between devices: none -> 48.2 us  [the longest x4 40.1 us: line_sums(): got = [lax.ppermute(part, axis, stages[0][0]) for part in parts]]
    all_gather x2 -> x0, waiting for transfers between devices: 43.5 us -> none  [the longest x1 23.9 us: local(): image_half = lax.all_gather(image_share, 'cols', axis=0, tiled=True)]
    all_to_all x1, blocking collectives: 57.8 us -> 18.5 us  [local(): lax.all_to_all(jnp.broadcast_to(image_share, shares.shape), 'cols', 0, 0,...]
    all_to_all x1, waiting for transfers between devices: 25.9 us -> 2.34 us  [local(): lax.all_to_all(outgoing.reshape(col_devices, per_peer * BLK, width), 'col...]
    ppermute x0 -> x12, waiting for transfers between devices: none -> 21.1 us  [the longest x4 11.3 us: line_sums(): got = [lax.ppermute(part, axis, stages[0][0]) for part in parts]]
    all_to_all x0 -> x4, waiting for transfers between devices: none -> 20.4 us  [to_cells(): lax.all_to_all(chunk.reshape(col_devices, per_peer * rows_each, width), '...]
    all_to_all x1, blocking collectives: 20.3 us -> 38.3 us  [local(): lax.all_to_all(partial_rows.reshape(col_devices, -1, width), 'cols', 0, 0...]
    all_to_all x0 -> x4, starting transfers between devices: none -> 15.4 us  [to_cells(): lax.all_to_all(chunk.reshape(col_devices, per_peer * rows_each, width), '...]
  transfers between devices with their start and end apart: 5 -> 19, of which waited for: 4 -> 10; matrix products, arithmetic and copies ran while one was open for 2% -> 4% of each run, Pallas kernels for 5% -> 8%
where the time goes in v2:
time: 240 us; the launch traced here: 239 us
  starting transfers between devices  72.4 us (30%)
  blocking collectives  56.7 us (24%)
  Pallas kernels  48.4 us (20%)
  waiting for transfers between devices  44.9 us (19%)
  other arithmetic  7.75 us (3%)
  local copies, waits for them, and re-layouts  7.09 us (3%)
    ppermute x4, starting transfers between devices, line_sums(): got = [lax.ppermute(part, axis, stages[0][0]) for part in parts]  40.1 us
    all_to_all x1, blocking collectives, local(): lax.all_to_all(partial_rows.reshape(col_devices, -1, width), 'cols', 0, 0...  38.3 us
    all_to_all x4, waiting for transfers between devices, to_cells(): lax.all_to_all(chunk.reshape(col_devices, per_peer * rows_each, width), '...  20.4 us
    all_to_all x1, blocking collectives, local(): lax.all_to_all(jnp.broadcast_to(image_share, shares.shape), 'cols', 0, 0,...  18.5 us
    all_to_all x4, starting transfers between devices, to_cells(): lax.all_to_all(chunk.reshape(col_devices, per_peer * rows_each, width), '...  15.4 us
    pallas_call x1, Pallas kernels, smoothing(): pl.pallas_call(smooth_body, out_shape=jax.ShapeDtypeStruct((cells, width)...  11.8 us
    ppermute x4, waiting for transfers between devices, line_sums(): got = [lax.ppermute(part, axis, stages[0][0]) for part in parts]  11.3 us
    ppermute x8, waiting for transfers between devices, line_sums(): got[k] = lax.ppermute(state[k], axis, stages[s + 1][0])  9.77 us
  transfers between devices with their start and end apart: 19, of which 10 were waited for; matrix products, arithmetic and copies ran while one was open for 4% of the time, Pallas kernels for 8%

profile of v2, /device:TPU:0, one launch (start us, length us, event | category | flops | bytes accessed | tf_op | source)
XLA Modules:
  0.0 239.1 jit_solution(17148123432337722633)
XLA Ops:
  0.6 7.1 %analyze.1 = bf16[64,128,128]{2,1,0:T(8,128)(2,1)} custom-call(s32[1,64]{1,0:T(1,128)} %order_ref.1, bf16[128,256]{1,0:T(8,128)(2,1)} %constant.30.clone.sign_ref, f32[128,128]{1,0:T(8,128)} %constant.31.clone.scale_ref, f32[64,128,128]{2,1,0:T(8,128)} %bitcast.29), custom_call_target="tpu_custom_call" | custom-call | flops 536870912 | bytes 6291456 | tf_op jit(solution)/shard_map/analyze/pallas_call | solution.py:69
  7.8 5.2 %all-to-all-start = ((bf16[8,1024,128]{2,1,0:T(8,128)(2,1)}), bf16[8,1024,128]{2,1,0:T(8,128)(2,1)S(1)}, u32[]{:S(2)}, u32[]{:S(2)}) async-start(bf16[8,1024,128]{2,1,0:T(8,128)(2,1)} %bitcast.31), calls=%async_computation | async-start | bytes 4194304 | tf_op jit(solution)/shard_map/all_to_all | solution.py:368
  13.0 0.8 fusion
  13.7 2.4 %collective-permute-start = (f32[64,128]{1,0:T(8,128)S(1)}, f32[64,128]{1,0:T(8,128)S(1)}, u32[]{:S(2)}, u32[]{:S(2)}) collective-permute-start(f32[64,128]{1,0:T(8,128)S(1)} %get-tuple-element.16), channel_id=1, source_target_pairs={{0,1},{1,2},{2,3},{3,4},{4,5},{5,6},{6,7},{8,9},{9,10},{10,11},{11... | collective-permute-start | bytes 98312 | tf_op jit(solution)/shard_map/ppermute | solution.py:346
  16.2 1.3 collective-permute-start.1
  18.1 0.6 reduce.1.rows_ref
  18.7 0.6 reduce.2.cols_ref
  19.3 1.1 collective-permute-done.1
  20.4 3.1 %pad_maximum_fusion.ext_ref = f32[8320,128]{1,0:T(8,128)S(1)} fusion(f32[64,128]{1,0:T(8,128)S(1)} %collective-permute-done.1, f32[8192,128]{1,0:T(8,128)} %param.11, f32[64,128]{1,0:T(8,128)S(1)} %collective-permute-done), kind=kLoop, calls=%fused_computation | loop fusion | flops 2129920 | bytes 8519680 | tf_op jit(solution)/shard_map/concatenate | solution.py:348
  23.5 11.8 %smoothing.1 = f32[8192,128]{1,0:T(8,128)S(1)} custom-call(s32[1]{0:T(128)} %bitcast.5.offset_ref, f32[8320,128]{1,0:T(8,128)S(1)} %pad_maximum_fusion.ext_ref, s32[4,8192]{1,0:T(4,128)S(1)} %copy-done.5, f32[4,8192]{1,0:T(4,128)S(1)} %copy-done.6), custom_call_target="tpu_custom_call" | custom-call | flops 3221225472 | bytes 16777216 | tf_op jit(solution)/shard_map/smoothing/pallas_call | solution.py:222
  35.3 1.9 copy-done
  37.3 2.3 all-to-all-done
  39.6 1.3 copy-done.7
  40.9 6.7 %forward.1 = bf16[32,128,128]{2,1,0:T(8,128)(2,1)} custom-call(s32[384]{0:T(512)} %reduce.1.rows_ref, s32[384]{0:T(512)} %reduce.2.cols_ref, s32[1]{0:T(128)} %bitcast.24.count_ref, bf16[384,128,128]{2,1,0:T(8,128)(2,1)} %bitcast.27, bf16[64,128,128]{2,1,0:T(8,128)(2,1)} %bitcast.32), custom_call_target="tpu_custom_call" | custom-call | flops 1610612736 | bytes 12582912 | tf_op jit(solution)/shard_map/forward/pallas_call | solution.py:124
  47.6 38.3 %all_to_all.35 = bf16[8,512,128]{2,1,0:T(8,128)(2,1)S(1)} all-to-all(bf16[8,512,128]{2,1,0:T(8,128)(2,1)} %bitcast.34), channel_id=1, replica_groups=mesh['rows'=4,'cols'=8] {'cols'}, dimensions={0} | all-to-all | bytes 2097152 | tf_op jit(solution)/shard_map/all_to_all | solution.py:379
  85.9 0.1 reduce_sum.21
  86.0 0.1 broadcast_in_dim.17
  86.2 18.5 %all_to_all.36 = bf16[8,512,128]{2,1,0:T(8,128)(2,1)} all-to-all(bf16[8,512,128]{2,1,0:T(8,128)(2,1)S(1)} %broadcast_in_dim.17), channel_id=1, replica_groups=mesh['rows'=4,'cols'=8] {'cols'}, dimensions={0} | all-to-all | bytes 2097152 | tf_op jit(solution)/shard_map/all_to_all | solution.py:383
  104.6 7.2 %adjoint.1 = (bf16[64,32,128]{2,1,0:T(8,128)(2,1)}, bf16[64,32,128]{2,1,0:T(8,128)(2,1)}, bf16[64,32,128]{2,1,0:T(8,128)(2,1)}, bf16[64,32,128]{2,1,0:T(8,128)(2,1)}) custom-call(s32[384]{0:T(512)} %reduce.1.rows_ref, s32[384]{0:T(512)} %reduce.2.cols_ref, s32[1]{0:T(128)} %bitcast.25.count_ref, bf16[384,128,128]{2,1,0:T(8,128)(2,1)} %bitcast.28, ...), custom_call_target="tpu_custom_call" | custom-call | flops 1610612736 | bytes 12582912 | tf_op jit(solution)/shard_map/adjoint/pallas_call | solution.py:175
  111.9 8.3 %collective-permute-start.2 = (bf16[64,32,128]{2,1,0:T(8,128)(2,1)}, bf16[64,32,128]{2,1,0:T(8,128)(2,1)S(1)}, u32[]{:S(2)}, u32[]{:S(2)}) collective-permute-start(bf16[64,32,128]{2,1,0:T(8,128)(2,1)} %get-tuple-element.11.refs_2_.refs_3_), channel_id=1, source_target_pairs={{0,8},{24,16},{1,9},{25,17},{2,10},{26,18},{3,11},{27,19},{4,12},{... | collective-permute-start | bytes 1572872 | tf_op jit(solution)/shard_map/ppermute | solution.py:324
  120.2 1.3 collective-permute-start.4
  121.5 11.3 %collective-permute-done.2.refs_1_ = bf16[64,32,128]{2,1,0:T(8,128)(2,1)S(1)} collective-permute-done((bf16[64,32,128]{2,1,0:T(8,128)(2,1)}, bf16[64,32,128]{2,1,0:T(8,128)(2,1)S(1)}, u32[]{:S(2)}, u32[]{:S(2)}) %collective-permute-start.2) | collective-permute-done | bytes 524320 | tf_op jit(solution)/shard_map/ppermute | solution.py:324
  132.8 1.0 copy-done.1
  133.9 0.1 merge.12.refs_3_.refs_2_
  134.0 0.8 collective-permute-start.3
  134.8 20.5 %collective-permute-start.7 = (bf16[64,32,128]{2,1,0:T(8,128)(2,1)}, bf16[64,32,128]{2,1,0:T(8,128)(2,1)S(1)}, u32[]{:S(2)}, u32[]{:S(2)}) collective-permute-start(bf16[64,32,128]{2,1,0:T(8,128)(2,1)} %get-tuple-element.13.refs_2_), channel_id=1, source_target_pairs={{0,8},{24,16},{1,9},{25,17},{2,10},{26,18},{3,11},{27,19},{4,12},{... | collective-permute-start | bytes 1572872 | tf_op jit(solution)/shard_map/ppermute | solution.py:324
  155.3 0.0 copy-start.4
  155.3 1.0 copy-done.4
  156.4 0.1 merge.13.refs_3_.refs_2_
  156.5 0.7 collective-permute-start.6
  157.2 0.1 merge.14.refs_3_.refs_2_
  157.3 1.3 collective-permute-start.5
  158.6 10.0 %collective-permute-start.10 = (bf16[64,32,128]{2,1,0:T(8,128)(2,1)S(1)}, bf16[64,32,128]{2,1,0:T(8,128)(2,1)S(1)}, u32[]{:S(2)}, u32[]{:S(2)}) collective-permute-start(bf16[64,32,128]{2,1,0:T(8,128)(2,1)S(1)} %copy-done.2), channel_id=1, source_target_pairs={{0,8},{24,16},{1,9},{25,17},{2,10},{26,18},{3,11},{27,19},{4,12},{... | collective-permute-start | bytes 1572872 | tf_op jit(solution)/shard_map/ppermute | solution.py:324
  168.7 0.0 collective-permute-done.7.refs_1_
  168.7 0.1 merge.15.refs_3_.refs_2_
  168.8 0.7 collective-permute-start.9
  169.5 0.1 merge.16.refs_3_.refs_2_
  169.6 1.3 collective-permute-start.8
  171.0 2.2 collective-permute-done.5.refs_1_
  173.2 2.0 merge.17.refs_3_
  175.1 4.2 %all-to-all-start.3 = ((bf16[8,256,128]{2,1,0:T(8,128)(2,1)}), bf16[8,256,128]{2,1,0:T(8,128)(2,1)}, u32[]{:S(2)}, u32[]{:S(2)}) async-start(bf16[8,256,128]{2,1,0:T(8,128)(2,1)} %bitcast.12), calls=%async_computation.3 | async-start | bytes 1048576 | tf_op jit(solution)/shard_map/all_to_all | solution.py:394
  179.4 0.1 merge.18.refs_3_.refs_2_
  179.5 0.7 collective-permute-start.12
  180.2 0.1 merge.19.refs_3_.refs_2_
  180.3 0.0 copy-start.12
  180.3 1.3 collective-permute-start.11
  181.6 2.0 merge.20.refs_3_
  183.6 5.6 %all-to-all-done.3 = bf16[8,256,128]{2,1,0:T(8,128)(2,1)} async-done(((bf16[8,256,128]{2,1,0:T(8,128)(2,1)}), bf16[8,256,128]{2,1,0:T(8,128)(2,1)}, u32[]{:S(2)}, u32[]{:S(2)}) %all-to-all-start.3) | async-done | bytes 524320 | tf_op jit(solution)/shard_map/all_to_all | solution.py:394
  189.2 4.1 %all-to-all-start.4 = ((bf16[8,256,128]{2,1,0:T(8,128)(2,1)}), bf16[8,256,128]{2,1,0:T(8,128)(2,1)}, u32[]{:S(2)}, u32[]{:S(2)}) async-start(bf16[8,256,128]{2,1,0:T(8,128)(2,1)} %bitcast.14), calls=%async_computation.4 | async-start | bytes 1048576 | tf_op jit(solution)/shard_map/all_to_all | solution.py:394
  193.4 0.1 merge.21.refs_3_.refs_2_
  193.5 1.3 collective-permute-start.13
  194.8 3.9 %collective-permute-done.11.refs_1_ = bf16[64,32,128]{2,1,0:T(8,128)(2,1)S(1)} collective-permute-done((bf16[64,32,128]{2,1,0:T(8,128)(2,1)S(1)}, bf16[64,32,128]{2,1,0:T(8,128)(2,1)S(1)}, u32[]{:S(2)}, u32[]{:S(2)}) %collective-permute-start.11) | collective-permute-done | bytes 524320 | tf_op jit(solution)/shard_map/ppermute | solution.py:336
  198.7 0.9 merge.22.refs_3_
  199.6 3.5 %all-to-all-done.4 = bf16[8,256,128]{2,1,0:T(8,128)(2,1)} async-done(((bf16[8,256,128]{2,1,0:T(8,128)(2,1)}), bf16[8,256,128]{2,1,0:T(8,128)(2,1)}, u32[]{:S(2)}, u32[]{:S(2)}) %all-to-all-start.4) | async-done | bytes 524320 | tf_op jit(solution)/shard_map/all_to_all | solution.py:394
  203.1 3.5 %all-to-all-start.5 = ((bf16[8,256,128]{2,1,0:T(8,128)(2,1)}), bf16[8,256,128]{2,1,0:T(8,128)(2,1)S(1)}, u32[]{:S(2)}, u32[]{:S(2)}) async-start(bf16[8,256,128]{2,1,0:T(8,128)(2,1)} %bitcast.16), calls=%async_computation.5 | async-start | bytes 1048576 | tf_op jit(solution)/shard_map/all_to_all | solution.py:394
  206.6 0.7 select_reduce_fusion.place_ref
  207.3 3.6 %collective-permute-done.13.refs_1_ = bf16[64,32,128]{2,1,0:T(8,128)(2,1)S(1)} collective-permute-done((bf16[64,32,128]{2,1,0:T(8,128)(2,1)S(1)}, bf16[64,32,128]{2,1,0:T(8,128)(2,1)S(1)}, u32[]{:S(2)}, u32[]{:S(2)}) %collective-permute-start.13) | collective-permute-done | bytes 524320 | tf_op jit(solution)/shard_map/ppermute | solution.py:336
  210.9 0.9 merge.23
  211.9 4.4 %all-to-all-done.5 = bf16[8,256,128]{2,1,0:T(8,128)(2,1)S(1)} async-done(((bf16[8,256,128]{2,1,0:T(8,128)(2,1)}), bf16[8,256,128]{2,1,0:T(8,128)(2,1)S(1)}, u32[]{:S(2)}, u32[]{:S(2)}) %all-to-all-start.5) | async-done | bytes 524320 | tf_op jit(solution)/shard_map/all_to_all | solution.py:394
  216.3 3.5 %all-to-all-start.6 = ((bf16[8,256,128]{2,1,0:T(8,128)(2,1)}), bf16[8,256,128]{2,1,0:T(8,128)(2,1)S(1)}, u32[]{:S(2)}, u32[]{:S(2)}) async-start(bf16[8,256,128]{2,1,0:T(8,128)(2,1)} %bitcast.18), calls=%async_computation.6 | async-start | bytes 1048576 | tf_op jit(solution)/shard_map/all_to_all | solution.py:394
  219.8 2.7 %bitcast_convert_fusion = f32[4096,128]{1,0:T(8,128)} fusion(bf16[8,512,128]{2,1,0:T(8,128)(2,1)} %all_to_all.36), kind=kLoop, calls=%fused_computation.1 | loop fusion | flops 524288 | bytes 3145728 | tf_op jit(solution)/shard_map/convert_element_type | solution.py:386
  222.5 7.0 %all-to-all-done.6 = bf16[8,256,128]{2,1,0:T(8,128)(2,1)S(1)} async-done(((bf16[8,256,128]{2,1,0:T(8,128)(2,1)}), bf16[8,256,128]{2,1,0:T(8,128)(2,1)S(1)}, u32[]{:S(2)}, u32[]{:S(2)}) %all-to-all-start.6) | async-done | bytes 524320 | tf_op jit(solution)/shard_map/all_to_all | solution.py:394
  229.5 0.8 copy-done.9
  230.3 8.8 %finish.1 = f32[64,128,128]{2,1,0:T(8,128)} custom-call(s32[64]{0:T(128)} %select_reduce_fusion.place_ref, bf16[128,256]{1,0:T(8,128)(2,1)} %constant.32.clone.basis_ref, bf16[64,32,128]{2,1,0:T(8,128)(2,1)} %bitcast.13.refs_0_, bf16[64,32,128]{2,1,0:T(8,128)(2,1)} %bitcast.15.refs_1_, bf16[64,32,128]{2,1,0:T(8,128)(2,1)} %bitcast.35, ...), custom_call_target="tpu_custom_call" | custom-call | flops 536870912 | bytes 10485760 | tf_op jit(solution)/shard_map/finish/pallas_call | solution.py:263
  (27 shorter events, 0.1 us)
Async XLA Ops:
  0.6 17.5 %copy-start.10 = (s32[1,384]{1,0:T(1,128)S(1)}, s32[1,384]{1,0:T(1,128)}, u32[]{:S(2)}) copy-start(s32[1,384]{1,0:T(1,128)} %param.13) | copy-start | bytes 4612
  0.6 18.1 %copy-start.11 = (s32[1,384]{1,0:T(1,128)S(1)}, s32[1,384]{1,0:T(1,128)}, u32[]{:S(2)}) copy-start(s32[1,384]{1,0:T(1,128)} %param.14) | copy-start | bytes 4612
  7.8 31.8 %all-to-all-start = ((bf16[8,1024,128]{2,1,0:T(8,128)(2,1)}), bf16[8,1024,128]{2,1,0:T(8,128)(2,1)S(1)}, u32[]{:S(2)}, u32[]{:S(2)}) async-start(bf16[8,1024,128]{2,1,0:T(8,128)(2,1)} %bitcast.31), calls=%async_computation | async-start | bytes 4194304 | tf_op jit(solution)/shard_map/all_to_all | solution.py:368
  13.7 5.6 %collective-permute-start = (f32[64,128]{1,0:T(8,128)S(1)}, f32[64,128]{1,0:T(8,128)S(1)}, u32[]{:S(2)}, u32[]{:S(2)}) collective-permute-start(f32[64,128]{1,0:T(8,128)S(1)} %get-tuple-element.16), channel_id=1, source_target_pairs={{0,1},{1,2},{2,3},{3,4},{4,5},{5,6},{6,7},{8,9},{9,10},{10,11},{11... | collective-permute-start | bytes 98312 | tf_op jit(solution)/shard_map/ppermute | solution.py:346
  16.2 4.2 %collective-permute-start.1 = (f32[64,128]{1,0:T(8,128)S(1)}, f32[64,128]{1,0:T(8,128)S(1)}, u32[]{:S(2)}, u32[]{:S(2)}) collective-permute-start(f32[64,128]{1,0:T(8,128)S(1)} %get-tuple-element.17), channel_id=1, source_target_pairs={{1,0},{2,1},{3,2},{4,3},{5,4},{6,5},{7,6},{9,8},{10,9},{11,10},{12... | collective-permute-start | bytes 98312 | tf_op jit(solution)/shard_map/ppermute | solution.py:347
  19.3 4.1 %copy-start.5 = (s32[4,8192]{1,0:T(4,128)S(1)}, s32[4,8192]{1,0:T(4,128)}, u32[]{:S(2)}) copy-start(s32[4,8192]{1,0:T(4,128)} %near_ref.1) | copy-start | bytes 393220
  19.3 4.2 %copy-start.6 = (f32[4,8192]{1,0:T(4,128)S(1)}, f32[4,8192]{1,0:T(4,128)}, u32[]{:S(2)}) copy-start(f32[4,8192]{1,0:T(4,128)} %weight_ref.1) | copy-start | bytes 393220
  35.3 2.0 copy-start
  39.6 1.3 copy-start.7
  111.9 21.0 %collective-permute-start.2 = (bf16[64,32,128]{2,1,0:T(8,128)(2,1)}, bf16[64,32,128]{2,1,0:T(8,128)(2,1)S(1)}, u32[]{:S(2)}, u32[]{:S(2)}) collective-permute-start(bf16[64,32,128]{2,1,0:T(8,128)(2,1)} %get-tuple-element.11.refs_2_.refs_3_), channel_id=1, source_target_pairs={{0,8},{24,16},{1,9},{25,17},{2,10},{26,18},{3,11},{27,19},{4,12},{... | collective-permute-start | bytes 1572872 | tf_op jit(solution)/shard_map/ppermute | solution.py:324
  120.2 35.2 %collective-permute-start.4 = (bf16[64,32,128]{2,1,0:T(8,128)(2,1)}, bf16[64,32,128]{2,1,0:T(8,128)(2,1)S(1)}, u32[]{:S(2)}, u32[]{:S(2)}) collective-permute-start(bf16[64,32,128]{2,1,0:T(8,128)(2,1)} %get-tuple-element.12.refs_2_), channel_id=1, source_target_pairs={{0,8},{24,16},{1,9},{25,17},{2,10},{26,18},{3,11},{27,19},{4,12},{... | collective-permute-start | bytes 1572872 | tf_op jit(solution)/shard_map/ppermute | solution.py:324
  132.8 1.0 copy-start.1
  133.9 24.8 %copy-start.2 = (bf16[64,32,128]{2,1,0:T(8,128)(2,1)S(1)}, bf16[64,32,128]{2,1,0:T(8,128)(2,1)}, u32[]{:S(2)}) copy-start(bf16[64,32,128]{2,1,0:T(8,128)(2,1)} %get-tuple-element.14.refs_2_) | copy-start | bytes 1572868
  133.9 34.8 %copy-start.3 = (bf16[64,32,128]{2,1,0:T(8,128)(2,1)S(1)}, bf16[64,32,128]{2,1,0:T(8,128)(2,1)}, u32[]{:S(2)}) copy-start(bf16[64,32,128]{2,1,0:T(8,128)(2,1)} %get-tuple-element.13.refs_2_) | copy-start | bytes 1572868
  134.0 23.2 %collective-permute-start.3 = (bf16[64,32,128]{2,1,0:T(8,128)(2,1)S(1)}, bf16[64,32,128]{2,1,0:T(8,128)(2,1)S(1)}, u32[]{:S(2)}, u32[]{:S(2)}) collective-permute-start(bf16[64,32,128]{2,1,0:T(8,128)(2,1)S(1)} %merge.12.refs_3_.refs_2_), channel_id=1, source_target_pairs={{8,16},{16,8},{9,17},{17,9},{10,18},{18,10},{11,19},{19,11},{12,20... | collective-permute-start | bytes 1572872 | tf_op jit(solution)/shard_map/ppermute | solution.py:336
  134.8 33.8 %collective-permute-start.7 = (bf16[64,32,128]{2,1,0:T(8,128)(2,1)}, bf16[64,32,128]{2,1,0:T(8,128)(2,1)S(1)}, u32[]{:S(2)}, u32[]{:S(2)}) collective-permute-start(bf16[64,32,128]{2,1,0:T(8,128)(2,1)} %get-tuple-element.13.refs_2_), channel_id=1, source_target_pairs={{0,8},{24,16},{1,9},{25,17},{2,10},{26,18},{3,11},{27,19},{4,12},{... | collective-permute-start | bytes 1572872 | tf_op jit(solution)/shard_map/ppermute | solution.py:324
  155.3 1.0 copy-start.4
  156.5 13.0 %collective-permute-start.6 = (bf16[64,32,128]{2,1,0:T(8,128)(2,1)S(1)}, bf16[64,32,128]{2,1,0:T(8,128)(2,1)S(1)}, u32[]{:S(2)}, u32[]{:S(2)}) collective-permute-start(bf16[64,32,128]{2,1,0:T(8,128)(2,1)S(1)} %merge.13.refs_3_.refs_2_), channel_id=1, source_target_pairs={{8,16},{16,8},{9,17},{17,9},{10,18},{18,10},{11,19},{19,11},{12,20... | collective-permute-start | bytes 1572872 | tf_op jit(solution)/shard_map/ppermute | solution.py:336
  157.3 15.8 %collective-permute-start.5 = (bf16[64,32,128]{2,1,0:T(8,128)(2,1)S(1)}, bf16[64,32,128]{2,1,0:T(8,128)(2,1)}, u32[]{:S(2)}, u32[]{:S(2)}) collective-permute-start(bf16[64,32,128]{2,1,0:T(8,128)(2,1)S(1)} %merge.14.refs_3_.refs_2_), channel_id=1, source_target_pairs={{8,0},{16,24},{9,1},{17,25},{10,2},{18,26},{11,3},{19,27},{12,4},{... | collective-permute-start | bytes 1572872 | tf_op jit(solution)/shard_map/ppermute | solution.py:336
  158.6 20.7 %collective-permute-start.10 = (bf16[64,32,128]{2,1,0:T(8,128)(2,1)S(1)}, bf16[64,32,128]{2,1,0:T(8,128)(2,1)S(1)}, u32[]{:S(2)}, u32[]{:S(2)}) collective-permute-start(bf16[64,32,128]{2,1,0:T(8,128)(2,1)S(1)} %copy-done.2), channel_id=1, source_target_pairs={{0,8},{24,16},{1,9},{25,17},{2,10},{26,18},{3,11},{27,19},{4,12},{... | collective-permute-start | bytes 1572872 | tf_op jit(solution)/shard_map/ppermute | solution.py:324
  168.8 11.4 %collective-permute-start.9 = (bf16[64,32,128]{2,1,0:T(8,128)(2,1)S(1)}, bf16[64,32,128]{2,1,0:T(8,128)(2,1)S(1)}, u32[]{:S(2)}, u32[]{:S(2)}) collective-permute-start(bf16[64,32,128]{2,1,0:T(8,128)(2,1)S(1)} %merge.15.refs_3_.refs_2_), channel_id=1, source_target_pairs={{8,16},{16,8},{9,17},{17,9},{10,18},{18,10},{11,19},{19,11},{12,20... | collective-permute-start | bytes 1572872 | tf_op jit(solution)/shard_map/ppermute | solution.py:336
  169.6 12.0 %collective-permute-start.8 = (bf16[64,32,128]{2,1,0:T(8,128)(2,1)S(1)}, bf16[64,32,128]{2,1,0:T(8,128)(2,1)}, u32[]{:S(2)}, u32[]{:S(2)}) collective-permute-start(bf16[64,32,128]{2,1,0:T(8,128)(2,1)S(1)} %merge.16.refs_3_.refs_2_), channel_id=1, source_target_pairs={{8,0},{16,24},{9,1},{17,25},{10,2},{18,26},{11,3},{19,27},{12,4},{... | collective-permute-start | bytes 1572872 | tf_op jit(solution)/shard_map/ppermute | solution.py:336
  175.1 14.1 %all-to-all-start.3 = ((bf16[8,256,128]{2,1,0:T(8,128)(2,1)}), bf16[8,256,128]{2,1,0:T(8,128)(2,1)}, u32[]{:S(2)}, u32[]{:S(2)}) async-start(bf16[8,256,128]{2,1,0:T(8,128)(2,1)} %bitcast.12), calls=%async_computation.3 | async-start | bytes 1048576 | tf_op jit(solution)/shard_map/all_to_all | solution.py:394
  179.5 13.9 %collective-permute-start.12 = (bf16[64,32,128]{2,1,0:T(8,128)(2,1)S(1)}, bf16[64,32,128]{2,1,0:T(8,128)(2,1)S(1)}, u32[]{:S(2)}, u32[]{:S(2)}) collective-permute-start(bf16[64,32,128]{2,1,0:T(8,128)(2,1)S(1)} %merge.18.refs_3_.refs_2_), channel_id=1, source_target_pairs={{8,16},{16,8},{9,17},{17,9},{10,18},{18,10},{11,19},{19,11},{12,20... | collective-permute-start | bytes 1572872 | tf_op jit(solution)/shard_map/ppermute | solution.py:336
  180.3 26.3 %copy-start.12 = (s32[1,64]{1,0:T(1,128)S(1)}, s32[1,64]{1,0:T(1,128)}, u32[]{:S(2)}) copy-start(s32[1,64]{1,0:T(1,128)} %order_ref.1) | copy-start | bytes 772
  180.3 18.4 %collective-permute-start.11 = (bf16[64,32,128]{2,1,0:T(8,128)(2,1)S(1)}, bf16[64,32,128]{2,1,0:T(8,128)(2,1)S(1)}, u32[]{:S(2)}, u32[]{:S(2)}) collective-permute-start(bf16[64,32,128]{2,1,0:T(8,128)(2,1)S(1)} %merge.19.refs_3_.refs_2_), channel_id=1, source_target_pairs={{8,0},{16,24},{9,1},{17,25},{10,2},{18,26},{11,3},{19,27},{12,4},{... | collective-permute-start | bytes 1572872 | tf_op jit(solution)/shard_map/ppermute | solution.py:336
  189.2 13.9 %all-to-all-start.4 = ((bf16[8,256,128]{2,1,0:T(8,128)(2,1)}), bf16[8,256,128]{2,1,0:T(8,128)(2,1)}, u32[]{:S(2)}, u32[]{:S(2)}) async-start(bf16[8,256,128]{2,1,0:T(8,128)(2,1)} %bitcast.14), calls=%async_computation.4 | async-start | bytes 1048576 | tf_op jit(solution)/shard_map/all_to_all | solution.py:394
  193.5 17.5 %collective-permute-start.13 = (bf16[64,32,128]{2,1,0:T(8,128)(2,1)S(1)}, bf16[64,32,128]{2,1,0:T(8,128)(2,1)S(1)}, u32[]{:S(2)}, u32[]{:S(2)}) collective-permute-start(bf16[64,32,128]{2,1,0:T(8,128)(2,1)S(1)} %merge.21.refs_3_.refs_2_), channel_id=1, source_target_pairs={{8,0},{16,24},{9,1},{17,25},{10,2},{18,26},{11,3},{19,27},{12,4},{... | collective-permute-start | bytes 1572872 | tf_op jit(solution)/shard_map/ppermute | solution.py:336
  203.1 13.2 %all-to-all-start.5 = ((bf16[8,256,128]{2,1,0:T(8,128)(2,1)}), bf16[8,256,128]{2,1,0:T(8,128)(2,1)S(1)}, u32[]{:S(2)}, u32[]{:S(2)}) async-start(bf16[8,256,128]{2,1,0:T(8,128)(2,1)} %bitcast.16), calls=%async_computation.5 | async-start | bytes 1048576 | tf_op jit(solution)/shard_map/all_to_all | solution.py:394
  216.3 13.2 %copy-start.8 = (bf16[8,256,128]{2,1,0:T(8,128)(2,1)}, bf16[8,256,128]{2,1,0:T(8,128)(2,1)S(1)}, u32[]{:S(2)}) copy-start(bf16[8,256,128]{2,1,0:T(8,128)(2,1)S(1)} %all-to-all-done.5) | copy-start | bytes 1572868
  216.3 13.2 %all-to-all-start.6 = ((bf16[8,256,128]{2,1,0:T(8,128)(2,1)}), bf16[8,256,128]{2,1,0:T(8,128)(2,1)S(1)}, u32[]{:S(2)}, u32[]{:S(2)}) async-start(bf16[8,256,128]{2,1,0:T(8,128)(2,1)} %bitcast.18), calls=%async_computation.6 | async-start | bytes 1048576 | tf_op jit(solution)/shard_map/all_to_all | solution.py:394
  229.5 0.8 copy-start.9

commit v3 on v1

v3 whole, which is shorter than its diff:
```python
import math

import jax
import jax.numpy as jnp
import numpy as np
from jax import lax
from jax.experimental import pallas as pl
from jax.experimental.pallas import tpu as pltpu
from jax.sharding import PartitionSpec as P

BLK = 128
RB_DEV = 32
RIM = 64
STEP = 16
CHUNKS = 2
MIB = 1 << 20
SMALL = 24 * MIB
ANY_SPEC = pl.BlockSpec(memory_space=pl.ANY)
VMEM_SPEC = pl.BlockSpec(memory_space=pltpu.VMEM)
HBM_SPEC = pl.BlockSpec(memory_space=pltpu.HBM)
SMEM_SPEC = pl.BlockSpec(memory_space=pltpu.SMEM)


def haar_matrix(order_n):
    matrix = np.ones((1, 1))
    while matrix.shape[0] < order_n:
        length = matrix.shape[0]
        upper = np.kron(matrix, np.array([[1.0, 1.0]]))
        lower = np.kron(np.eye(length), np.array([[1.0, -1.0]]))
        matrix = np.concatenate([upper, lower], axis=0) / math.sqrt(2.0)
    return matrix


def analyze_body(order_ref, sign_ref, scale_ref, model_ref, out_ref, block_ref, sems):
    blocks = model_ref.shape[0]
    copies = [
        pltpu.make_async_copy(model_ref.at[order_ref[0, j]], block_ref.at[j], sems.at[j])
        for j in range(blocks)
    ]
    for copy in copies:
        copy.start()
    for j, copy in enumerate(copies):
        copy.wait()
        x = block_ref[j]
        high = x.astype(jnp.bfloat16)
        low = (x - high.astype(jnp.float32)).astype(jnp.bfloat16)
        raw = jnp.dot(
            sign_ref[...], jnp.concatenate([high, low], axis=0),
            preferred_element_type=jnp.float32,
        )
        out_ref[j] = (raw * scale_ref[...]).astype(jnp.bfloat16)


def analyze(order, model_blocks):
    blocks = model_blocks.shape[0]
    width = model_blocks.shape[2]
    haar = haar_matrix(BLK)
    scale = np.abs(haar).max(axis=1)
    sign = np.sign(haar)
    signs = jnp.asarray(np.concatenate([sign, sign], axis=1), jnp.bfloat16)
    scales = jnp.asarray(np.broadcast_to(scale[:, None], (BLK, width)), jnp.float32)
    return pl.pallas_call(
        analyze_body,
        out_shape=jax.ShapeDtypeStruct((blocks, BLK, width), jnp.bfloat16),
        in_specs=[SMEM_SPEC, VMEM_SPEC, VMEM_SPEC, ANY_SPEC],
        out_specs=VMEM_SPEC,
        scratch_shapes=[
            pltpu.VMEM((blocks, BLK, width), jnp.float32),
            pltpu.SemaphoreType.DMA((blocks,)),
        ],
        compiler_params=pltpu.CompilerParams(vmem_limit_bytes=56 * MIB),
        cost_estimate=pl.CostEstimate(
            flops=4 * blocks * BLK * BLK * width, bytes_accessed=6 * blocks * BLK * width,
            transcendentals=0,
        ),
        name="analyze",
    )(order, signs, scales, model_blocks)


def load_body(sens_ref, after_ref, out_ref, sems):
    pieces = sems.shape[0]
    each = sens_ref.shape[0] // pieces
    copies = [
        pltpu.make_async_copy(
            sens_ref.at[pl.ds(i * each, each)], out_ref.at[pl.ds(i * each, each)], sems.at[i]
        )
        for i in range(pieces)
    ]
    for copy in copies:
        copy.start()
    for copy in copies:
        copy.wait()


def load(sens, after):
    return pl.pallas_call(
        load_body,
        out_shape=pltpu.VMEM(sens.shape, sens.dtype),
        in_specs=[HBM_SPEC, HBM_SPEC],
        out_specs=VMEM_SPEC,
        scratch_shapes=[pltpu.SemaphoreType.DMA((16,))],
        compiler_params=pltpu.CompilerParams(vmem_limit_bytes=SMALL),
        cost_estimate=pl.CostEstimate(
            flops=0, bytes_accessed=4 * sens.size, transcendentals=0
        ),
        name="load",
    )(sens, after)


def forward_body(rows_ref, cols_ref, count_ref, sens_ref, wave_ref, out_ref, acc_ref):
    row_blocks = out_ref.shape[0]
    last = rows_ref.shape[0] - 1
    count = count_ref[0]
    acc_ref[...] = jnp.zeros_like(acc_ref)

    @pl.loop(0, (count + STEP - 1) // STEP)
    def _(step):
        for k in range(STEP):
            place = step * STEP + k
            slot = jnp.minimum(place, last)
            row = jnp.where(place < count, rows_ref[slot], row_blocks)
            acc_ref[row] += jnp.dot(
                sens_ref[slot], wave_ref[cols_ref[slot]], preferred_element_type=jnp.float32
            )

    out_ref[...] = acc_ref[:row_blocks].astype(out_ref.dtype)


def forward(rows, cols, count, sens, wave):
    slots = sens.shape[0]
    width = wave.shape[2]
    return pl.pallas_call(
        forward_body,
        out_shape=jax.ShapeDtypeStruct((RB_DEV, BLK, width), jnp.bfloat16),
        in_specs=[SMEM_SPEC, SMEM_SPEC, SMEM_SPEC, VMEM_SPEC, VMEM_SPEC],
        out_specs=VMEM_SPEC,
        scratch_shapes=[pltpu.VMEM((RB_DEV + 1, BLK, width), jnp.float32)],
        compiler_params=pltpu.CompilerParams(vmem_limit_bytes=SMALL),
        cost_estimate=pl.CostEstimate(
            flops=2 * slots * BLK * BLK * width, bytes_accessed=2 * slots * BLK * BLK,
            transcendentals=0,
        ),
        name="forward",
    )(rows, cols, count, sens, wave)


def adjoint_body(list_ref, bounds_ref, sens_ref, image_ref, out_ref, acc_ref, *, chunk, blocks):
    parts, cols, piece = out_ref.shape[:3]
    first, end = bounds_ref[chunk], bounds_ref[chunk + 1]
    last = list_ref.shape[0] - 1
    acc_ref[...] = jnp.zeros_like(acc_ref)

    @pl.loop(0, (end - first + STEP - 1) // STEP)
    def _(step):
        for k in range(STEP):
            place = first + step * STEP + k
            entry = list_ref[jnp.minimum(place, last)]
            col = jnp.where(place < end, entry % blocks, cols)
            row = (entry // blocks) % RB_DEV
            slot = entry // (blocks * RB_DEV)
            acc_ref[col] += lax.dot_general(
                sens_ref[slot], image_ref[row], (((0,), (0,)), ((), ())),
                preferred_element_type=jnp.float32,
            )

    for r in range(parts):
        out_ref[r] = acc_ref[:cols, r * piece : (r + 1) * piece].astype(out_ref.dtype)


def adjoint(listed, bounds, sens, image, chunk, chunks, blocks, parts):
    slots = sens.shape[0]
    width = image.shape[2]
    cols = blocks // chunks
    return pl.pallas_call(
        lambda *refs: adjoint_body(*refs, chunk=chunk, blocks=blocks),
        out_shape=jax.ShapeDtypeStruct((parts, cols, BLK // parts, width), jnp.bfloat16),
        in_specs=[SMEM_SPEC, SMEM_SPEC, VMEM_SPEC, VMEM_SPEC],
        out_specs=VMEM_SPEC,
        scratch_shapes=[pltpu.VMEM((cols + 1, BLK, width), jnp.float32)],
        compiler_params=pltpu.CompilerParams(vmem_limit_bytes=SMALL),
        cost_estimate=pl.CostEstimate(
            flops=2 * slots * BLK * BLK * width // chunks,
            bytes_accessed=2 * slots * BLK * BLK // chunks, transcendentals=0,
        ),
        name="adjoint",
    )(listed, bounds, sens, image)


def slot_list(rows, cols, count, blocks, per_peer, chunks):
    slots = rows.shape[0]
    each = per_peer // chunks
    slot = lax.iota(jnp.int32, slots)
    peer, q = cols // per_peer, cols % per_peer
    chunk = jnp.where(slot < count, q // each, chunks)
    entry = (slot * RB_DEV + rows) * blocks + peer * each + q % each
    key = chunk * slots + slot
    rank = jnp.sum((key[None, :] < key[:, None]).astype(jnp.int32), axis=1)
    listed = jnp.sum(jnp.where(rank[None, :] == slot[:, None], entry[None, :], 0), axis=1)
    starts = lax.iota(jnp.int32, chunks + 1)
    bounds = jnp.sum((chunk[None, :] < starts[:, None]).astype(jnp.int32), axis=1)
    return listed, bounds


def smooth_body(offset_ref, ext_ref, near_ref, weight_ref, out_ref):
    tiles = out_ref.shape[0] // BLK
    first = pl.program_id(0) * tiles
    span = lax.broadcasted_iota(jnp.int32, (2 * BLK, BLK), 0)
    center = lax.broadcasted_iota(jnp.int32, (2 * BLK, BLK), 1) + RIM
    for t in range(tiles):
        start = (first + t) * BLK
        cells = slice(t * BLK, (t + 1) * BLK)
        near = near_ref[:, cells] - (offset_ref[0] + start)
        face = weight_ref[:, cells]
        total = jnp.sum(face, axis=0, keepdims=True)
        mix = jnp.where(span == center, total, 0.0)
        for k in range(4):
            mix = mix - jnp.where(span == near[k : k + 1], face[k : k + 1], 0.0)
        window = ext_ref[pl.ds(pl.multiple_of(start, BLK), 2 * BLK), :]
        out_ref[cells, :] = lax.dot_general(
            mix, window, (((0,), (0,)), ((), ())),
            precision=lax.Precision.HIGHEST, preferred_element_type=jnp.float32,
        )


def smoothing(offset, extended, neighbors, face_weight):
    cells = neighbors.shape[1]
    width = extended.shape[1]
    per_step = 8 * BLK
    return pl.pallas_call(
        smooth_body,
        out_shape=jax.ShapeDtypeStruct((cells, width), jnp.float32),
        grid_spec=pltpu.PrefetchScalarGridSpec(
            num_scalar_prefetch=1,
            grid=(cells // per_step,),
            in_specs=[
                pl.BlockSpec(extended.shape, lambda i, *_: (0, 0)),
                pl.BlockSpec((4, per_step), lambda i, *_: (0, i)),
                pl.BlockSpec((4, per_step), lambda i, *_: (0, i)),
            ],
            out_specs=pl.BlockSpec((per_step, width), lambda i, *_: (i, 0)),
        ),
        compiler_params=pltpu.CompilerParams(vmem_limit_bytes=24 * MIB),
        cost_estimate=pl.CostEstimate(
            flops=24 * cells * BLK * width, bytes_accessed=16 * cells * width, transcendentals=0
        ),
        name="smoothing",
    )(offset, extended, neighbors, face_weight)


def finish_body(cells_ref, basis_ref, wave_ref, base_ref, out_ref, block_ref, got, put, *, chunk):
    parts, cols = wave_ref.shape[:2]
    fetches, stores = [], []
    for i in range(cols):
        cell = cells_ref[chunk * cols + i]
        fetches.append(pltpu.make_async_copy(base_ref.at[cell], block_ref.at[i], got.at[i]))
        stores.append(pltpu.make_async_copy(block_ref.at[i], out_ref.at[cell], put.at[i]))
    for fetch in fetches:
        fetch.start()
    for i in range(cols):
        pieces = [wave_ref[r, i] for r in range(parts)]
        both = jnp.concatenate(pieces + pieces, axis=0)
        value = jnp.dot(basis_ref[...], both, preferred_element_type=jnp.float32)
        fetches[i].wait()
        block_ref[i] += value
        stores[i].start()
    for store in stores:
        store.wait()


def finish(cells, wave, base, chunk):
    width = base.shape[2]
    cols = wave.shape[1]
    basis = haar_matrix(BLK).T.astype(np.float32)
    high = basis.astype(jnp.bfloat16)
    low = (basis - high.astype(np.float32)).astype(jnp.bfloat16)
    basis2 = jnp.asarray(np.concatenate([high, low], axis=1))
    return pl.pallas_call(
        lambda *refs: finish_body(*refs, chunk=chunk),
        out_shape=jax.ShapeDtypeStruct(base.shape, base.dtype),
        in_specs=[SMEM_SPEC, VMEM_SPEC, VMEM_SPEC, HBM_SPEC],
        out_specs=HBM_SPEC,
        input_output_aliases={3: 0},
        scratch_shapes=[
            pltpu.VMEM((cols, BLK, width), jnp.float32),
            pltpu.SemaphoreType.DMA((cols,)),
            pltpu.SemaphoreType.DMA((cols,)),
        ],
        compiler_params=pltpu.CompilerParams(vmem_limit_bytes=SMALL),
        cost_estimate=pl.CostEstimate(
            flops=4 * cols * BLK * BLK * width, bytes_accessed=10 * cols * BLK * width,
            transcendentals=0,
        ),
        name="finish",
    )(cells, basis2, wave, base)


def extend(block, axis, width):
    count = lax.axis_size(axis)
    forward_pairs = [(i, i + 1) for i in range(count - 1)]
    backward_pairs = [(target, source) for source, target in forward_pairs]
    low = lax.ppermute(block[block.shape[0] - width :], axis, forward_pairs)
    high = lax.ppermute(block[:width], axis, backward_pairs)
    return jnp.concatenate([low, block, high], axis=0)


def local(model_dir, sens_blocks, blk_row, blk_col, blk_count, send_order, neighbors, face_weight):
    cell_count, width = model_dir.shape
    blocks = cell_count // BLK
    col_devices = lax.axis_size("cols")
    row_devices = lax.axis_size("rows")
    per_peer = blocks // col_devices
    piece = BLK // row_devices
    model_blocks = model_dir.reshape(blocks, BLK, width)
    sens = sens_blocks[0]
    chunks = math.gcd(CHUNKS, per_peer)
    each = per_peer // chunks

    outgoing = analyze(send_order, model_blocks)
    wave = lax.all_to_all(
        outgoing.reshape(col_devices, per_peer * BLK, width), "cols", 0, 0, tiled=True
    ).reshape(blocks, BLK, width)
    held = load(sens, outgoing)
    blk_row, blk_col, blk_count, _ = lax.optimization_barrier(
        (blk_row, blk_col, blk_count, outgoing)
    )
    rows, cols, count = blk_row[0], blk_col[0], blk_count[0]
    listed, bounds = slot_list(rows, cols, count[0], blocks, per_peer, chunks)
    cells = send_order.reshape(col_devices, chunks, each).transpose(1, 0, 2).reshape(blocks)

    partial_rows = forward(rows, cols, count, held, wave)
    shares = lax.all_to_all(
        partial_rows.reshape(col_devices, -1, width), "cols", 0, 0, tiled=True
    )
    image_share = jnp.sum(shares.astype(jnp.float32), axis=0).astype(jnp.bfloat16)
    image_half = lax.all_to_all(
        jnp.broadcast_to(image_share, shares.shape), "cols", 0, 0, tiled=True
    ).reshape(-1, width)
    data_image = image_half.astype(jnp.float32)

    image_blocks = image_half.reshape(RB_DEV, BLK, width)
    gathered = []
    for chunk in range(chunks):
        part = adjoint(listed, bounds, held, image_blocks, chunk, chunks, blocks, row_devices)
        got = lax.all_to_all(
            part.reshape(row_devices * col_devices, each * piece, width),
            ("rows", "cols"), 0, 0, tiled=True,
        ).reshape(row_devices, col_devices * each, piece, width)
        total = jnp.sum(got.astype(jnp.float32), axis=0).astype(jnp.bfloat16)
        gathered.append(lax.all_gather(total, "rows", axis=0, tiled=False))
        if chunk == 0:
            model_late, _ = lax.optimization_barrier((model_dir, total))

    extended = extend(model_late, "cols", RIM)
    offset = (lax.axis_index("cols") * cell_count - RIM).astype(jnp.int32).reshape(1)
    normal = smoothing(offset, extended, neighbors, face_weight).reshape(blocks, BLK, width)
    for chunk, wave_back in enumerate(gathered):
        normal = finish(cells, wave_back, normal, chunk)
    return (data_image, normal.reshape(cell_count, width))


def solution(mesh):
    placed = (
        P("cols", None),
        P("rows", "cols", None, None),
        P("rows", "cols"),
        P("rows", "cols"),
        P("rows", "cols"),
        P("cols", None),
        P(None, "cols"),
        P(None, "cols"),
    )
    return jax.shard_map(
        local,
        mesh=mesh,
        in_specs=placed,
        out_specs=(P("rows", None), P("cols", None)),
        check_vma=False,
    )
```

time: 233 us -> 243 us (1.043); the launches traced: 232 us -> 245 us
  blocking collectives: 78.1 us -> 21 us
  Pallas kernels: 29.5 us -> 52.8 us
  waiting for transfers between devices: 73 us -> 92.8 us
  starting transfers between devices: 7.82 us -> 27.3 us
  local copies, waits for them, and re-layouts: 20.9 us -> 27.9 us
    all_to_all x0 -> x3, waiting for transfers between devices: none -> 72.5 us  [the longest x2 57.7 us: local(): lax.all_to_all(part.reshape(row_devices * col_devices, each * piece, widt...]
    all_to_all x1 -> x0, blocking collectives: 57.8 us -> none  [local(): lax.all_to_all(partial_cols.reshape(row_devices * col_devices, per_peer *...]
    all_gather x2, waiting for transfers between devices: 43.5 us -> 2.62 us  [local(): gathered.append(lax.all_gather(total, 'rows', axis=0, tiled=False))]
    all_to_all x0 -> x3, starting transfers between devices: none -> 19.2 us  [the longest x2 15.6 us: local(): lax.all_to_all(part.reshape(row_devices * col_devices, each * piece, widt...]
    pallas_call x2 -> x5, Pallas kernels: 9.25 us -> 22.4 us  [the longest x2 15.4 us: finish(): pl.pallas_call(lambda *refs: finish_body(*refs, chunk=chunk), out_shape=j...]
    all_to_all x1, waiting for transfers between devices: 25.9 us -> 15.8 us  [local(): lax.all_to_all(outgoing.reshape(col_devices, per_peer * BLK, width), 'col...]
    pallas_call x1, Pallas kernels: 4.9 us -> 14.7 us  [analyze(): pl.pallas_call(analyze_body, out_shape=jax.ShapeDtypeStruct((blocks, BLK,...]
    unnamed x30 -> x29, local copies, waits for them, and re-layouts: 20.1 us -> 25.9 us
  transfers between devices with their start and end apart: 5 -> 8, of which waited for: 4 -> 6; matrix products, arithmetic and copies ran while one was open for 2% -> 4% of each run, Pallas kernels for 5% -> 10%
where the time goes in v3:
time: 243 us; the launch traced here: 245 us
  waiting for transfers between devices  92.8 us (38%)
  Pallas kernels  52.8 us (22%)
  local copies, waits for them, and re-layouts  27.9 us (11%)
  starting transfers between devices  27.3 us (11%)
  blocking collectives  21 us (9%)
  between operations  14.9 us (6%)
  other arithmetic  7.82 us (3%)
    all_to_all x2, waiting for transfers between devices, local(): lax.all_to_all(part.reshape(row_devices * col_devices, each * piece, widt...  57.7 us
    unnamed x29, local copies, waits for them, and re-layouts  25.9 us
    all_to_all x1, blocking collectives, local(): lax.all_to_all(partial_rows.reshape(col_devices, -1, width), 'cols', 0, 0...  21 us
    all_to_all x1, waiting for transfers between devices, local(): lax.all_to_all(outgoing.reshape(col_devices, per_peer * BLK, width), 'col...  15.8 us
    all_to_all x2, starting transfers between devices, local(): lax.all_to_all(part.reshape(row_devices * col_devices, each * piece, widt...  15.6 us
    pallas_call x2, Pallas kernels, finish(): pl.pallas_call(lambda *refs: finish_body(*refs, chunk=chunk), out_shape=j...  15.4 us
    all_to_all x1, waiting for transfers between devices, local(): lax.all_to_all(jnp.broadcast_to(image_share, shares.shape), 'cols', 0, 0,...  14.8 us
    pallas_call x1, Pallas kernels, analyze(): pl.pallas_call(analyze_body, out_shape=jax.ShapeDtypeStruct((blocks, BLK,...  14.7 us
  transfers between devices with their start and end apart: 8, of which 6 were waited for; matrix products, arithmetic and copies ran while one was open for 4% of the time, Pallas kernels for 10%

profile of v3, /device:TPU:0, one launch (start us, length us, event | category | flops | bytes accessed | tf_op | source)
XLA Modules:
  0.0 244.6 jit_solution(7048872832923372731)
XLA Ops:
  7.2 14.7 %analyze.1.after_ref = bf16[64,128,128]{2,1,0:T(8,128)(2,1)} custom-call(s32[1,64]{1,0:T(1,128)} %order_ref.1, bf16[128,256]{1,0:T(8,128)(2,1)} %constant.78.clone.sign_ref, f32[128,128]{1,0:T(8,128)} %constant.79.clone.scale_ref, f32[64,128,128]{2,1,0:T(8,128)} %bitcast.31), custom_call_target="tpu_custom_call" | custom-call | flops 536870912 | bytes 6291456 | tf_op jit(solution)/shard_map/analyze/pallas_call | solution.py:62
  21.8 0.0 copy-start.4
  21.8 5.3 %all-to-all-start = ((bf16[8,1024,128]{2,1,0:T(8,128)(2,1)}), bf16[8,1024,128]{2,1,0:T(8,128)(2,1)}, u32[]{:S(2)}, u32[]{:S(2)}) async-start(bf16[8,1024,128]{2,1,0:T(8,128)(2,1)} %bitcast.24), calls=%async_computation | async-start | bytes 4194304 | tf_op jit(solution)/shard_map/all_to_all | solution.py:319
  27.8 0.0 copy-done.4
  27.8 0.0 copy-start.5
  27.8 4.6 %copy-done.5 = bf16[1,384,128,128]{3,2,1,0:T(8,128)(2,1)S(1)} copy-done((bf16[1,384,128,128]{3,2,1,0:T(8,128)(2,1)S(1)}, bf16[1,384,128,128]{3,2,1,0:T(8,128)(2,1)}, u32[]{:S(2)}) %copy-start.5) | copy-done | bytes 12582936
  32.4 0.0 copy-start.11
  32.4 0.0 copy-start.12
  32.4 1.0 load.1.sens_ref.refs_2_
  33.4 0.0 copy-start
  33.4 4.6 %copy-done = bf16[384,128,128]{2,1,0:T(8,128)(2,1)} copy-done((bf16[384,128,128]{2,1,0:T(8,128)(2,1)}, bf16[384,128,128]{2,1,0:T(8,128)(2,1)S(1)}, u32[]{:S(2)}) %copy-start) | copy-done | bytes 12582936
  38.0 0.0 copy-done.11
  38.0 0.0 copy-done.12
  38.1 15.8 %all-to-all-done = bf16[8,1024,128]{2,1,0:T(8,128)(2,1)} async-done(((bf16[8,1024,128]{2,1,0:T(8,128)(2,1)}), bf16[8,1024,128]{2,1,0:T(8,128)(2,1)}, u32[]{:S(2)}, u32[]{:S(2)}) %all-to-all-start) | async-done | bytes 2097184 | tf_op jit(solution)/shard_map/all_to_all | solution.py:319
  53.9 0.0 copy-start.1
  53.9 4.6 %copy-done.1 = bf16[384,128,128]{2,1,0:T(8,128)(2,1)S(1)} copy-done((bf16[384,128,128]{2,1,0:T(8,128)(2,1)S(1)}, bf16[384,128,128]{2,1,0:T(8,128)(2,1)}, u32[]{:S(2)}) %copy-start.1) | copy-done | bytes 12582936
  58.5 3.1 %forward.1 = bf16[32,128,128]{2,1,0:T(8,128)(2,1)S(1)} custom-call(s32[384]{0:T(512)S(1)} %get-tuple-element.13.rows_ref, s32[384]{0:T(512)S(1)} %get-tuple-element.14.cols_ref, s32[1]{0:T(128)} %bitcast.21.count_ref, bf16[384,128,128]{2,1,0:T(8,128)(2,1)S(1)} %copy-done.1, bf16[64,128,128]{2,1,0:T(8,128)(2,1)} %bitcast.4.wave_ref), custom_call_target="tpu_custom_call" | custom-call | flops 1610612736 | bytes 12582912 | tf_op jit(solution)/shard_map/forward/pallas_call | solution.py:132
  61.6 21.0 %all_to_all.25 = bf16[8,512,128]{2,1,0:T(8,128)(2,1)S(1)} all-to-all(bf16[8,512,128]{2,1,0:T(8,128)(2,1)S(1)} %bitcast.28), channel_id=1, replica_groups=mesh['rows'=4,'cols'=8] {'cols'}, dimensions={0} | all-to-all | bytes 2097152 | tf_op jit(solution)/shard_map/all_to_all | solution.py:331
  82.5 0.1 reduce_sum.63
  82.7 1.1 broadcast_in_dim.26
  83.8 3.6 %all-to-all-start.2 = ((bf16[8,512,128]{2,1,0:T(8,128)(2,1)}), bf16[8,512,128]{2,1,0:T(8,128)(2,1)S(1)}, u32[]{:S(2)}, u32[]{:S(2)}) async-start(bf16[8,512,128]{2,1,0:T(8,128)(2,1)} %broadcast_in_dim.26), calls=%async_computation.2 | async-start | bytes 2097152 | tf_op jit(solution)/shard_map/all_to_all | solution.py:335
  87.4 0.1 convert_reduce_fusion.1.refs_1_
  87.5 0.2 convert_reduce_fusion
  87.7 0.2 select_reduce_fusion.refs_0_
  87.9 14.8 %all-to-all-done.2 = bf16[8,512,128]{2,1,0:T(8,128)(2,1)S(1)} async-done(((bf16[8,512,128]{2,1,0:T(8,128)(2,1)}), bf16[8,512,128]{2,1,0:T(8,128)(2,1)S(1)}, u32[]{:S(2)}, u32[]{:S(2)}) %all-to-all-start.2) | async-done | bytes 1048608 | tf_op jit(solution)/shard_map/all_to_all | solution.py:335
  102.7 0.0 copy-start.2
  102.7 4.6 %copy-done.2 = bf16[384,128,128]{2,1,0:T(8,128)(2,1)S(1)} copy-done((bf16[384,128,128]{2,1,0:T(8,128)(2,1)S(1)}, bf16[384,128,128]{2,1,0:T(8,128)(2,1)}, u32[]{:S(2)}) %copy-start.2) | copy-done | bytes 12582936
  107.3 2.7 %adjoint.3 = bf16[4,32,32,128]{3,2,1,0:T(8,128)(2,1)} custom-call(s32[384]{0:T(512)S(1)} %select_reduce_fusion.refs_0_, s32[3]{0:T(128)S(1)} %convert_reduce_fusion.1.refs_1_, bf16[384,128,128]{2,1,0:T(8,128)(2,1)S(1)} %copy-done.2, bf16[32,128,128]{2,1,0:T(8,128)(2,1)S(1)} %bitcast.25), custom_call_target="tpu_custom_call" | custom-call | flops 805306368 | bytes 6291456 | tf_op jit(solution)/shard_map/adjoint/pallas_call | solution.py:174
  110.0 12.0 %all-to-all-start.4 = ((bf16[32,128,128]{2,1,0:T(8,128)(2,1)}), bf16[32,128,128]{2,1,0:T(8,128)(2,1)S(1)}, u32[]{:S(2)}, u32[]{:S(2)}) async-start(bf16[32,128,128]{2,1,0:T(8,128)(2,1)} %bitcast.13), calls=%async_computation.4 | async-start | bytes 2097152 | tf_op jit(solution)/shard_map/all_to_all | solution.py:344
  122.0 0.0 copy-start.3
  122.0 4.6 %copy-done.3 = bf16[384,128,128]{2,1,0:T(8,128)(2,1)S(1)} copy-done((bf16[384,128,128]{2,1,0:T(8,128)(2,1)S(1)}, bf16[384,128,128]{2,1,0:T(8,128)(2,1)}, u32[]{:S(2)}) %copy-start.3) | copy-done | bytes 12582936
  126.6 0.0 copy-start.13
  126.6 3.2 %adjoint.2 = bf16[4,32,32,128]{3,2,1,0:T(8,128)(2,1)} custom-call(s32[384]{0:T(512)S(1)} %select_reduce_fusion.refs_0_, s32[3]{0:T(128)S(1)} %convert_reduce_fusion.1.refs_1_, bf16[384,128,128]{2,1,0:T(8,128)(2,1)S(1)} %copy-done.3, bf16[32,128,128]{2,1,0:T(8,128)(2,1)S(1)} %bitcast.26), custom_call_target="tpu_custom_call" | custom-call | flops 805306368 | bytes 6291456 | tf_op jit(solution)/shard_map/adjoint/pallas_call | solution.py:174
  129.8 18.4 %all-to-all-done.4 = bf16[32,128,128]{2,1,0:T(8,128)(2,1)S(1)} async-done(((bf16[32,128,128]{2,1,0:T(8,128)(2,1)}), bf16[32,128,128]{2,1,0:T(8,128)(2,1)S(1)}, u32[]{:S(2)}, u32[]{:S(2)}) %all-to-all-start.4) | async-done | bytes 1048608 | tf_op jit(solution)/shard_map/all_to_all | solution.py:344
  148.2 3.6 %all-to-all-start.3 = ((bf16[32,128,128]{2,1,0:T(8,128)(2,1)}), bf16[32,128,128]{2,1,0:T(8,128)(2,1)S(1)}, u32[]{:S(2)}, u32[]{:S(2)}) async-start(bf16[32,128,128]{2,1,0:T(8,128)(2,1)} %bitcast.10), calls=%async_computation.3 | async-start | bytes 2097152 | tf_op jit(solution)/shard_map/all_to_all | solution.py:344
  151.9 0.0 all-gather.7.cloned.1.call-start
  151.9 0.9 reduce_sum.68
  152.8 0.0 all-gather.7.cloned.1.call-update
  152.9 0.0 all-gather.5.cloned.1.call-start
  152.9 0.5 broadcast.167
  153.4 0.0 copy-done.13
  153.4 0.7 reduce.13
  154.1 0.1 reshape.110
  154.2 0.1 reshape.111.refs_0_
  154.3 39.3 %all-to-all-done.3 = bf16[32,128,128]{2,1,0:T(8,128)(2,1)S(1)} async-done(((bf16[32,128,128]{2,1,0:T(8,128)(2,1)}), bf16[32,128,128]{2,1,0:T(8,128)(2,1)S(1)}, u32[]{:S(2)}, u32[]{:S(2)}) %all-to-all-start.3) | async-done | bytes 1048608 | tf_op jit(solution)/shard_map/all_to_all | solution.py:344
  193.6 0.9 reduce_sum.67
  194.5 0.8 fusion.9
  195.2 1.3 collective-permute-start
  196.5 1.5 collective-permute-start.1
  198.0 0.0 all-gather.5.cloned.1.call-update
  198.0 1.5 bitcast_convert_fusion
  199.6 0.0 collective-permute-done
  199.6 1.8 collective-permute-done.1
  201.4 3.1 %pad_maximum_fusion.ext_ref = f32[8320,128]{1,0:T(8,128)S(1)} fusion(f32[64,128]{1,0:T(8,128)S(1)} %collective-permute-done.1, f32[8192,128]{1,0:T(8,128)} %param.12, f32[64,128]{1,0:T(8,128)S(1)} %collective-permute-done), kind=kLoop, calls=%fused_computation | loop fusion | flops 2129920 | bytes 8519680 | tf_op jit(solution)/shard_map/concatenate | solution.py:303
  204.5 0.0 copy-done.9
  204.5 0.0 copy-done.10
  204.5 0.0 copy-start.8
  204.5 12.7 %smoothing.1 = f32[8192,128]{1,0:T(8,128)} custom-call(s32[1]{0:T(128)} %bitcast.16.offset_ref, f32[8320,128]{1,0:T(8,128)S(1)} %pad_maximum_fusion.ext_ref, s32[4,8192]{1,0:T(4,128)S(1)} %copy-done.9, f32[4,8192]{1,0:T(4,128)S(1)} %copy-done.10), custom_call_target="tpu_custom_call" | custom-call | flops 3221225472 | bytes 16777216 | tf_op jit(solution)/shard_map/smoothing/pallas_call | solution.py:229
  217.2 0.0 copy-done.8
  217.2 1.2 copy-done.6
  218.4 7.7 %finish.2.refs_3_ = f32[64,128,128]{2,1,0:T(8,128)} custom-call(s32[64]{0:T(128)S(1)} %reshape.111.refs_0_, bf16[128,256]{1,0:T(8,128)(2,1)S(1)} %copy-done.8, bf16[4,32,32,128]{3,2,1,0:T(8,128)(2,1)S(1)} %bitcast.29, f32[64,128,128]{2,1,0:T(8,128)} %bitcast.32), custom_call_target="tpu_custom_call", output_to_operand_aliasing={{}: (3, {})} | custom-call | flops 268435456 | bytes 5242880 | tf_op jit(solution)/shard_map/finish/pallas_call | solution.py:277
  226.1 2.6 %all-gather.5.cloned.1.call-done = bf16[128,32,128]{2,1,0:T(8,128)(2,1)} async-done(((bf16[32,32,128]{2,1,0:T(8,128)(2,1)}), bf16[128,32,128]{2,1,0:T(8,128)(2,1)}) %all-gather.5.cloned.1.call-update) | async-done | bytes 1048592 | tf_op jit(solution)/shard_map/all_gather | solution.py:349
  228.7 1.2 copy-done.7
  230.0 7.7 %finish.3 = f32[64,128,128]{2,1,0:T(8,128)} custom-call(s32[64]{0:T(128)S(1)} %reshape.111.refs_0_, bf16[128,256]{1,0:T(8,128)(2,1)S(1)} %copy-done.8, bf16[4,32,32,128]{3,2,1,0:T(8,128)(2,1)S(1)} %bitcast.30, f32[64,128,128]{2,1,0:T(8,128)} %finish.2.refs_3_), custom_call_target="tpu_custom_call", output_to_operand_aliasing={{}: (3, {})} | custom-call | flops 268435456 | bytes 5242880 | tf_op jit(solution)/shard_map/finish/pallas_call | solution.py:277
  (10 shorter events, 0.1 us)
Async XLA Ops:
  21.8 6.0 %copy-start.4 = (bf16[64,128,128]{2,1,0:T(8,128)(2,1)S(1)}, bf16[64,128,128]{2,1,0:T(8,128)(2,1)}, u32[]{:S(2)}) copy-start(bf16[64,128,128]{2,1,0:T(8,128)(2,1)} %analyze.1.after_ref) | copy-start | bytes 6291460
  21.8 32.1 %all-to-all-start = ((bf16[8,1024,128]{2,1,0:T(8,128)(2,1)}), bf16[8,1024,128]{2,1,0:T(8,128)(2,1)}, u32[]{:S(2)}, u32[]{:S(2)}) async-start(bf16[8,1024,128]{2,1,0:T(8,128)(2,1)} %bitcast.24), calls=%async_computation | async-start | bytes 4194304 | tf_op jit(solution)/shard_map/all_to_all | solution.py:319
  27.8 4.6 %copy-start.5 = (bf16[1,384,128,128]{3,2,1,0:T(8,128)(2,1)S(1)}, bf16[1,384,128,128]{3,2,1,0:T(8,128)(2,1)}, u32[]{:S(2)}) copy-start(bf16[1,384,128,128]{3,2,1,0:T(8,128)(2,1)} %param.13) | copy-start | bytes 37748740
  32.4 5.6 %copy-start.11 = (s32[1,384]{1,0:T(1,128)S(1)}, s32[1,384]{1,0:T(1,128)}, u32[]{:S(2)}) copy-start(s32[1,384]{1,0:T(1,128)} %param.15) | copy-start | bytes 4612
  32.4 5.6 %copy-start.12 = (s32[1,384]{1,0:T(1,128)S(1)}, s32[1,384]{1,0:T(1,128)}, u32[]{:S(2)}) copy-start(s32[1,384]{1,0:T(1,128)} %param.14) | copy-start | bytes 4612
  33.4 4.6 %copy-start = (bf16[384,128,128]{2,1,0:T(8,128)(2,1)}, bf16[384,128,128]{2,1,0:T(8,128)(2,1)S(1)}, u32[]{:S(2)}) copy-start(bf16[384,128,128]{2,1,0:T(8,128)(2,1)S(1)} %load.1.sens_ref.refs_2_) | copy-start | bytes 37748740
  53.9 4.6 %copy-start.1 = (bf16[384,128,128]{2,1,0:T(8,128)(2,1)S(1)}, bf16[384,128,128]{2,1,0:T(8,128)(2,1)}, u32[]{:S(2)}) copy-start(bf16[384,128,128]{2,1,0:T(8,128)(2,1)} %copy-done) | copy-start | bytes 37748740
  83.8 18.9 %all-to-all-start.2 = ((bf16[8,512,128]{2,1,0:T(8,128)(2,1)}), bf16[8,512,128]{2,1,0:T(8,128)(2,1)S(1)}, u32[]{:S(2)}, u32[]{:S(2)}) async-start(bf16[8,512,128]{2,1,0:T(8,128)(2,1)} %broadcast_in_dim.26), calls=%async_computation.2 | async-start | bytes 2097152 | tf_op jit(solution)/shard_map/all_to_all | solution.py:335
  102.7 4.6 %copy-start.2 = (bf16[384,128,128]{2,1,0:T(8,128)(2,1)S(1)}, bf16[384,128,128]{2,1,0:T(8,128)(2,1)}, u32[]{:S(2)}) copy-start(bf16[384,128,128]{2,1,0:T(8,128)(2,1)} %copy-done) | copy-start | bytes 37748740
  110.0 38.2 %all-to-all-start.4 = ((bf16[32,128,128]{2,1,0:T(8,128)(2,1)}), bf16[32,128,128]{2,1,0:T(8,128)(2,1)S(1)}, u32[]{:S(2)}, u32[]{:S(2)}) async-start(bf16[32,128,128]{2,1,0:T(8,128)(2,1)} %bitcast.13), calls=%async_computation.4 | async-start | bytes 2097152 | tf_op jit(solution)/shard_map/all_to_all | solution.py:344
  122.0 4.6 %copy-start.3 = (bf16[384,128,128]{2,1,0:T(8,128)(2,1)S(1)}, bf16[384,128,128]{2,1,0:T(8,128)(2,1)}, u32[]{:S(2)}) copy-start(bf16[384,128,128]{2,1,0:T(8,128)(2,1)} %copy-done) | copy-start | bytes 37748740
  126.6 26.9 %copy-start.13 = (s32[1,64]{1,0:T(1,128)S(1)}, s32[1,64]{1,0:T(1,128)}, u32[]{:S(2)}) copy-start(s32[1,64]{1,0:T(1,128)} %order_ref.1) | copy-start | bytes 772
  148.2 45.3 %all-to-all-start.3 = ((bf16[32,128,128]{2,1,0:T(8,128)(2,1)}), bf16[32,128,128]{2,1,0:T(8,128)(2,1)S(1)}, u32[]{:S(2)}, u32[]{:S(2)}) async-start(bf16[32,128,128]{2,1,0:T(8,128)(2,1)} %bitcast.10), calls=%async_computation.3 | async-start | bytes 2097152 | tf_op jit(solution)/shard_map/all_to_all | solution.py:344
  151.9 65.3 %all-gather.7.cloned.1.call-start = ((), (), s32[]{:S(2)}) async-start(), calls=%async_computation.6 | async-start | bytes 1310720 | tf_op jit(solution)/shard_map/all_gather | solution.py:349
  152.9 75.9 %all-gather.5.cloned.1.call-start = ((), (), s32[]{:S(2)}) async-start(), calls=%async_computation.5 | async-start | bytes 1310720 | tf_op jit(solution)/shard_map/all_gather | solution.py:349
  195.2 4.3 %collective-permute-start = (f32[64,128]{1,0:T(8,128)S(1)}, f32[64,128]{1,0:T(8,128)S(1)}, u32[]{:S(2)}, u32[]{:S(2)}) collective-permute-start(f32[64,128]{1,0:T(8,128)S(1)} %get-tuple-element.18), channel_id=1, source_target_pairs={{0,1},{1,2},{2,3},{3,4},{4,5},{5,6},{6,7},{8,9},{9,10},{10,11},{11... | collective-permute-start | bytes 98312 | tf_op jit(solution)/shard_map/ppermute | solution.py:301
  196.5 4.9 %collective-permute-start.1 = (f32[64,128]{1,0:T(8,128)S(1)}, f32[64,128]{1,0:T(8,128)S(1)}, u32[]{:S(2)}, u32[]{:S(2)}) collective-permute-start(f32[64,128]{1,0:T(8,128)S(1)} %get-tuple-element.19), channel_id=1, source_target_pairs={{1,0},{2,1},{3,2},{4,3},{5,4},{6,5},{7,6},{9,8},{10,9},{11,10},{12... | collective-permute-start | bytes 98312 | tf_op jit(solution)/shard_map/ppermute | solution.py:302
  199.6 4.9 %copy-start.9 = (s32[4,8192]{1,0:T(4,128)S(1)}, s32[4,8192]{1,0:T(4,128)}, u32[]{:S(2)}) copy-start(s32[4,8192]{1,0:T(4,128)} %near_ref.1) | copy-start | bytes 393220
  199.6 4.9 %copy-start.10 = (f32[4,8192]{1,0:T(4,128)S(1)}, f32[4,8192]{1,0:T(4,128)}, u32[]{:S(2)}) copy-start(f32[4,8192]{1,0:T(4,128)} %weight_ref.1) | copy-start | bytes 393220
  204.5 12.7 %copy-start.8 = (bf16[128,256]{1,0:T(8,128)(2,1)S(1)}, bf16[128,256]{1,0:T(8,128)(2,1)}, u32[]{:S(2)}) copy-start(bf16[128,256]{1,0:T(8,128)(2,1)} %constant.80.clone.refs_1_) | copy-start | bytes 196612
  217.2 1.2 copy-start.6
  228.7 1.2 copy-start.7
Sparse Core Ops, SparseCore 0:
  154.3 41.0 all-gather.6
  198.2 30.5 all-gather.4

commit v4 on v3

v4 whole, which is shorter than its diff:
```python
import math

import jax
import jax.numpy as jnp
import numpy as np
from jax import lax
from jax.experimental import pallas as pl
from jax.experimental.pallas import tpu as pltpu
from jax.sharding import PartitionSpec as P

BLK = 128
RB_DEV = 32
RIM = 64
STEP = 16
CHUNKS = 4
MIB = 1 << 20
SMALL = 16 * MIB
LARGE = 56 * MIB
ANY_SPEC = pl.BlockSpec(memory_space=pl.ANY)
VMEM_SPEC = pl.BlockSpec(memory_space=pltpu.VMEM)
SMEM_SPEC = pl.BlockSpec(memory_space=pltpu.SMEM)


def haar_matrix(order_n):
    matrix = np.ones((1, 1))
    while matrix.shape[0] < order_n:
        length = matrix.shape[0]
        upper = np.kron(matrix, np.array([[1.0, 1.0]]))
        lower = np.kron(np.eye(length), np.array([[1.0, -1.0]]))
        matrix = np.concatenate([upper, lower], axis=0) / math.sqrt(2.0)
    return matrix


def fetch(source, target, sems, pieces):
    each = source.shape[0] // pieces
    parts = [pl.ds(i * each, each) for i in range(pieces)]
    return [
        pltpu.make_async_copy(source.at[part], target.at[part], sems.at[i])
        for i, part in enumerate(parts)
    ]


def start_all(copies):
    for copy in copies:
        copy.start()


def wait_all(copies):
    for copy in copies:
        copy.wait()


def analyze_body(order_ref, model_ref, out_ref, block_ref, coeff_ref, got, put):
    blocks, _, width = model_ref.shape
    steps = put.shape[0]
    each = blocks // steps
    loads = fetch(model_ref, block_ref, got, got.shape[0])
    start_all(loads)
    row = lax.broadcasted_iota(jnp.int32, (BLK, BLK), 0)
    col = lax.broadcasted_iota(jnp.int32, (BLK, BLK), 1)
    level = jnp.ones_like(row)
    scale = jnp.full((BLK, width), BLK**-0.5, jnp.float32)
    wide_row = lax.broadcasted_iota(jnp.int32, (BLK, width), 0)
    size = 2
    while size < BLK:
        level = jnp.where(row >= size, size, level)
        scale = jnp.where(wide_row >= size, (size / BLK) ** 0.5, scale)
        size *= 2
    span = BLK // level
    inside = col - (row - level) * span
    sign = jnp.where(inside * 2 < span, 1.0, -1.0)
    sign = jnp.where((inside >= 0) & (inside < span), sign, 0.0)
    sign = jnp.where(row == 0, 1.0, sign).astype(jnp.bfloat16)
    both_signs = jnp.concatenate([sign, sign], axis=1)
    stores = fetch(coeff_ref, out_ref, put, steps)
    wait_all(loads)
    for step in range(steps):
        for j in range(step * each, (step + 1) * each):
            x = block_ref[order_ref[0, j]]
            high = x.astype(jnp.bfloat16)
            low = (x - high.astype(jnp.float32)).astype(jnp.bfloat16)
            raw = jnp.dot(
                both_signs, jnp.concatenate([high, low], axis=0),
                preferred_element_type=jnp.float32,
            )
            coeff_ref[j] = (raw * scale).astype(jnp.bfloat16)
        stores[step].start()
    wait_all(stores)


def analyze(order, model_blocks):
    blocks, _, width = model_blocks.shape
    return pl.pallas_call(
        analyze_body,
        out_shape=jax.ShapeDtypeStruct((blocks, BLK, width), jnp.bfloat16),
        in_specs=[SMEM_SPEC, ANY_SPEC],
        out_specs=ANY_SPEC,
        scratch_shapes=[
            pltpu.VMEM((blocks, BLK, width), jnp.float32),
            pltpu.VMEM((blocks, BLK, width), jnp.bfloat16),
            pltpu.SemaphoreType.DMA((16,)),
            pltpu.SemaphoreType.DMA((4,)),
        ],
        compiler_params=pltpu.CompilerParams(vmem_limit_bytes=LARGE),
        cost_estimate=pl.CostEstimate(
            flops=4 * blocks * BLK * BLK * width, bytes_accessed=6 * blocks * BLK * width,
            transcendentals=0,
        ),
        name="analyze",
    )(order, model_blocks)


def slot_loop(count, sens_ref, block_ref, sems, others, work):
    steps = sems.shape[0]
    each = sens_ref.shape[0] // steps

    def block_copy(step):
        part = pl.ds(step * each, each)
        return pltpu.make_async_copy(sens_ref.at[part], block_ref.at[part], sems.at[step])

    start_all(others)
    needed = (count + each - 1) // each

    @pl.loop(0, needed)
    def _(step):
        block_copy(step).start()

    wait_all(others)

    @pl.loop(0, needed)
    def _(step):
        block_copy(step).wait()
        for k in range(each):
            slot = step * each + k
            work(slot, block_ref[slot], slot < count)


def forward_body(rows_ref, cols_ref, count_ref, sens_ref, wave_ref, out_ref,
                 block_ref, held_ref, acc_ref, half_ref, sems, got, put):
    row_blocks = out_ref.shape[0]
    acc_ref[...] = jnp.zeros_like(acc_ref)

    def work(slot, block, live):
        row = jnp.where(live, rows_ref[0, slot], row_blocks)
        acc_ref[row] += jnp.dot(
            block, held_ref[cols_ref[0, slot]], preferred_element_type=jnp.float32
        )

    waves = fetch(wave_ref, held_ref, got, got.shape[0])
    slot_loop(count_ref[0, 0], sens_ref, block_ref, sems, waves, work)
    half_ref[...] = acc_ref[:row_blocks].astype(half_ref.dtype)
    stores = fetch(half_ref, out_ref, put, put.shape[0])
    start_all(stores)
    wait_all(stores)


def forward(rows, cols, count, sens, wave):
    slots = sens.shape[0]
    width = wave.shape[2]
    return pl.pallas_call(
        forward_body,
        out_shape=jax.ShapeDtypeStruct((RB_DEV, BLK, width), jnp.bfloat16),
        in_specs=[SMEM_SPEC, SMEM_SPEC, SMEM_SPEC, ANY_SPEC, ANY_SPEC],
        out_specs=ANY_SPEC,
        scratch_shapes=[
            pltpu.VMEM(sens.shape, sens.dtype),
            pltpu.VMEM(wave.shape, wave.dtype),
            pltpu.VMEM((RB_DEV + 1, BLK, width), jnp.float32),
            pltpu.VMEM((RB_DEV, BLK, width), jnp.bfloat16),
            pltpu.SemaphoreType.DMA((slots // STEP,)),
            pltpu.SemaphoreType.DMA((8,)),
            pltpu.SemaphoreType.DMA((4,)),
        ],
        compiler_params=pltpu.CompilerParams(vmem_limit_bytes=LARGE),
        cost_estimate=pl.CostEstimate(
            flops=2 * slots * BLK * BLK * width, bytes_accessed=2 * slots * BLK * BLK,
            transcendentals=0,
        ),
        name="forward",
    )(rows, cols, count, sens, wave)


def adjoint_body(rows_ref, cols_ref, count_ref, sens_ref, image_ref, after_ref, *refs, per_peer):
    chunks = len(refs) - 7
    out_refs = refs[:chunks]
    block_ref, held_ref, acc_ref, half_ref, sems, got, put = refs[chunks:]
    cols = acc_ref.shape[0] - 1
    peers, each = cols // per_peer, per_peer // chunks
    acc_ref[...] = jnp.zeros_like(acc_ref)

    def work(slot, block, live):
        col = jnp.where(live, cols_ref[0, slot], cols)
        acc_ref[col] += lax.dot_general(
            block, held_ref[rows_ref[0, slot]], (((0,), (0,)), ((), ())),
            preferred_element_type=jnp.float32,
        )

    images = fetch(image_ref, held_ref, got, got.shape[0])
    slot_loop(count_ref[0, 0], sens_ref, block_ref, sems, images, work)
    stores = []
    for chunk, out_ref in enumerate(out_refs):
        for peer in range(peers):
            first = peer * per_peer + chunk * each
            half_ref[chunk, peer * each : (peer + 1) * each] = acc_ref[
                first : first + each
            ].astype(half_ref.dtype)
        stores.append(pltpu.make_async_copy(half_ref.at[chunk], out_ref, put.at[chunk]))
        stores[-1].start()
    wait_all(stores)


def adjoint(rows, cols, count, sens, image, after, blocks, per_peer, chunks):
    slots = sens.shape[0]
    width = image.shape[2]
    chunk = (blocks // chunks, BLK, width)
    return pl.pallas_call(
        lambda *refs: adjoint_body(*refs, per_peer=per_peer),
        out_shape=[jax.ShapeDtypeStruct(chunk, jnp.bfloat16)] * chunks,
        in_specs=[SMEM_SPEC, SMEM_SPEC, SMEM_SPEC, ANY_SPEC, ANY_SPEC, ANY_SPEC],
        out_specs=[ANY_SPEC] * chunks,
        scratch_shapes=[
            pltpu.VMEM(sens.shape, sens.dtype),
            pltpu.VMEM(image.shape, image.dtype),
            pltpu.VMEM((blocks + 1, BLK, width), jnp.float32),
            pltpu.VMEM((chunks, *chunk), jnp.bfloat16),
            pltpu.SemaphoreType.DMA((slots // STEP,)),
            pltpu.SemaphoreType.DMA((4,)),
            pltpu.SemaphoreType.DMA((chunks,)),
        ],
        compiler_params=pltpu.CompilerParams(vmem_limit_bytes=LARGE),
        cost_estimate=pl.CostEstimate(
            flops=2 * slots * BLK * BLK * width, bytes_accessed=2 * slots * BLK * BLK,
            transcendentals=0,
        ),
        name="adjoint",
    )(rows, cols, count, sens, image, after)


def smooth_body(offset_ref, low_ref, model_ref, high_ref, near_ref, weight_ref, after_ref,
                out_ref, ext_ref, value_ref, got, ends, put):
    cells = model_ref.shape[0]
    steps = put.shape[0]
    tiles = cells // BLK // steps
    each = cells // got.shape[0]
    loads = [
        pltpu.make_async_copy(
            model_ref.at[pl.ds(i * each, each)], ext_ref.at[pl.ds(RIM + i * each, each)], got.at[i]
        )
        for i in range(got.shape[0])
    ]
    loads.append(pltpu.make_async_copy(low_ref, ext_ref.at[pl.ds(0, RIM)], ends.at[0]))
    loads.append(
        pltpu.make_async_copy(high_ref, ext_ref.at[pl.ds(RIM + cells, RIM)], ends.at[1])
    )
    start_all(loads)
    wait_all(loads)
    span = lax.broadcasted_iota(jnp.int32, (2 * BLK, BLK), 0)
    center = lax.broadcasted_iota(jnp.int32, (2 * BLK, BLK), 1) + RIM

    def store(step):
        part = pl.ds(step * tiles * BLK, tiles * BLK)
        return pltpu.make_async_copy(value_ref.at[part], out_ref.at[part], put.at[step])

    @pl.loop(0, steps)
    def _(step):
        for t in range(tiles):
            start = pl.multiple_of((step * tiles + t) * BLK, BLK)
            near = near_ref[:, pl.ds(start, BLK)] - (offset_ref[0] + start)
            face = weight_ref[:, pl.ds(start, BLK)]
            mix = jnp.where(span == center, jnp.sum(face, axis=0, keepdims=True), 0.0)
            for k in range(4):
                mix = mix - jnp.where(span == near[k : k + 1], face[k : k + 1], 0.0)
            window = ext_ref[pl.ds(start, 2 * BLK), :]
            mix_high = mix.astype(jnp.bfloat16)
            mix_low = (mix - mix_high.astype(jnp.float32)).astype(jnp.bfloat16)
            near_high = window.astype(jnp.bfloat16)
            near_low = (window - near_high.astype(jnp.float32)).astype(jnp.bfloat16)
            value_ref[pl.ds(start, BLK), :] = lax.dot_general(
                jnp.concatenate([mix_high, mix_high, mix_low], axis=0),
                jnp.concatenate([near_high, near_low, near_high], axis=0),
                (((0,), (0,)), ((), ())), preferred_element_type=jnp.float32,
            )
        store(step).start()

    for step in range(steps):
        store(step).wait()


def smoothing(offset, low, model, high, neighbors, face_weight, after):
    cells, width = model.shape
    return pl.pallas_call(
        smooth_body,
        out_shape=jax.ShapeDtypeStruct((cells, width), jnp.float32),
        in_specs=[SMEM_SPEC, ANY_SPEC, ANY_SPEC, ANY_SPEC, VMEM_SPEC, VMEM_SPEC, ANY_SPEC],
        out_specs=ANY_SPEC,
        scratch_shapes=[
            pltpu.VMEM((cells + 2 * RIM, width), jnp.float32),
            pltpu.VMEM((cells, width), jnp.float32),
            pltpu.SemaphoreType.DMA((16,)),
            pltpu.SemaphoreType.DMA((2,)),
            pltpu.SemaphoreType.DMA((8,)),
        ],
        compiler_params=pltpu.CompilerParams(vmem_limit_bytes=LARGE),
        cost_estimate=pl.CostEstimate(
            flops=24 * cells * BLK * width, bytes_accessed=16 * cells * width, transcendentals=0
        ),
        name="smoothing",
    )(offset, low, model, high, neighbors, face_weight, after)


def finish_body(take_ref, cells_ref, basis_ref, got_ref, mine_ref, base_ref, after_ref,
                out_ref, token_ref, block_ref, got, put, *, chunk):
    cols = got_ref.shape[0]
    fetches, stores = [], []
    for i in range(cols):
        cell = cells_ref[chunk * cols + i]
        fetches.append(pltpu.make_async_copy(base_ref.at[cell], block_ref.at[i], got.at[i]))
        stores.append(pltpu.make_async_copy(block_ref.at[i], out_ref.at[cell], put.at[i]))
    start_all(fetches)
    wait_all(fetches)
    for i in range(cols):
        wave = jnp.where(take_ref[0] > 0, got_ref[i], mine_ref[i])
        both = jnp.concatenate([wave, wave], axis=0)
        block_ref[i] += jnp.dot(basis_ref[...], both, preferred_element_type=jnp.float32)
    start_all(stores)
    token_ref[...] = jnp.zeros_like(token_ref)
    wait_all(stores)


def finish(take, cells, got, mine, base, after, chunk):
    cols, _, width = got.shape
    basis = haar_matrix(BLK).T.astype(np.float32)
    high = basis.astype(jnp.bfloat16)
    low = (basis - high.astype(np.float32)).astype(jnp.bfloat16)
    basis2 = jnp.asarray(np.concatenate([high, low], axis=1))
    return pl.pallas_call(
        lambda *refs: finish_body(*refs, chunk=chunk),
        out_shape=[
            jax.ShapeDtypeStruct(base.shape, base.dtype),
            jax.ShapeDtypeStruct((8, BLK), jnp.float32),
        ],
        in_specs=[SMEM_SPEC, SMEM_SPEC, VMEM_SPEC, VMEM_SPEC, VMEM_SPEC, ANY_SPEC, ANY_SPEC],
        out_specs=[ANY_SPEC, VMEM_SPEC],
        input_output_aliases={5: 0},
        scratch_shapes=[
            pltpu.VMEM((cols, BLK, width), jnp.float32),
            pltpu.SemaphoreType.DMA((cols,)),
            pltpu.SemaphoreType.DMA((cols,)),
        ],
        compiler_params=pltpu.CompilerParams(vmem_limit_bytes=SMALL),
        cost_estimate=pl.CostEstimate(
            flops=4 * cols * BLK * BLK * width, bytes_accessed=10 * cols * BLK * width,
            transcendentals=0,
        ),
        name="finish",
    )(take, cells, basis2, got, mine, base, after)


def merge_body(got_ref, mine_ref, after_ref, out_ref):
    total = got_ref[...].astype(jnp.float32) + mine_ref[...].astype(jnp.float32)
    out_ref[...] = total.astype(out_ref.dtype)


def merge(got, mine, after):
    return pl.pallas_call(
        merge_body,
        out_shape=jax.ShapeDtypeStruct(mine.shape, mine.dtype),
        in_specs=[VMEM_SPEC, VMEM_SPEC, ANY_SPEC],
        out_specs=VMEM_SPEC,
        compiler_params=pltpu.CompilerParams(vmem_limit_bytes=SMALL),
        cost_estimate=pl.CostEstimate(
            flops=mine.size, bytes_accessed=6 * mine.size, transcendentals=0
        ),
        name="merge",
    )(got, mine, after)


def line_sums(parts, axis, deliver):
    count = lax.axis_size(axis)
    half = count // 2
    me = lax.axis_index(axis)
    stages = []
    for hop in range(half - 1):
        stages.append(([(hop, hop + 1), (count - 1 - hop, count - 2 - hop)], False))
    stages.append(([(half - 1, half), (half, half - 1)], False))
    for hop in range(half - 1):
        left, right = half - 1 - hop, half + hop
        stages.append(([(left, left - 1), (right, right + 1)], True))
    state = list(parts)
    got = [lax.ppermute(part, axis, stages[0][0]) for part in parts]
    after = parts[0]
    for time in range(len(parts) + len(stages) - 1):
        for s, (pairs, outwards) in enumerate(stages):
            k = time - s
            if not 0 <= k < len(parts):
                continue
            last = s + 1 == len(stages)
            if outwards:
                take = (me == pairs[0][1]) | (me == pairs[1][1])
                take = take.astype(jnp.int32).reshape(1)
                if last:
                    after = deliver(k, take, got[k], state[k], after)
                else:
                    state[k] = jnp.where(take[0] > 0, got[k], state[k])
            else:
                state[k] = after = merge(got[k], state[k], after)
                if last:
                    after = deliver(k, jnp.zeros((1,), jnp.int32), state[k], state[k], after)
            if not last:
                got[k] = lax.ppermute(state[k], axis, stages[s + 1][0])


def halo(block, axis, width):
    count = lax.axis_size(axis)
    forward_pairs = [(i, i + 1) for i in range(count - 1)]
    backward_pairs = [(target, source) for source, target in forward_pairs]
    low = lax.ppermute(block[block.shape[0] - width :], axis, forward_pairs)
    high = lax.ppermute(block[:width], axis, backward_pairs)
    return low, high


def local(model_dir, sens_blocks, blk_row, blk_col, blk_count, send_order, neighbors, face_weight):
    cell_count, width = model_dir.shape
    blocks = cell_count // BLK
    col_devices = lax.axis_size("cols")
    per_peer = blocks // col_devices
    model_blocks = model_dir.reshape(blocks, BLK, width)
    sens = sens_blocks[0]
    chunks = math.gcd(CHUNKS, per_peer)
    each = per_peer // chunks

    outgoing = analyze(send_order, model_blocks)
    wave = lax.all_to_all(
        outgoing.reshape(col_devices, per_peer * BLK, width), "cols", 0, 0, tiled=True
    ).reshape(blocks, BLK, width)

    model_late, order_late, _ = lax.optimization_barrier((model_dir, send_order, outgoing))
    low, high = halo(model_late, "cols", RIM)
    offset = (lax.axis_index("cols") * cell_count - RIM).astype(jnp.int32).reshape(1)
    cells = order_late.reshape(col_devices, chunks, each).transpose(1, 0, 2).reshape(blocks)

    partial_rows = forward(blk_row, blk_col, blk_count, sens, wave)
    shares = lax.all_to_all(
        partial_rows.reshape(col_devices, -1, width), "cols", 0, 0, tiled=True
    )
    smooth = smoothing(offset, low, model_dir, high, neighbors, face_weight, partial_rows)
    image_share = jnp.sum(shares.astype(jnp.float32), axis=0).astype(jnp.bfloat16)
    image_half = lax.all_to_all(
        jnp.broadcast_to(image_share, shares.shape), "cols", 0, 0, tiled=True
    ).reshape(-1, width)
    data_image = image_half.astype(jnp.float32)

    partial_cols = adjoint(
        blk_row, blk_col, blk_count, sens, image_half.reshape(RB_DEV, BLK, width), smooth,
        blocks, per_peer, chunks,
    )
    returned = [
        lax.all_to_all(
            part.reshape(col_devices, each * BLK, width), "cols", 0, 0, tiled=True
        ).reshape(col_devices * each, BLK, width)
        for part in partial_cols
    ]
    normal = smooth.reshape(blocks, BLK, width)

    def deliver(chunk, take, got, mine, after):
        nonlocal normal
        normal, token = finish(take, cells, got, mine, normal, after, chunk)
        return token

    line_sums(returned, "rows", deliver)
    return (data_image, normal.reshape(cell_count, width))


def solution(mesh):
    placed = (
        P("cols", None),
        P("rows", "cols", None, None),
        P("rows", "cols"),
        P("rows", "cols"),
        P("rows", "cols"),
        P("cols", None),
        P(None, "cols"),
        P(None, "cols"),
    )
    return jax.shard_map(
        local,
        mesh=mesh,
        in_specs=placed,
        out_specs=(P("rows", None), P("cols", None)),
        check_vma=False,
    )
```

time: 243 us -> 218 us (0.90); the launches traced: 245 us -> 216 us
  waiting for transfers between devices: 92.8 us -> 67.3 us
  blocking collectives: 21 us -> 43.9 us
  local copies, waits for them, and re-layouts: 27.9 us -> 9.19 us
  starting transfers between devices: 27.3 us -> 44.7 us
  between operations: 14.9 us -> 1.66 us
  other arithmetic: 7.82 us -> 2.24 us
  Pallas kernels: 52.8 us -> 47.3 us
    all_to_all x2 -> x3, waiting for transfers between devices: 57.7 us -> 15.8 us  [local(): lax.all_to_all(part.reshape(col_devices, each * BLK, width), 'cols', 0, 0...]
    all_to_all x0 -> x1, blocking collectives: none -> 24.5 us  [local(): lax.all_to_all(part.reshape(col_devices, each * BLK, width), 'cols', 0, 0...]
    ppermute x2 -> x14, waiting for transfers between devices: 1.83 us -> 25.4 us  [the longest x8 22.5 us: line_sums(): got[k] = lax.ppermute(state[k], axis, stages[s + 1][0])]
    ppermute x2 -> x14, starting transfers between devices: 2.75 us -> 25.3 us  [the longest x4 12.9 us: line_sums(): got = [lax.ppermute(part, axis, stages[0][0]) for part in parts]]
    unnamed x29 -> x22, local copies, waits for them, and re-layouts: 25.9 us -> 6.57 us
    all_to_all x1, waiting for transfers between devices: 14.8 us -> 0.01 us  [local(): lax.all_to_all(jnp.broadcast_to(image_share, shares.shape), 'cols', 0, 0,...]
    all_to_all x1, waiting for transfers between devices: 15.8 us -> 26 us  [local(): lax.all_to_all(outgoing.reshape(col_devices, per_peer * BLK, width), 'col...]
    pallas_call x1, Pallas kernels: 14.7 us -> 5.02 us  [analyze(): pl.pallas_call(analyze_body, out_shape=jax.ShapeDtypeStruct((blocks, BLK,...]
  transfers between devices with their start and end apart: 8 -> 19, of which waited for: 6 -> 8; matrix products, arithmetic and copies ran while one was open for 4% -> 2% of each run, Pallas kernels for 10% -> 12%
where the time goes in v4:
time: 218 us; the launch traced here: 216 us
  waiting for transfers between devices  67.3 us (31%)
  Pallas kernels  47.3 us (22%)
  starting transfers between devices  44.7 us (21%)
  blocking collectives  43.9 us (20%)
  local copies, waits for them, and re-layouts  9.19 us (4%)
  other arithmetic  2.24 us (1%)
    all_to_all x1, waiting for transfers between devices, local(): lax.all_to_all(outgoing.reshape(col_devices, per_peer * BLK, width), 'col...  26 us
    all_to_all x1, blocking collectives, local(): lax.all_to_all(part.reshape(col_devices, each * BLK, width), 'cols', 0, 0...  24.5 us
    ppermute x8, waiting for transfers between devices, line_sums(): got[k] = lax.ppermute(state[k], axis, stages[s + 1][0])  22.5 us
    all_to_all x1, blocking collectives, local(): lax.all_to_all(partial_rows.reshape(col_devices, -1, width), 'cols', 0, 0...  19.4 us
    all_to_all x3, waiting for transfers between devices, local(): lax.all_to_all(part.reshape(col_devices, each * BLK, width), 'cols', 0, 0...  15.8 us
    pallas_call x4, Pallas kernels, finish(): pl.pallas_call(lambda *refs: finish_body(*refs, chunk=chunk), out_shape=[...  14.3 us
    pallas_call x1, Pallas kernels, smoothing(): pl.pallas_call(smooth_body, out_shape=jax.ShapeDtypeStruct((cells, width)...  13.4 us
    ppermute x4, starting transfers between devices, line_sums(): got = [lax.ppermute(part, axis, stages[0][0]) for part in parts]  12.9 us
  transfers between devices with their start and end apart: 19, of which 8 were waited for; matrix products, arithmetic and copies ran while one was open for 2% of the time, Pallas kernels for 12%

profile of v4, /device:TPU:0, one launch (start us, length us, event | category | flops | bytes accessed | tf_op | source)
XLA Modules:
  0.0 216.3 jit_solution(15979033718345831056)
XLA Ops:
  0.6 5.0 %analyze.1 = bf16[64,128,128]{2,1,0:T(8,128)(2,1)} custom-call(s32[1,64]{1,0:T(1,128)} %order_ref.1, f32[64,128,128]{2,1,0:T(8,128)} %bitcast.38), custom_call_target="tpu_custom_call" | custom-call | flops 536870912 | bytes 6291456 | tf_op jit(solution)/shard_map/analyze/pallas_call | solution.py:93
  5.7 5.2 %all-to-all-start = ((bf16[8,1024,128]{2,1,0:T(8,128)(2,1)}), bf16[8,1024,128]{2,1,0:T(8,128)(2,1)S(1)}, u32[]{:S(2)}, u32[]{:S(2)}) async-start(bf16[8,1024,128]{2,1,0:T(8,128)(2,1)} %bitcast.37), calls=%async_computation | async-start | bytes 4194304 | tf_op jit(solution)/shard_map/all_to_all | solution.py:433
  11.5 26.0 %all-to-all-done = bf16[8,1024,128]{2,1,0:T(8,128)(2,1)S(1)} async-done(((bf16[8,1024,128]{2,1,0:T(8,128)(2,1)}), bf16[8,1024,128]{2,1,0:T(8,128)(2,1)S(1)}, u32[]{:S(2)}, u32[]{:S(2)}) %all-to-all-start) | async-done | bytes 2097184 | tf_op jit(solution)/shard_map/all_to_all | solution.py:433
  37.5 1.3 copy-done.7
  38.8 5.7 %forward.1.after_ref = bf16[32,128,128]{2,1,0:T(8,128)(2,1)} custom-call(s32[1,384]{1,0:T(1,128)} %refs_0_.1, s32[1,384]{1,0:T(1,128)} %refs_1_.1, s32[1,1]{1,0:T(1,128)S(6)} %copy.24.count_ref.refs_2_, bf16[384,128,128]{2,1,0:T(8,128)(2,1)} %bitcast.33, bf16[64,128,128]{2,1,0:T(8,128)(2,1)} %bitcast.36), custom_call_target="tpu_custom_call" | custom-call | flops 1610612736 | bytes 12582912 | tf_op jit(solution)/shard_map/forward/pallas_call | solution.py:160
  44.5 19.4 %all_to_all.35 = bf16[8,512,128]{2,1,0:T(8,128)(2,1)S(1)} all-to-all(bf16[8,512,128]{2,1,0:T(8,128)(2,1)} %bitcast.39), channel_id=1, replica_groups=mesh['rows'=4,'cols'=8] {'cols'}, dimensions={0} | all-to-all | bytes 2097152 | tf_op jit(solution)/shard_map/all_to_all | solution.py:443
  63.9 0.1 reduce_sum.12
  64.0 1.1 broadcast_in_dim.3
  65.1 3.6 %all-to-all-start.2 = ((bf16[8,512,128]{2,1,0:T(8,128)(2,1)}), bf16[8,512,128]{2,1,0:T(8,128)(2,1)S(1)}, u32[]{:S(2)}, u32[]{:S(2)}) async-start(bf16[8,512,128]{2,1,0:T(8,128)(2,1)} %broadcast_in_dim.3), calls=%async_computation.2 | async-start | bytes 2097152 | tf_op jit(solution)/shard_map/all_to_all | solution.py:448
  68.7 0.8 fusion
  69.5 2.3 %collective-permute-start = (f32[64,128]{1,0:T(8,128)S(1)}, f32[64,128]{1,0:T(8,128)S(1)}, u32[]{:S(2)}, u32[]{:S(2)}) collective-permute-start(f32[64,128]{1,0:T(8,128)S(1)} %get-tuple-element.29), channel_id=1, source_target_pairs={{0,1},{1,2},{2,3},{3,4},{4,5},{5,6},{6,7},{8,9},{9,10},{10,11},{11... | collective-permute-start | bytes 98312 | tf_op jit(solution)/shard_map/ppermute | solution.py:417
  71.8 1.3 collective-permute-start.1
  73.1 2.9 %collective-permute-done.1.high_ref = f32[64,128]{1,0:T(8,128)S(1)} collective-permute-done((f32[64,128]{1,0:T(8,128)S(1)}, f32[64,128]{1,0:T(8,128)S(1)}, u32[]{:S(2)}, u32[]{:S(2)}) %collective-permute-start.1) | collective-permute-done | bytes 32800 | tf_op jit(solution)/shard_map/ppermute | solution.py:418
  76.0 0.6 copy-done.10
  76.6 13.4 %smoothing.1.refs_5_ = f32[8192,128]{1,0:T(8,128)} custom-call(s32[1]{0:T(128)} %bitcast.9.offset_ref, f32[64,128]{1,0:T(8,128)} %copy-done.9, f32[8192,128]{1,0:T(8,128)} %model_ref.1, f32[64,128]{1,0:T(8,128)} %copy-done.10, s32[4,8192]{1,0:T(4,128)} %near_ref.1, f32[4,8192]{1,0:T(4,128)} %weight_ref.1, bf16[32,128,128]{2,1,0:T(8,128)(2,1)} %forward.1.after_ref), custom_call_target="tpu_custom_call" | custom-call | flops 3221225472 | bytes 16777216 | tf_op jit(solution)/shard_map/smoothing/pallas_call | solution.py:291
  90.0 0.0 copy-start.5
  90.0 1.0 copy-done.5
  91.0 5.9 %adjoint.1 = (bf16[16,128,128]{2,1,0:T(8,128)(2,1)}, bf16[16,128,128]{2,1,0:T(8,128)(2,1)}, bf16[16,128,128]{2,1,0:T(8,128)(2,1)}, bf16[16,128,128]{2,1,0:T(8,128)(2,1)}) custom-call(s32[1,384]{1,0:T(1,128)} %refs_0_.1, s32[1,384]{1,0:T(1,128)} %refs_1_.1, s32[1,1]{1,0:T(1,128)S(6)} %copy.24.count_ref.refs_2_, bf16[384,128,128]{2,1,0:T(8,128)(2,1)} %bitcast.34, ...), custom_call_target="tpu_custom_call" | custom-call | flops 1610612736 | bytes 12582912 | tf_op jit(solution)/shard_map/adjoint/pallas_call | solution.py:216
  96.9 24.5 %all_to_all.36 = bf16[8,256,128]{2,1,0:T(8,128)(2,1)S(1)} all-to-all(bf16[8,256,128]{2,1,0:T(8,128)(2,1)} %bitcast.43), channel_id=1, replica_groups=mesh['rows'=4,'cols'=8] {'cols'}, dimensions={0} | all-to-all | bytes 1048576 | tf_op jit(solution)/shard_map/all_to_all | solution.py:458
  121.4 3.5 %all-to-all-start.5 = ((bf16[8,256,128]{2,1,0:T(8,128)(2,1)}), bf16[8,256,128]{2,1,0:T(8,128)(2,1)S(1)}, u32[]{:S(2)}, u32[]{:S(2)}) async-start(bf16[8,256,128]{2,1,0:T(8,128)(2,1)} %bitcast.42), calls=%async_computation.5 | async-start | bytes 1048576 | tf_op jit(solution)/shard_map/all_to_all | solution.py:458
  124.9 1.3 collective-permute-start.3
  126.2 8.3 %all-to-all-done.5 = bf16[8,256,128]{2,1,0:T(8,128)(2,1)S(1)} async-done(((bf16[8,256,128]{2,1,0:T(8,128)(2,1)}), bf16[8,256,128]{2,1,0:T(8,128)(2,1)S(1)}, u32[]{:S(2)}, u32[]{:S(2)}) %all-to-all-start.5) | async-done | bytes 524320 | tf_op jit(solution)/shard_map/all_to_all | solution.py:458
  134.5 3.6 %all-to-all-start.6 = ((bf16[8,256,128]{2,1,0:T(8,128)(2,1)}), bf16[8,256,128]{2,1,0:T(8,128)(2,1)S(1)}, u32[]{:S(2)}, u32[]{:S(2)}) async-start(bf16[8,256,128]{2,1,0:T(8,128)(2,1)} %bitcast.41), calls=%async_computation.6 | async-start | bytes 1048576 | tf_op jit(solution)/shard_map/all_to_all | solution.py:458
  138.2 1.3 collective-permute-start.5
  139.5 0.0 collective-permute-done.3.got_ref
  139.5 0.1 merge.8.after_ref.mine_ref
  139.6 0.7 collective-permute-start.4
  140.3 7.5 %all-to-all-done.6 = bf16[8,256,128]{2,1,0:T(8,128)(2,1)S(1)} async-done(((bf16[8,256,128]{2,1,0:T(8,128)(2,1)}), bf16[8,256,128]{2,1,0:T(8,128)(2,1)S(1)}, u32[]{:S(2)}, u32[]{:S(2)}) %all-to-all-start.6) | async-done | bytes 524320 | tf_op jit(solution)/shard_map/all_to_all | solution.py:458
  147.8 3.5 %all-to-all-start.3 = ((bf16[8,256,128]{2,1,0:T(8,128)(2,1)}), bf16[8,256,128]{2,1,0:T(8,128)(2,1)S(1)}, u32[]{:S(2)}, u32[]{:S(2)}) async-start(bf16[8,256,128]{2,1,0:T(8,128)(2,1)} %bitcast.40), calls=%async_computation.3 | async-start | bytes 1048576 | tf_op jit(solution)/shard_map/all_to_all | solution.py:458
  151.3 0.0 copy-start
  151.4 3.3 %collective-permute-start.8 = (bf16[16,128,128]{2,1,0:T(8,128)(2,1)S(1)}, bf16[16,128,128]{2,1,0:T(8,128)(2,1)}, u32[]{:S(2)}, u32[]{:S(2)}) collective-permute-start(bf16[16,128,128]{2,1,0:T(8,128)(2,1)S(1)} %bitcast.27), channel_id=1, source_target_pairs={{0,8},{24,16},{1,9},{25,17},{2,10},{26,18},{3,11},{27,19},{4,12},{... | collective-permute-start | bytes 1572872 | tf_op jit(solution)/shard_map/ppermute | solution.py:390
  154.7 0.8 copy-done.1
  155.5 1.0 copy-done.2
  156.5 0.1 merge.9.after_ref.mine_ref
  156.6 1.5 collective-permute-start.7
  158.1 0.8 copy-done.3
  158.9 1.0 copy-done.4
  159.9 0.1 merge.10.after_ref.refs_4_
  160.1 1.3 collective-permute-start.6
  161.4 6.9 %collective-permute-start.2 = (bf16[16,128,128]{2,1,0:T(8,128)(2,1)S(1)}, bf16[16,128,128]{2,1,0:T(8,128)(2,1)S(1)}, u32[]{:S(2)}, u32[]{:S(2)}) collective-permute-start(bf16[16,128,128]{2,1,0:T(8,128)(2,1)S(1)} %bitcast.25), channel_id=1, source_target_pairs={{0,8},{24,16},{1,9},{25,17},{2,10},{26,18},{3,11},{27,19},{4,12},{... | collective-permute-start | bytes 1572872 | tf_op jit(solution)/shard_map/ppermute | solution.py:390
  168.3 0.5 broadcast.3
  168.8 0.6 reduce.4
  169.4 0.1 reshape.72
  169.5 0.1 reshape.73.refs_1_
  169.7 1.2 merge.11.after_ref.mine_ref
  170.8 0.7 collective-permute-start.11
  171.5 1.2 merge.12.refs_6_.refs_4_
  172.7 1.3 collective-permute-start.10
  174.0 3.9 %collective-permute-done.6.refs_3_ = bf16[16,128,128]{2,1,0:T(8,128)(2,1)S(1)} collective-permute-done((bf16[16,128,128]{2,1,0:T(8,128)(2,1)S(1)}, bf16[16,128,128]{2,1,0:T(8,128)(2,1)S(1)}, u32[]{:S(2)}, u32[]{:S(2)}) %collective-permute-start.6) | collective-permute-done | bytes 524320 | tf_op jit(solution)/shard_map/ppermute | solution.py:410
  177.9 3.4 %finish.4 = (f32[64,128,128]{2,1,0:T(8,128)}, f32[8,128]{1,0:T(8,128)S(1)}) custom-call(s32[1]{0:T(128)} %bitcast.6.refs_0_, s32[64]{0:T(128)S(1)} %reshape.73.refs_1_, bf16[128,256]{1,0:T(8,128)(2,1)S(1)} %copy-done, bf16[16,128,128]{2,1,0:T(8,128)(2,1)S(1)} %collective-permute-done.6.refs_3_, ...), custom_call_target="tpu_custom_call", output_to_operand_aliasing={{0}: (5, {})} | custom-call | flops 134217728 | bytes 2621440 | tf_op jit(solution)/shard_map/finish/pallas_call | solution.py:336
  181.4 0.1 merge.13.after_ref.mine_ref
  181.5 0.7 collective-permute-start.9
  182.2 0.1 merge.14.refs_6_.refs_4_
  182.4 0.0 copy-start.6
  182.4 1.4 collective-permute-start.13
  183.8 6.4 %collective-permute-done.10.refs_3_ = bf16[16,128,128]{2,1,0:T(8,128)(2,1)S(1)} collective-permute-done((bf16[16,128,128]{2,1,0:T(8,128)(2,1)S(1)}, bf16[16,128,128]{2,1,0:T(8,128)(2,1)S(1)}, u32[]{:S(2)}, u32[]{:S(2)}) %collective-permute-start.10) | collective-permute-done | bytes 524320 | tf_op jit(solution)/shard_map/ppermute | solution.py:410
  190.2 3.4 %finish.5 = (f32[64,128,128]{2,1,0:T(8,128)}, f32[8,128]{1,0:T(8,128)S(1)}) custom-call(s32[1]{0:T(128)} %bitcast.6.refs_0_, s32[64]{0:T(128)S(1)} %reshape.73.refs_1_, bf16[128,256]{1,0:T(8,128)(2,1)S(1)} %copy-done, bf16[16,128,128]{2,1,0:T(8,128)(2,1)S(1)} %collective-permute-done.10.refs_3_, ...), custom_call_target="tpu_custom_call", output_to_operand_aliasing={{0}: (5, {})} | custom-call | flops 134217728 | bytes 2621440 | tf_op jit(solution)/shard_map/finish/pallas_call | solution.py:336
  193.7 0.1 merge.15.refs_6_.refs_4_
  193.8 1.3 collective-permute-start.12
  195.1 1.5 bitcast_convert_fusion
  196.6 5.0 %collective-permute-done.13.refs_3_ = bf16[16,128,128]{2,1,0:T(8,128)(2,1)S(1)} collective-permute-done((bf16[16,128,128]{2,1,0:T(8,128)(2,1)S(1)}, bf16[16,128,128]{2,1,0:T(8,128)(2,1)S(1)}, u32[]{:S(2)}, u32[]{:S(2)}) %collective-permute-start.13) | collective-permute-done | bytes 524320 | tf_op jit(solution)/shard_map/ppermute | solution.py:410
  201.6 3.4 %finish.6 = (f32[64,128,128]{2,1,0:T(8,128)}, f32[8,128]{1,0:T(8,128)S(1)}) custom-call(s32[1]{0:T(128)} %bitcast.6.refs_0_, s32[64]{0:T(128)S(1)} %reshape.73.refs_1_, bf16[128,256]{1,0:T(8,128)(2,1)S(1)} %copy-done, bf16[16,128,128]{2,1,0:T(8,128)(2,1)S(1)} %collective-permute-done.13.refs_3_, ...), custom_call_target="tpu_custom_call", output_to_operand_aliasing={{0}: (5, {})} | custom-call | flops 134217728 | bytes 2621440 | tf_op jit(solution)/shard_map/finish/pallas_call | solution.py:336
  205.1 7.2 %collective-permute-done.12.refs_3_ = bf16[16,128,128]{2,1,0:T(8,128)(2,1)S(1)} collective-permute-done((bf16[16,128,128]{2,1,0:T(8,128)(2,1)S(1)}, bf16[16,128,128]{2,1,0:T(8,128)(2,1)S(1)}, u32[]{:S(2)}, u32[]{:S(2)}) %collective-permute-start.12) | collective-permute-done | bytes 524320 | tf_op jit(solution)/shard_map/ppermute | solution.py:410
  212.2 4.0 %finish.7 = (f32[64,128,128]{2,1,0:T(8,128)}, f32[8,128]{1,0:T(8,128)}) custom-call(s32[1]{0:T(128)} %bitcast.6.refs_0_, s32[64]{0:T(128)S(1)} %reshape.73.refs_1_, bf16[128,256]{1,0:T(8,128)(2,1)S(1)} %copy-done, bf16[16,128,128]{2,1,0:T(8,128)(2,1)S(1)} %collective-permute-done.12.refs_3_, ...), custom_call_target="tpu_custom_call", output_to_operand_aliasing={{0}: (5, {})} | custom-call | flops 134217728 | bytes 2621440 | tf_op jit(solution)/shard_map/finish/pallas_call | solution.py:336
  (23 shorter events, 0.1 us)
Async XLA Ops:
  5.7 31.8 %all-to-all-start = ((bf16[8,1024,128]{2,1,0:T(8,128)(2,1)}), bf16[8,1024,128]{2,1,0:T(8,128)(2,1)S(1)}, u32[]{:S(2)}, u32[]{:S(2)}) async-start(bf16[8,1024,128]{2,1,0:T(8,128)(2,1)} %bitcast.37), calls=%async_computation | async-start | bytes 4194304 | tf_op jit(solution)/shard_map/all_to_all | solution.py:433
  37.5 1.3 copy-start.7
  65.1 24.9 %all-to-all-start.2 = ((bf16[8,512,128]{2,1,0:T(8,128)(2,1)}), bf16[8,512,128]{2,1,0:T(8,128)(2,1)S(1)}, u32[]{:S(2)}, u32[]{:S(2)}) async-start(bf16[8,512,128]{2,1,0:T(8,128)(2,1)} %broadcast_in_dim.3), calls=%async_computation.2 | async-start | bytes 2097152 | tf_op jit(solution)/shard_map/all_to_all | solution.py:448
  69.5 3.6 %collective-permute-start = (f32[64,128]{1,0:T(8,128)S(1)}, f32[64,128]{1,0:T(8,128)S(1)}, u32[]{:S(2)}, u32[]{:S(2)}) collective-permute-start(f32[64,128]{1,0:T(8,128)S(1)} %get-tuple-element.29), channel_id=1, source_target_pairs={{0,1},{1,2},{2,3},{3,4},{4,5},{5,6},{6,7},{8,9},{9,10},{10,11},{11... | collective-permute-start | bytes 98312 | tf_op jit(solution)/shard_map/ppermute | solution.py:417
  71.8 4.2 %collective-permute-start.1 = (f32[64,128]{1,0:T(8,128)S(1)}, f32[64,128]{1,0:T(8,128)S(1)}, u32[]{:S(2)}, u32[]{:S(2)}) collective-permute-start(f32[64,128]{1,0:T(8,128)S(1)} %get-tuple-element.28), channel_id=1, source_target_pairs={{1,0},{2,1},{3,2},{4,3},{5,4},{6,5},{7,6},{9,8},{10,9},{11,10},{12... | collective-permute-start | bytes 98312 | tf_op jit(solution)/shard_map/ppermute | solution.py:418
  73.1 2.9 %copy-start.9 = (f32[64,128]{1,0:T(8,128)}, f32[64,128]{1,0:T(8,128)S(1)}, u32[]{:S(2)}) copy-start(f32[64,128]{1,0:T(8,128)S(1)} %collective-permute-done.low_ref) | copy-start | bytes 98308
  76.0 0.6 copy-start.10
  90.0 1.0 copy-start.5
  121.4 13.2 %all-to-all-start.5 = ((bf16[8,256,128]{2,1,0:T(8,128)(2,1)}), bf16[8,256,128]{2,1,0:T(8,128)(2,1)S(1)}, u32[]{:S(2)}, u32[]{:S(2)}) async-start(bf16[8,256,128]{2,1,0:T(8,128)(2,1)} %bitcast.42), calls=%async_computation.5 | async-start | bytes 1048576 | tf_op jit(solution)/shard_map/all_to_all | solution.py:458
  124.9 14.6 %collective-permute-start.3 = (bf16[16,128,128]{2,1,0:T(8,128)(2,1)S(1)}, bf16[16,128,128]{2,1,0:T(8,128)(2,1)S(1)}, u32[]{:S(2)}, u32[]{:S(2)}) collective-permute-start(bf16[16,128,128]{2,1,0:T(8,128)(2,1)S(1)} %bitcast.22), channel_id=1, source_target_pairs={{0,8},{24,16},{1,9},{25,17},{2,10},{26,18},{3,11},{27,19},{4,12},{... | collective-permute-start | bytes 1572872 | tf_op jit(solution)/shard_map/ppermute | solution.py:390
  134.5 34.3 %copy-start.8 = (s32[1,64]{1,0:T(1,128)S(1)}, s32[1,64]{1,0:T(1,128)}, u32[]{:S(2)}) copy-start(s32[1,64]{1,0:T(1,128)} %order_ref.1) | copy-start | bytes 772
  134.5 13.3 %all-to-all-start.6 = ((bf16[8,256,128]{2,1,0:T(8,128)(2,1)}), bf16[8,256,128]{2,1,0:T(8,128)(2,1)S(1)}, u32[]{:S(2)}, u32[]{:S(2)}) async-start(bf16[8,256,128]{2,1,0:T(8,128)(2,1)} %bitcast.41), calls=%async_computation.6 | async-start | bytes 1048576 | tf_op jit(solution)/shard_map/all_to_all | solution.py:458
  138.2 16.5 %collective-permute-start.5 = (bf16[16,128,128]{2,1,0:T(8,128)(2,1)S(1)}, bf16[16,128,128]{2,1,0:T(8,128)(2,1)S(1)}, u32[]{:S(2)}, u32[]{:S(2)}) collective-permute-start(bf16[16,128,128]{2,1,0:T(8,128)(2,1)S(1)} %bitcast.29), channel_id=1, source_target_pairs={{0,8},{24,16},{1,9},{25,17},{2,10},{26,18},{3,11},{27,19},{4,12},{... | collective-permute-start | bytes 1572872 | tf_op jit(solution)/shard_map/ppermute | solution.py:390
  139.6 18.4 %collective-permute-start.4 = (bf16[16,128,128]{2,1,0:T(8,128)(2,1)S(1)}, bf16[16,128,128]{2,1,0:T(8,128)(2,1)S(1)}, u32[]{:S(2)}, u32[]{:S(2)}) collective-permute-start(bf16[16,128,128]{2,1,0:T(8,128)(2,1)S(1)} %merge.8.after_ref.mine_ref), channel_id=1, source_target_pairs={{8,16},{16,8},{9,17},{17,9},{10,18},{18,10},{11,19},{19,11},{12,20... | collective-permute-start | bytes 1572872 | tf_op jit(solution)/shard_map/ppermute | solution.py:410
  147.8 13.5 %all-to-all-start.3 = ((bf16[8,256,128]{2,1,0:T(8,128)(2,1)}), bf16[8,256,128]{2,1,0:T(8,128)(2,1)S(1)}, u32[]{:S(2)}, u32[]{:S(2)}) async-start(bf16[8,256,128]{2,1,0:T(8,128)(2,1)} %bitcast.40), calls=%async_computation.3 | async-start | bytes 1048576 | tf_op jit(solution)/shard_map/all_to_all | solution.py:458
  151.3 26.6 %copy-start = (bf16[128,256]{1,0:T(8,128)(2,1)S(1)}, bf16[128,256]{1,0:T(8,128)(2,1)}, u32[]{:S(2)}) copy-start(bf16[128,256]{1,0:T(8,128)(2,1)} %constant.22.clone.refs_2_) | copy-start | bytes 196612
  151.4 18.3 %collective-permute-start.8 = (bf16[16,128,128]{2,1,0:T(8,128)(2,1)S(1)}, bf16[16,128,128]{2,1,0:T(8,128)(2,1)}, u32[]{:S(2)}, u32[]{:S(2)}) collective-permute-start(bf16[16,128,128]{2,1,0:T(8,128)(2,1)S(1)} %bitcast.27), channel_id=1, source_target_pairs={{0,8},{24,16},{1,9},{25,17},{2,10},{26,18},{3,11},{27,19},{4,12},{... | collective-permute-start | bytes 1572872 | tf_op jit(solution)/shard_map/ppermute | solution.py:390
  154.7 0.8 copy-start.1
  155.5 1.0 copy-start.2
  156.6 14.9 %collective-permute-start.7 = (bf16[16,128,128]{2,1,0:T(8,128)(2,1)S(1)}, bf16[16,128,128]{2,1,0:T(8,128)(2,1)}, u32[]{:S(2)}, u32[]{:S(2)}) collective-permute-start(bf16[16,128,128]{2,1,0:T(8,128)(2,1)S(1)} %merge.9.after_ref.mine_ref), channel_id=1, source_target_pairs={{8,16},{16,8},{9,17},{17,9},{10,18},{18,10},{11,19},{19,11},{12,20... | collective-permute-start | bytes 1572872 | tf_op jit(solution)/shard_map/ppermute | solution.py:410
  158.1 0.8 copy-start.3
  158.9 1.0 copy-start.4
  160.1 17.9 %collective-permute-start.6 = (bf16[16,128,128]{2,1,0:T(8,128)(2,1)S(1)}, bf16[16,128,128]{2,1,0:T(8,128)(2,1)S(1)}, u32[]{:S(2)}, u32[]{:S(2)}) collective-permute-start(bf16[16,128,128]{2,1,0:T(8,128)(2,1)S(1)} %merge.10.after_ref.refs_4_), channel_id=1, source_target_pairs={{8,0},{16,24},{9,1},{17,25},{10,2},{18,26},{11,3},{19,27},{12,4},{... | collective-permute-start | bytes 1572872 | tf_op jit(solution)/shard_map/ppermute | solution.py:410
  161.4 20.0 %collective-permute-start.2 = (bf16[16,128,128]{2,1,0:T(8,128)(2,1)S(1)}, bf16[16,128,128]{2,1,0:T(8,128)(2,1)S(1)}, u32[]{:S(2)}, u32[]{:S(2)}) collective-permute-start(bf16[16,128,128]{2,1,0:T(8,128)(2,1)S(1)} %bitcast.25), channel_id=1, source_target_pairs={{0,8},{24,16},{1,9},{25,17},{2,10},{26,18},{3,11},{27,19},{4,12},{... | collective-permute-start | bytes 1572872 | tf_op jit(solution)/shard_map/ppermute | solution.py:390
  170.8 11.4 %collective-permute-start.11 = (bf16[16,128,128]{2,1,0:T(8,128)(2,1)S(1)}, bf16[16,128,128]{2,1,0:T(8,128)(2,1)S(1)}, u32[]{:S(2)}, u32[]{:S(2)}) collective-permute-start(bf16[16,128,128]{2,1,0:T(8,128)(2,1)S(1)} %merge.11.after_ref.mine_ref), channel_id=1, source_target_pairs={{8,16},{16,8},{9,17},{17,9},{10,18},{18,10},{11,19},{19,11},{12,20... | collective-permute-start | bytes 1572872 | tf_op jit(solution)/shard_map/ppermute | solution.py:410
  172.7 17.5 %collective-permute-start.10 = (bf16[16,128,128]{2,1,0:T(8,128)(2,1)S(1)}, bf16[16,128,128]{2,1,0:T(8,128)(2,1)S(1)}, u32[]{:S(2)}, u32[]{:S(2)}) collective-permute-start(bf16[16,128,128]{2,1,0:T(8,128)(2,1)S(1)} %merge.12.refs_6_.refs_4_), channel_id=1, source_target_pairs={{8,0},{16,24},{9,1},{17,25},{10,2},{18,26},{11,3},{19,27},{12,4},{... | collective-permute-start | bytes 1572872 | tf_op jit(solution)/shard_map/ppermute | solution.py:410
  181.5 12.2 %collective-permute-start.9 = (bf16[16,128,128]{2,1,0:T(8,128)(2,1)S(1)}, bf16[16,128,128]{2,1,0:T(8,128)(2,1)S(1)}, u32[]{:S(2)}, u32[]{:S(2)}) collective-permute-start(bf16[16,128,128]{2,1,0:T(8,128)(2,1)S(1)} %merge.13.after_ref.mine_ref), channel_id=1, source_target_pairs={{8,16},{16,8},{9,17},{17,9},{10,18},{18,10},{11,19},{19,11},{12,20... | collective-permute-start | bytes 1572872 | tf_op jit(solution)/shard_map/ppermute | solution.py:410
  182.4 12.8 %copy-start.6 = (bf16[8,512,128]{2,1,0:T(8,128)(2,1)S(1)}, bf16[8,512,128]{2,1,0:T(8,128)(2,1)}, u32[]{:S(2)}) copy-start(bf16[8,512,128]{2,1,0:T(8,128)(2,1)} %copy-done.5) | copy-start | bytes 3145732
  182.4 19.2 %collective-permute-start.13 = (bf16[16,128,128]{2,1,0:T(8,128)(2,1)S(1)}, bf16[16,128,128]{2,1,0:T(8,128)(2,1)S(1)}, u32[]{:S(2)}, u32[]{:S(2)}) collective-permute-start(bf16[16,128,128]{2,1,0:T(8,128)(2,1)S(1)} %merge.14.refs_6_.refs_4_), channel_id=1, source_target_pairs={{8,0},{16,24},{9,1},{17,25},{10,2},{18,26},{11,3},{19,27},{12,4},{... | collective-permute-start | bytes 1572872 | tf_op jit(solution)/shard_map/ppermute | solution.py:410
  193.8 18.4 %collective-permute-start.12 = (bf16[16,128,128]{2,1,0:T(8,128)(2,1)S(1)}, bf16[16,128,128]{2,1,0:T(8,128)(2,1)S(1)}, u32[]{:S(2)}, u32[]{:S(2)}) collective-permute-start(bf16[16,128,128]{2,1,0:T(8,128)(2,1)S(1)} %merge.15.refs_6_.refs_4_), channel_id=1, source_target_pairs={{8,0},{16,24},{9,1},{17,25},{10,2},{18,26},{11,3},{19,27},{12,4},{... | collective-permute-start | bytes 1572872 | tf_op jit(solution)/shard_map/ppermute | solution.py:410
